TPU v7x, 128 devices: a whole 4x4x4 slice. The times are simulated.
128 devices in a mesh: fsdp: 8 (over z, core), expert: 16 (over y, x).
Axes of the slice: x: 4, y: 4, z: 4, core: 2. Of those that a mesh axis runs over, the one named last changes fastest.
Arguments:
- layer_input: bfloat16 [16, 1024, 2048], P('expert', 'fsdp'), may hold values from -6 to 6
- routes: int32 [16, 1024, 8], P('expert', 'fsdp'), may hold values from 0 to 31, all different within a row; in each aligned block of 128 rows (0 to 127, 128 to 255, ..., all dimensions but the last counted through in order) at most 40 rows name the same one
- cotangent: bfloat16 [16, 1024, 2048], P('expert', 'fsdp'), may hold values from -6 to 6
- attn_gain: float32 [2048], replicated, may hold values from 0.5 to 1.5
- query_gain: float32 [128], replicated, may hold values from 0.1 to 1.9
- key_gain: float32 [128], replicated, may hold values from 0.1 to 1.9
- mlp_gain: float32 [2048], replicated, may hold values from 0.5 to 1.5
- w_query: bfloat16 [2048, 4096], P('fsdp'), may hold values from -0.125 to 0.125
- key_weight: bfloat16 [2048, 512], P('fsdp'), may hold values from -0.125 to 0.125
- value_weight: bfloat16 [2048, 512], P('fsdp'), may hold values from -0.125 to 0.125
- w_out: bfloat16 [4096, 2048], P('fsdp'), may hold values from -0.75 to 0.75
- w_router: bfloat16 [2048, 32], P('fsdp'), may hold values from -0.0625 to 0.0625
- w_gate: bfloat16 [32, 2048, 768], P('expert', 'fsdp'), may hold values from -0.125 to 0.125
- w_up: bfloat16 [32, 2048, 768], P('expert', 'fsdp'), may hold values from -0.125 to 0.125
- w_down: bfloat16 [32, 768, 2048], P('expert', 'fsdp'), may hold values from -0.875 to 0.875
Outputs:
- output: bfloat16 [16, 1024, 2048], P('expert', 'fsdp')
- grad_input: bfloat16 [16, 1024, 2048], P('expert', 'fsdp')
- grad_attn_gain: float32 [2048], replicated
- grad_query_gain: float32 [128], replicated
- grad_key_gain: float32 [128], replicated
- grad_mlp_gain: float32 [2048], replicated
- grad_w_query: float32 [2048, 4096], P('fsdp')
- grad_w_key: float32 [2048, 512], P('fsdp')
- grad_w_value: float32 [2048, 512], P('fsdp')
- grad_w_out: float32 [4096, 2048], P('fsdp')
- grad_w_router: float32 [2048, 32], P('fsdp')
- grad_w_gate: float32 [32, 2048, 768], P('expert', 'fsdp')
- grad_w_up: float32 [32, 2048, 768], P('expert', 'fsdp')
- grad_w_down: float32 [32, 768, 2048], P('expert', 'fsdp')
Inputs may be any that keep to these rules, and one draw needn't show every extreme that they name: `routes`: each token names 8 different experts. Among the rows of one device no expert is named more than 40 times, and in some device's rows an expert is named exactly 40 times.
All inputs are finite; a program needn't handle non-finite values.
Results may differ from a plain program's by a relative error of at most 0.025.
Values may be sent and summed in bfloat16 or wider, within the bound.
No kernel may reach another device: no remote copies, remote signals or barrier semaphores. Data moves between devices by JAX's collectives and lax.ppermute only.
A program may use at most 256 MiB of HBM per device.

v0:
```python
import functools

import jax
import jax.numpy as jnp
from jax import lax
from jax.sharding import Mesh
from jax.sharding import PartitionSpec as P

MODEL_WIDTH = 2048
QUERY_HEADS = 32
KEY_VALUE_HEADS = 4
HEAD_SIZE = 128
TOPK = 8
EXP_DEV = 2
FSDP = ("fsdp_0", "fsdp_1")
EXPERT = ("expert_0", "expert_1")
FSDP_EXPERT = ("fsdp_0", "fsdp_1", "expert_0", "expert_1")


epsilon = 1e-06
rope_base = 1000000.0


def sent_together(arrays, axis, dim, along):
    widths = [a.shape[along] for a in arrays]
    both = jnp.concatenate(arrays, axis=along)
    filled = lax.all_gather(both, axis, axis=dim, tiled=True)
    return tuple(jnp.split(filled, [sum(widths[:k]) for k in range(1, len(widths))], axis=along))


def sent_together_2(arrays, axis, dim, along):
    both = jnp.concatenate(arrays, axis=along)
    filled, at, outs = (lax.psum_scatter(both, axis, scatter_dimension=dim, tiled=True), 0, [])
    for a in arrays:
        outs.append(lax.slice_in_dim(filled, at, at + a.shape[along], axis=along))
        at += a.shape[along]
    return tuple(outs)


def by_axis(value, axes):
    return functools.reduce(lax.psum, axes, value)


def inv_rms(values):
    return lax.rsqrt(jnp.mean(values * values, axis=-1, keepdims=True) + epsilon)


def norm_back(grad_norm, normed, scale_part):
    return scale_part * (grad_norm - normed * jnp.mean(grad_norm * normed, axis=-1, keepdims=True))


def turned(values):
    middle = values.shape[-1] // 2
    return jnp.concatenate([-values[..., middle:], values[..., :middle]], axis=-1)


def turned_back(values):
    middle = values.shape[-1] // 2
    return jnp.concatenate([values[..., middle:], -values[..., :middle]], axis=-1)


def rope_tables(positions):
    frequency = rope_base ** (-(jnp.arange(HEAD_SIZE // 2).astype(jnp.float32) * 2.0 / HEAD_SIZE))
    frequency = jnp.concatenate([frequency, frequency])
    angles = positions[:, None] * frequency[None, :]
    return (jnp.cos(angles)[:, None, :], jnp.sin(angles)[:, None, :])


def column_share(matrix, shard_place, shards):
    share_width = matrix.shape[1] // shards
    return lax.dynamic_slice_in_dim(matrix, shard_place * share_width, share_width, 1)


def local(
    layer_input,
    routes,
    cotangent,
    attn_gain,
    query_gain,
    key_gain,
    mlp_gain,
    w_query,
    key_weight,
    value_weight,
    w_out,
    w_router,
    w_gate,
    w_up,
    w_down,
):
    token_count = layer_input.shape[1]
    shards = lax.axis_size(FSDP)
    owners = lax.axis_size(EXPERT)
    experts = EXP_DEV * owners
    capacity = max(2, 5 * token_count * TOPK // (4 * experts))
    sequence_length = token_count * shards
    group_count = QUERY_HEADS // KEY_VALUE_HEADS
    inv_root = HEAD_SIZE ** (-0.5)
    shard_place = lax.axis_index(FSDP)
    offset = shard_place * token_count
    query_pos = offset + jnp.arange(token_count, dtype=jnp.int32)
    key_pos = jnp.arange(sequence_length, dtype=jnp.int32)
    causal = query_pos[:, None] >= key_pos[None, :]
    cosine, sine_table = rope_tables(query_pos.astype(jnp.float32))
    residual = layer_input[0].astype(jnp.float32)
    upstream = cotangent[0].astype(jnp.float32)
    chosen_ids = routes[0]
    scale_one = inv_rms(residual)
    normed_one = residual * scale_one
    first_hidden = (normed_one * attn_gain).astype(jnp.bfloat16)
    query_full, key_full, value_full, out_full, router_full = (
        *sent_together((w_query, key_weight, value_weight), FSDP, 0, 1),
        lax.all_gather(w_out, FSDP, axis=0, tiled=True),
        lax.all_gather(w_router, FSDP, axis=0, tiled=True),
    )
    query_raw = jnp.dot(first_hidden, query_full, preferred_element_type=jnp.float32).reshape(
        token_count, QUERY_HEADS, HEAD_SIZE
    )
    key_unrotated = jnp.dot(first_hidden, key_full, preferred_element_type=jnp.float32).reshape(
        token_count, KEY_VALUE_HEADS, HEAD_SIZE
    )
    value_own = jnp.dot(first_hidden, value_full, preferred_element_type=jnp.float32).astype(
        jnp.bfloat16
    )
    query_scale = inv_rms(query_raw)
    query_hat = query_raw * query_scale
    query_in = query_hat * query_gain
    query_reduced = (query_in * cosine + turned(query_in) * sine_table).astype(jnp.bfloat16)
    key_scale = inv_rms(key_unrotated)
    key_hat = key_unrotated * key_scale
    key_in = key_hat * key_gain
    key_reduced = (key_in * cosine + turned(key_in) * sine_table).astype(jnp.bfloat16)
    key_every_head, value_every_head = sent_together(
        (key_reduced.reshape(token_count, KEY_VALUE_HEADS * HEAD_SIZE), value_own), FSDP, 0, 1
    )
    query_grouped = query_reduced.reshape(
        token_count, KEY_VALUE_HEADS, group_count, HEAD_SIZE
    ).transpose(1, 0, 2, 3)
    key_grouped = key_every_head.reshape(sequence_length, KEY_VALUE_HEADS, HEAD_SIZE).transpose(
        1, 0, 2
    )
    value_grouped = value_every_head.reshape(sequence_length, KEY_VALUE_HEADS, HEAD_SIZE).transpose(
        1, 0, 2
    )

    def scores_of(query_part, key_part):
        raw_scores = (
            jnp.einsum("trd,jd->rtj", query_part, key_part, preferred_element_type=jnp.float32)
            * inv_root
        )
        return jnp.where(causal[None], raw_scores, -1e30)

    def attend(operands):
        query_part, key_part, value_part = operands
        attention_scores = scores_of(query_part, key_part)
        peak_score = jnp.max(attention_scores, axis=-1, keepdims=True)
        exp_total = jnp.sum(jnp.exp(attention_scores - peak_score), axis=-1, keepdims=True)
        log_total = peak_score + jnp.log(exp_total)
        attention_probs = jnp.exp(attention_scores - log_total).astype(jnp.bfloat16)
        attention_output = jnp.einsum(
            "rtj,jd->trd", attention_probs, value_part, preferred_element_type=jnp.float32
        )
        return (attention_output.astype(jnp.bfloat16), log_total)

    attended_groups, log_totals = lax.map(attend, (query_grouped, key_grouped, value_grouped))
    attended_low = attended_groups.transpose(1, 0, 2, 3).reshape(
        token_count, QUERY_HEADS * HEAD_SIZE
    )
    attn_proj = jnp.dot(attended_low, out_full, preferred_element_type=jnp.float32)
    resid_two = residual + attn_proj
    scale_two = inv_rms(resid_two)
    normed_two = resid_two * scale_two
    hidden_two = (normed_two * mlp_gain).astype(jnp.bfloat16)
    logits = jnp.dot(hidden_two, router_full, preferred_element_type=jnp.float32)
    expert_ids = jnp.arange(experts, dtype=jnp.int32)
    picked_table = (chosen_ids[:, :, None] == expert_ids[None, None, :]).astype(jnp.float32)
    chosen = jnp.sum(picked_table * logits[:, None, :], axis=-1)
    gate_probs = jax.nn.softmax(chosen, axis=-1)
    flat_ids = chosen_ids.reshape(-1)
    member = (flat_ids[:, None] == expert_ids[None, :]).astype(jnp.int32)
    rank_within = jnp.sum((jnp.cumsum(member, axis=0) - 1) * member, axis=1)
    slot_index = flat_ids * capacity + rank_within
    assigned = (
        jnp.zeros((experts * capacity,), jnp.int32)
        .at[slot_index]
        .set(jnp.arange(token_count * TOPK, dtype=jnp.int32))
    )
    occupied = jnp.zeros((experts * capacity,), jnp.bool_).at[slot_index].set(True)
    zero_low = jnp.zeros((), jnp.bfloat16)
    send_rows = jnp.where(occupied[:, None], hidden_two[assigned // TOPK], zero_low).reshape(
        owners, EXP_DEV, capacity, MODEL_WIDTH
    )
    gate_all, up_all, down_all = (
        *sent_together((w_gate, w_up), FSDP, 1, 0),
        lax.all_gather(w_down, FSDP, axis=1, tiled=True),
    )
    arrived = lax.all_to_all(send_rows, EXPERT, split_axis=0, concat_axis=0, tiled=True)
    gate_pre = jnp.einsum("secd,edf->secf", arrived, gate_all, preferred_element_type=jnp.float32)
    up_pre = jnp.einsum("secd,edf->secf", arrived, up_all, preferred_element_type=jnp.float32)
    inner_act = (jax.nn.silu(gate_pre) * up_pre).astype(jnp.bfloat16)
    result = jnp.einsum(
        "secf,efd->secd", inner_act, down_all, preferred_element_type=jnp.float32
    ).astype(jnp.bfloat16)
    expert_out, received, gate_pre, up_pre, inner_act = (
        result,
        arrived,
        gate_pre,
        up_pre,
        inner_act,
    )
    returned = lax.all_to_all(expert_out, EXPERT, split_axis=0, concat_axis=0, tiled=True)
    route_out = (
        returned.reshape(experts * capacity, MODEL_WIDTH)[slot_index]
        .reshape(token_count, TOPK, MODEL_WIDTH)
        .astype(jnp.float32)
    )
    output = (resid_two + jnp.sum(gate_probs[:, :, None] * route_out, axis=1)).astype(jnp.bfloat16)
    gate_grad = jnp.sum(upstream[:, None, :] * route_out, axis=-1)
    chosen_grad = gate_probs * (gate_grad - jnp.sum(gate_probs * gate_grad, axis=-1, keepdims=True))
    logit_grad = jnp.sum(picked_table * chosen_grad[:, :, None], axis=1).astype(jnp.bfloat16)
    route_grad = (
        (gate_probs[:, :, None] * upstream[:, None, :])
        .astype(jnp.bfloat16)
        .reshape(token_count * TOPK, MODEL_WIDTH)
    )
    send_grads = jnp.where(occupied[:, None], route_grad[assigned], zero_low).reshape(
        owners, EXP_DEV, capacity, MODEL_WIDTH
    )
    grads_in = lax.all_to_all(send_grads, EXPERT, split_axis=0, concat_axis=0, tiled=True)
    inner_grad = jnp.einsum(
        "secd,efd->secf", grads_in, down_all, preferred_element_type=jnp.float32
    )
    grad_down = jnp.einsum(
        "secf,secd->efd", inner_act, grads_in, preferred_element_type=jnp.float32
    )
    logistic = jax.nn.sigmoid(gate_pre)
    up_grad = (inner_grad * gate_pre * logistic).astype(jnp.bfloat16)
    gate_pre_grad = (inner_grad * up_pre * logistic * (1.0 + gate_pre * (1.0 - logistic))).astype(
        jnp.bfloat16
    )
    grad_gate = jnp.einsum(
        "secd,secf->edf", received, gate_pre_grad, preferred_element_type=jnp.float32
    )
    grad_up = jnp.einsum("secd,secf->edf", received, up_grad, preferred_element_type=jnp.float32)
    row_grads = (
        jnp.einsum("secf,edf->secd", gate_pre_grad, gate_all, preferred_element_type=jnp.float32)
        + jnp.einsum("secf,edf->secd", up_grad, up_all, preferred_element_type=jnp.float32)
    ).astype(jnp.bfloat16)
    grads_back = lax.all_to_all(row_grads, EXPERT, split_axis=0, concat_axis=0, tiled=True)
    expert_back = (
        grads_back.reshape(experts * capacity, MODEL_WIDTH)[slot_index]
        .reshape(token_count, TOPK, MODEL_WIDTH)
        .astype(jnp.float32)
    )
    hidden_two_grad = jnp.einsum(
        "te,de->td", logit_grad, router_full, preferred_element_type=jnp.float32
    ) + jnp.sum(expert_back, axis=1)
    expert_sums = (
        *tuple(
            (
                part.astype(jnp.float32)
                for part in sent_together_2(
                    (grad_gate.astype(jnp.bfloat16), grad_up.astype(jnp.bfloat16)), FSDP, 1, 0
                )
            )
        ),
        lax.psum_scatter(
            grad_down.astype(jnp.bfloat16), FSDP, scatter_dimension=1, tiled=True
        ).astype(jnp.float32),
    )
    grad_mlp_gain = jnp.sum(hidden_two_grad * normed_two, axis=0)
    resid_two_grad = upstream + norm_back(hidden_two_grad * mlp_gain, normed_two, scale_two)
    proj_grad = resid_two_grad.astype(jnp.bfloat16)
    attention_output_grad = jnp.einsum(
        "td,id->ti", proj_grad, out_full, preferred_element_type=jnp.float32
    ).astype(jnp.bfloat16)
    attention_grad_grouped = attention_output_grad.reshape(
        token_count, KEY_VALUE_HEADS, group_count, HEAD_SIZE
    ).transpose(1, 0, 2, 3)

    def attend_back(operands):
        query_part, key_part, value_part, grad_part, log_total = operands
        attention_scores = scores_of(query_part, key_part)
        attention_probs = jnp.exp(attention_scores - log_total)
        prob_grad = jnp.einsum(
            "trd,jd->rtj", grad_part, value_part, preferred_element_type=jnp.float32
        )
        score_grad = (
            attention_probs
            * (prob_grad - jnp.sum(attention_probs * prob_grad, axis=-1, keepdims=True))
        ).astype(jnp.bfloat16)
        value_grad = jnp.einsum(
            "rtj,trd->jd",
            attention_probs.astype(jnp.bfloat16),
            grad_part,
            preferred_element_type=jnp.float32,
        )
        query_grad = (
            jnp.einsum("rtj,jd->trd", score_grad, key_part, preferred_element_type=jnp.float32)
            * inv_root
        )
        key_grad = (
            jnp.einsum("rtj,trd->jd", score_grad, query_part, preferred_element_type=jnp.float32)
            * inv_root
        )
        return (query_grad, key_grad, value_grad)

    query_grad, key_grad_piece, value_grad_piece = lax.map(
        attend_back, (query_grouped, key_grouped, value_grouped, attention_grad_grouped, log_totals)
    )
    key_grad_matrix = key_grad_piece.transpose(1, 0, 2).reshape(
        sequence_length, KEY_VALUE_HEADS * HEAD_SIZE
    )
    value_grad_matrix = value_grad_piece.transpose(1, 0, 2).reshape(
        sequence_length, KEY_VALUE_HEADS * HEAD_SIZE
    )
    key_grad_sum, value_grad_sum = tuple(
        (
            part.astype(jnp.float32)
            for part in sent_together_2(
                (key_grad_matrix.astype(jnp.bfloat16), value_grad_matrix.astype(jnp.bfloat16)),
                FSDP,
                0,
                1,
            )
        )
    )
    value_low_grad = value_grad_sum.astype(jnp.bfloat16)
    key_rot_grad = (
        lax.optimization_barrier(key_grad_sum.astype(jnp.bfloat16))
        .astype(jnp.float32)
        .reshape(token_count, KEY_VALUE_HEADS, HEAD_SIZE)
    )
    query_rot_grad = lax.optimization_barrier(
        query_grad.transpose(1, 0, 2, 3)
        .reshape(token_count, QUERY_HEADS, HEAD_SIZE)
        .astype(jnp.bfloat16)
    ).astype(jnp.float32)
    query_in_grad = query_rot_grad * cosine + turned_back(query_rot_grad * sine_table)
    key_in_grad = key_rot_grad * cosine + turned_back(key_rot_grad * sine_table)
    grad_query_gain = jnp.sum(query_in_grad * query_hat, axis=(0, 1))
    grad_key_gain = jnp.sum(key_in_grad * key_hat, axis=(0, 1))
    query_raw_grad = (
        norm_back(query_in_grad * query_gain, query_hat, query_scale)
        .astype(jnp.bfloat16)
        .reshape(token_count, QUERY_HEADS * HEAD_SIZE)
    )
    key_raw_grad = (
        norm_back(key_in_grad * key_gain, key_hat, key_scale)
        .astype(jnp.bfloat16)
        .reshape(token_count, KEY_VALUE_HEADS * HEAD_SIZE)
    )
    hidden_one_grad = (
        jnp.einsum("ti,di->td", query_raw_grad, query_full, preferred_element_type=jnp.float32)
        + jnp.einsum("ti,di->td", key_raw_grad, key_full, preferred_element_type=jnp.float32)
        + jnp.einsum("ti,di->td", value_low_grad, value_full, preferred_element_type=jnp.float32)
    )
    grad_attn_gain = jnp.sum(hidden_one_grad * normed_one, axis=0)
    input_grad = resid_two_grad + norm_back(hidden_one_grad * attn_gain, normed_one, scale_one)
    gathered = sent_together(
        (
            first_hidden,
            query_raw_grad,
            key_raw_grad,
            value_low_grad,
            attended_low,
            proj_grad,
            hidden_two,
            logit_grad,
        ),
        FSDP,
        0,
        1,
    )
    (
        first_rows,
        query_rows,
        key_rows,
        value_rows,
        attend_rows,
        project_rows,
        second_rows,
        logit_rows,
    ) = gathered
    first_cols = column_share(first_rows, shard_place, shards)
    attend_cols = column_share(attend_rows, shard_place, shards)
    second_cols = column_share(second_rows, shard_place, shards)
    local_shares = (
        jnp.einsum("td,ti->di", first_cols, query_rows, preferred_element_type=jnp.float32),
        jnp.einsum("td,ti->di", first_cols, key_rows, preferred_element_type=jnp.float32),
        jnp.einsum("td,ti->di", first_cols, value_rows, preferred_element_type=jnp.float32),
        jnp.einsum("ti,td->id", attend_cols, project_rows, preferred_element_type=jnp.float32),
        jnp.einsum("td,te->de", second_cols, logit_rows, preferred_element_type=jnp.float32),
    )
    shares = (
        lax.psum(local_shares[0].astype(jnp.bfloat16), EXPERT).astype(jnp.float32),
        lax.psum(local_shares[1].astype(jnp.bfloat16), EXPERT).astype(jnp.float32),
        lax.psum(local_shares[2].astype(jnp.bfloat16), EXPERT).astype(jnp.float32),
        lax.psum(local_shares[3].astype(jnp.bfloat16), EXPERT).astype(jnp.float32),
        lax.psum(local_shares[4].astype(jnp.bfloat16), EXPERT).astype(jnp.float32),
    )
    gain_sums = (
        by_axis(grad_attn_gain, FSDP_EXPERT),
        by_axis(grad_query_gain, FSDP_EXPERT),
        by_axis(grad_key_gain, FSDP_EXPERT),
        by_axis(grad_mlp_gain, FSDP_EXPERT),
    )
    return (
        output[None],
        input_grad.astype(jnp.bfloat16)[None],
        gain_sums[0],
        gain_sums[1],
        gain_sums[2],
        gain_sums[3],
        shares[0],
        shares[1],
        shares[2],
        shares[3],
        shares[4],
        expert_sums[0],
        expert_sums[1],
        expert_sums[2],
    )


def solution(mesh):
    torus = Mesh(mesh.devices.reshape(4, 2, 4, 4), ("fsdp_0", "fsdp_1", "expert_0", "expert_1"))
    placed = (
        P(EXPERT, FSDP, None),
        P(EXPERT, FSDP, None),
        P(EXPERT, FSDP, None),
        P(),
        P(),
        P(),
        P(),
        P(FSDP, None),
        P(FSDP, None),
        P(FSDP, None),
        P(FSDP, None),
        P(FSDP, None),
        P(EXPERT, FSDP, None),
        P(EXPERT, FSDP, None),
        P(EXPERT, FSDP, None),
    )
    return jax.shard_map(
        local,
        mesh=torus,
        in_specs=placed,
        out_specs=(
            P(EXPERT, FSDP, None),
            P(EXPERT, FSDP, None),
            P(),
            P(),
            P(),
            P(),
            P(FSDP, None),
            P(FSDP, None),
            P(FSDP, None),
            P(FSDP, None),
            P(FSDP, None),
            P(EXPERT, FSDP, None),
            P(EXPERT, FSDP, None),
            P(EXPERT, FSDP, None),
        ),
        check_vma=False,
    )
```

profile of v0, /device:TPU:0, one launch (start us, length us, event | category | flops | bytes accessed | tf_op | source)
XLA Modules:
  0.0 1166.5 jit_solution(14673234770049234152)
XLA Ops:
  11.7 104.5 %all-gather.7.cloned.1.call-done = bf16[2048,5120]{1,0:T(8,128)(2,1)} async-done(((bf16[256,5120]{1,0:T(8,128)(2,1)}), bf16[2048,5120]{1,0:T(8,128)(2,1)}) %all-gather.7.cloned.1.call-update) | async-done | bytes 20971536 | tf_op jit(solution)/shard_map/all_gather | solution.py:27
  129.6 12.8 %all_gather.24 = bf16[2048,32]{0,1:T(8,128)(2,1)S(1)} all-gather(bf16[256,32]{0,1:T(8,128)(2,1)S(1)} %copy-done.59), channel_id=1, replica_groups=mesh['fsdp_0'=4,'fsdp_1'=2,'expert_0'=4,'expert_1'=4] {'fsdp_0','fsdp_1'}, dimensions={0}, use_global_device_ids=true | all-gather | bytes 147456 | tf_op jit(solution)/shard_map/all_gather | solution.py:114
  143.7 9.0 reduce-window.6
  162.3 14.7 %slice_bitcast_fusion = bf16[4096,2048]{0,1:T(8,128)(2,1)} fusion(bf16[2048,5120]{1,0:T(8,128)(2,1)} %all-gather.7.cloned.1.call-done), kind=kLoop, calls=%fused_computation.78 | loop fusion | bytes 33554432 | tf_op jit(solution)/shard_map/dot_general | solution.py:116
  177.0 22.6 %copy.142 = bf16[4096,2048]{1,0:T(8,128)(2,1)} copy(bf16[4096,2048]{0,1:T(8,128)(2,1)} %slice_bitcast_fusion) | data formatting | bytes 33554432 | tf_op jit(solution)/shard_map/dot_general | solution.py:116
  216.6 20.6 %while.28 = (s32[]{:T(128)}, bf16[4,128,8,128]{1,3,2,0:T(8,128)(2,1)}, f32[4,8,128,1]{2,1,3,0:T(8,128)}, bf16[4,1024,128]{1,2,0:T(8,128)(2,1)}, bf16[4,1024,128]...) while((s32[]{:T(128)}, ...), condition=%wide.region_6.7_spmd.clone, body=%wide.region_3.6_spmd.clone.sunk | while | flops 548666368 | bytes 14191201 | solution.py:165
  259.1 13.6 %gather_fusion.2 = bf16[1280,2048]{1,0:T(8,128)(2,1)} fusion(bf16[1024,2048]{1,0:T(8,128)(2,1)} %fusion.69, s32[2048]{0:T(1024)S(1)} %get-tuple-element.294), kind=kCustom, calls=%fused_computation.2 | custom fusion | bytes 10490880 | tf_op jit(solution)/shard_map/gather | solution.py:226
  272.7 9.2 broadcast_select_fusion
  281.9 69.5 %all_to_all.20 = bf16[16,2,40,2048]{3,2,1,0:T(8,128)(2,1)} all-to-all(bf16[16,2,40,2048]{3,2,1,0:T(8,128)(2,1)} %get-tuple-element.279), channel_id=1, replica_groups=mesh['fsdp_0'=4,'fsdp_1'=2,'expert_0'=4,'expert_1'=4] {'expert_0','exper..., dimensions={0} | all-to-all | bytes 10485760 | tf_op jit(solution)/shard_map/all_to_all | solution.py:197
  351.3 13.3 %all-to-all-start.2 = ((bf16[16,2,40,2048]{3,2,1,0:T(8,128)(2,1)}), bf16[16,2,40,2048]{3,2,1,0:T(8,128)(2,1)}, u32[]{:S(2)}, u32[]{:S(2)}) async-start(bf16[16,2,40,2048]{3,2,1,0:T(8,128)(2,1)} %get-tuple-element.278), calls=%async_computation.2 | async-start | bytes 10485760 | tf_op jit(solution)/shard_map/all_to_all | solution.py:229
  364.7 10.6 fusion.79
  384.3 48.4 %all-to-all-done.2 = bf16[16,2,40,2048]{3,2,1,0:T(8,128)(2,1)} async-done(((bf16[16,2,40,2048]{3,2,1,0:T(8,128)(2,1)}), bf16[16,2,40,2048]{3,2,1,0:T(8,128)(2,1)}, u32[]{:S(2)}, u32[]{:S(2)}) %all-to-all-start.2) | async-done | bytes 5242912 | tf_op jit(solution)/shard_map/all_to_all | solution.py:229
  432.8 14.9 %fusion.94 = (bf16[16,2,40,768]{3,2,0,1:T(8,128)(2,1)}, bf16[16,2,40,768]{3,2,0,1:T(8,128)(2,1)}, bf16[16,2,40,768]{3,2,0,1:T(8,128)(2,1)}) fusion(f32[2,768,16,40]{1,3,2,0:T(8,128)} %fusion.79, f32[2,768,16,40]{1,3,2,0:T(8,128)} %fusion.81, bf16[2,768,2048]{2,1,0:T(8,128)(2,1)} %all-gather.15.cloned.1.call-done, bf16[16,2,40,2048]{3,2,1,0:T(8,128)(2,1)} %all-to-all-done.2), kind=kOutput, calls=%fused_computation.121 | convolution fusion | flops 4042260480 | bytes 25296896 | tf_op jit(solution)/shard_map/secd,efd->secf/dot_general | solution.py:230
  447.6 11.5 fusion.78
  459.1 13.0 %fusion.74 = bf16[16,2,40,2048]{3,2,0,1:T(8,128)(2,1)} fusion(f32[2,2048,16,40]{1,3,2,0:T(8,128)} %fusion.78, bf16[16,2,40,768]{3,2,0,1:T(8,128)(2,1)} %get-tuple-element.258, bf16[4,2048,768]{2,1,0:T(8,128)(2,1)} %all-gather.13.cloned.1.call-done), kind=kOutput, calls=%fused_computation.99 | convolution fusion | flops 4031774720 | bytes 23986176 | tf_op jit(solution)/shard_map/secf,edf->secd/dot_general | solution.py:247
  493.0 63.5 %all-to-all-done.3 = bf16[16,2,40,2048]{3,2,1,0:T(8,128)(2,1)} async-done(((bf16[16,2,40,2048]{3,2,1,0:T(8,128)(2,1)}), bf16[16,2,40,2048]{3,2,1,0:T(8,128)(2,1)}, u32[]{:S(2)}, u32[]{:S(2)}) %all-to-all-start.3) | async-done | bytes 5242912 | tf_op jit(solution)/shard_map/all_to_all | solution.py:249
  562.4 12.4 %gather_fusion.3 = bf16[1024,2048]{1,0:T(8,128)(2,1)} fusion(bf16[1280,2048]{1,0:T(8,128)(2,1)} %bitcast.43, s32[1024]{0:T(1024)S(1)} %broadcast_clamp_fusion), kind=kCustom, calls=%fused_computation.3 | custom fusion | bytes 8392704 | tf_op jit(solution)/shard_map/gather | solution.py:251
  580.8 50.8 %all-to-all-done.1 = bf16[16,2,40,2048]{3,2,1,0:T(8,128)(2,1)} async-done(((bf16[16,2,40,2048]{3,2,1,0:T(8,128)(2,1)}), bf16[16,2,40,2048]{3,2,1,0:T(8,128)(2,1)}, u32[]{:S(2)}, u32[]{:S(2)}) %all-to-all-start.1) | async-done | bytes 5242912 | tf_op jit(solution)/shard_map/all_to_all | solution.py:211
  631.6 12.1 %gather_fusion.1 = bf16[1024,2048]{1,0:T(8,128)(2,1)} fusion(bf16[1280,2048]{1,0:T(8,128)(2,1)} %bitcast.30, s32[1024]{0:T(1024)S(1)} %broadcast_clamp_fusion), kind=kCustom, calls=%fused_computation.1 | custom fusion | bytes 8392704 | tf_op jit(solution)/shard_map/gather | solution.py:213
  654.4 12.4 %fusion.112 = bf16[16,8,32,128]{3,1,2,0:T(8,128)(2,1)} fusion(bf16[128,2048]{1,0:T(8,128)(2,1)S(1)} %fusion.169, bf16[4096,2048]{1,0:T(8,128)(2,1)} %all-gather.11.cloned.1.call-done), kind=kOutput, calls=%fused_computation.157 | convolution fusion | flops 2148007936 | bytes 18350080 | tf_op jit(solution)/shard_map/td,id->ti/dot_general | solution.py:274
  669.8 50.4 %while.29 = (s32[]{:T(128)}, bf16[4,128,8,128]{1,3,2,0:T(8,128)(2,1)}, bf16[4,1024,128]{1,2,0:T(8,128)(2,1)}, bf16[4,1024,128]{1,2,0:T(8,128)(2,1)}, bf16[4,1024...) while((s32[]{:T(128)}, ...), condition=%wide.region_24.25_spmd.clone, body=%wide.region_22.24_spmd.clone.sunk | while | flops 1358429184 | bytes 61375188 | solution.py:308
  734.9 22.0 %reduce-scatter.10.cloned.1.call-done = bf16[128,1024]{1,0:T(8,128)(2,1)} async-done(((bf16[1024,1024]{1,0:T(8,128)(2,1)}), bf16[128,1024]{1,0:T(8,128)(2,1)}) %reduce-scatter.10.cloned.1.call-update) | async-done | bytes 262160
  763.9 9.8 bitcast_convert_fusion
  782.5 9.5 bitcast_convert_fusion.2
  798.0 118.9 %all-gather.17.cloned.1.call-done = bf16[1024,15392]{0,1:T(8,128)(2,1)} async-done(((bf16[128,15392]{0,1:T(8,128)(2,1)}), bf16[1024,15392]{0,1:T(8,128)(2,1)}) %all-gather.17.cloned.1.call-update) | async-done | bytes 31522832 | tf_op jit(solution)/shard_map/all_gather | solution.py:27
  942.8 10.4 fusion.63
  959.9 15.7 %all-reduce.2 = (f32[2048]{0:T(1024)S(1)}, f32[128]{0:T(128)S(1)}, f32[128]{0:T(128)S(1)}, f32[2048]{0:T(1024)S(1)}) all-reduce(f32[2048]{0:T(1024)S(1)} %get-tuple-element.192, f32[128]{0:T(128)S(1)} %copy-done.73, f32[128]{0:T(128)S(1)} %get-tuple-element.194, ...), channel_id=1, replica_groups=mesh['fsdp_0'=4,'fsdp_1'=2,'expert_0'=4,'expert_1'=4] {'fsdp_0'}, use_global_device_ids=true, to_apply=%region_30.31 | all-reduce | flops 4352 | bytes 34816 | tf_op jit(solution)/shard_map/psum | solution.py:41
  979.0 17.0 %all-reduce.1 = (f32[2048]{0:T(1024)S(1)}, f32[128]{0:T(128)S(1)}, f32[128]{0:T(128)S(1)}, f32[2048]{0:T(1024)S(1)}) all-reduce(f32[2048]{0:T(1024)S(1)} %get-tuple-element.242, f32[128]{0:T(128)S(1)} %get-tuple-element.243, ...), channel_id=1, replica_groups=mesh['fsdp_0'=4,'fsdp_1'=2,'expert_0'=4,'expert_1'=4] {'expert_0'}, use_global_device_ids=true, to_apply=%region_32.33 | all-reduce | flops 4352 | bytes 34816 | tf_op jit(solution)/shard_map/psum | solution.py:41
  995.9 17.5 %all-reduce = (f32[2048]{0:T(1024)}, f32[128]{0:T(128)}, f32[128]{0:T(128)}, f32[2048]{0:T(1024)}) all-reduce(f32[2048]{0:T(1024)S(1)} %get-tuple-element.234, f32[128]{0:T(128)S(1)} %get-tuple-element.235, f32[128]{0:T(128)S(1)} %get-tuple-element.236, ...), channel_id=1, replica_groups=mesh['fsdp_0'=4,'fsdp_1'=2,'expert_0'=4,'expert_1'=4] {'expert_1'}, use_global_device_ids=true, to_apply=%region_33.34 | all-reduce | flops 4352 | bytes 34816 | tf_op jit(solution)/shard_map/psum | solution.py:41
  1019.0 18.6 %reduce-scatter.6.cloned.1.call-done = bf16[4,256,768]{2,1,0:T(8,128)(2,1)} async-done(((bf16[4,2048,768]{2,1,0:T(8,128)(2,1)}), bf16[4,256,768]{2,1,0:T(8,128)(2,1)}) %reduce-scatter.6.cloned.1.call-update) | async-done | bytes 1572880 | tf_op jit(solution)/shard_map/reduce_scatter | solution.py:33
  1042.3 75.1 %psum.167 = bf16[256,32]{0,1:T(8,128)(2,1)S(1)} all-reduce(bf16[256,32]{0,1:T(8,128)(2,1)S(1)} %convolution_convert_fusion.3), channel_id=1, replica_groups=mesh['fsdp_0'=4,'fsdp_1'=2,'expert_0'=4,'expert_1'=4] {'expert_0','exper..., use_global_device_ids=true, to_apply=%region_53.54 | all-reduce | flops 8192 | bytes 32768 | tf_op jit(solution)/shard_map/psum | solution.py:400
  1118.0 32.8 %all-reduce.7.cloned.1.call-done = (bf16[256,4096]{1,0:T(8,128)(2,1)}, bf16[256,512]{1,0:T(8,128)(2,1)}, bf16[256,512]{1,0:T(8,128)(2,1)}, bf16[512,2048]{1,0:T(8,128)(2,1)}) async-done(((bf16[256,4096]{1,0:T(8,128)(2,1)}, bf16[256,512]{1,0:T(8,128)(2,1)}, bf16[256,512]{1,0:T(8,128)(2,1)}, bf16[512,2048]{1,0:T(8,128)(2,1)}), (bf16[256,4096]{1,0:T(8,128)(2,1)}, bf16[256,512]{1,0:T(8,128)(2,1)}, ...) | async-done | bytes 4718608 | tf_op jit(solution)/shard_map/psum | solution.py:396
  (388 shorter events, 284.6 us)
Async XLA Ops:
  7.2 109.0 %all-gather.7.cloned.1.call-start = ((), (), s32[]{:S(2)}) async-start(), calls=%async_computation.7 | async-start | bytes 23592960 | tf_op jit(solution)/shard_map/all_gather | solution.py:27
  10.8 199.8 %all-gather.9.cloned.1.call-start = ((), (), s32[]{:S(2)}) async-start(), calls=%async_computation.8 | async-start | bytes 2359296 | tf_op jit(solution)/shard_map/all_gather | solution.py:27
  11.2 188.4 %copy-start.69 = (f32[128]{0:T(128)}, f32[128]{0:T(128)S(1)}, u32[]{:S(2)}) copy-start(f32[128]{0:T(128)S(1)} %add_rsqrt_fusion.3) | copy-start | bytes 1540
  11.5 197.1 %copy-start.30 = (f32[128,128]{0,1:T(8,128)}, f32[128,128]{0,1:T(8,128)S(1)}, u32[]{:S(2)}) copy-start(f32[128,128]{0,1:T(8,128)S(1)} %get-tuple-element.282) | copy-start | bytes 196612
  11.5 197.1 %copy-start.36 = (f32[128,128]{0,1:T(8,128)}, f32[128,128]{0,1:T(8,128)S(1)}, u32[]{:S(2)}) copy-start(f32[128,128]{0,1:T(8,128)S(1)} %get-tuple-element.283) | copy-start | bytes 196612
  11.7 112.0 %copy-start.33 = (bf16[128,2048]{1,0:T(8,128)(2,1)}, bf16[128,2048]{1,0:T(8,128)(2,1)S(1)}, u32[]{:S(2)}) copy-start(bf16[128,2048]{1,0:T(8,128)(2,1)S(1)} %fusion.122) | copy-start | bytes 1572868
  126.5 113.5 %all-gather.11.cloned.1.call-start = ((), (), s32[]{:S(2)}) async-start(), calls=%async_computation.9 | async-start | bytes 18874368 | tf_op jit(solution)/shard_map/all_gather | solution.py:113
  127.3 237.4 %all-gather.13.cloned.1.call-start = ((), (), s32[]{:S(2)}) async-start(), calls=%async_computation.10 | async-start | bytes 14155776 | tf_op jit(solution)/shard_map/all_gather | solution.py:27
  128.6 255.7 %all-gather.15.cloned.1.call-start = ((), (), s32[]{:S(2)}) async-start(), calls=%async_computation.11 | async-start | bytes 7077888 | tf_op jit(solution)/shard_map/all_gather | solution.py:195
  248.6 403.6 %copy-start.5 = (f32[128,2048]{1,0:T(8,128)}, f32[128,2048]{1,0:T(8,128)S(1)}, u32[]{:S(2)}) copy-start(f32[128,2048]{1,0:T(8,128)S(1)} %get-tuple-element.289) | copy-start | bytes 3145732
  248.7 403.6 %copy-start.65 = (f32[128]{0:T(128)}, f32[128]{0:T(128)S(1)}, u32[]{:S(2)}) copy-start(f32[128]{0:T(128)S(1)} %add_rsqrt_fusion.2) | copy-start | bytes 1540
  351.3 81.4 %all-to-all-start.2 = ((bf16[16,2,40,2048]{3,2,1,0:T(8,128)(2,1)}), bf16[16,2,40,2048]{3,2,1,0:T(8,128)(2,1)}, u32[]{:S(2)}, u32[]{:S(2)}) async-start(bf16[16,2,40,2048]{3,2,1,0:T(8,128)(2,1)} %get-tuple-element.278), calls=%async_computation.2 | async-start | bytes 10485760 | tf_op jit(solution)/shard_map/all_to_all | solution.py:229
  477.7 78.8 %all-to-all-start.3 = ((bf16[16,2,40,2048]{3,2,1,0:T(8,128)(2,1)}), bf16[16,2,40,2048]{3,2,1,0:T(8,128)(2,1)}, u32[]{:S(2)}, u32[]{:S(2)}) async-start(bf16[16,2,40,2048]{3,2,1,0:T(8,128)(2,1)} %copy.158), calls=%async_computation.3 | async-start | bytes 10485760 | tf_op jit(solution)/shard_map/all_to_all | solution.py:249
  493.0 68.2 %copy-start.61 = (s32[1024,1]{0,1:T(1,128)S(1)}, s32[1024,1]{0,1:T(1,128)}, u32[]{:S(2)}) copy-start(s32[1024,1]{0,1:T(1,128)} %copy-done.60) | copy-start | bytes 12292
  493.0 68.3 %copy-start.25 = (bf16[128,4,8,128]{3,2,1,0:T(8,128)(2,1)S(1)}, bf16[128,4,8,128]{3,2,1,0:T(8,128)(2,1)}, u32[]{:S(2)}) copy-start(bf16[128,4,8,128]{3,2,1,0:T(8,128)(2,1)} %get-tuple-element.263) | copy-start | bytes 3145732
  556.5 75.1 %all-to-all-start.1 = ((bf16[16,2,40,2048]{3,2,1,0:T(8,128)(2,1)}), bf16[16,2,40,2048]{3,2,1,0:T(8,128)(2,1)}, u32[]{:S(2)}, u32[]{:S(2)}) async-start(bf16[16,2,40,2048]{3,2,1,0:T(8,128)(2,1)} %copy.153), calls=%async_computation.1 | async-start | bytes 10485760 | tf_op jit(solution)/shard_map/all_to_all | solution.py:211
  561.2 195.7 %reduce-scatter.10.cloned.1.call-start = ((), (), s32[]{:S(2)}) async-start(), calls=%async_computation.15 | async-start | bytes 2359296
  724.5 192.4 %all-gather.17.cloned.1.call-start = ((), (), s32[]{:S(2)}) async-start(), calls=%async_computation.12 | async-start | bytes 35463168 | tf_op jit(solution)/shard_map/all_gather | solution.py:27
  732.9 26.0 %copy-start.57 = (f32[128,4]{0,1:T(4,128)S(1)}, f32[128,4]{0,1:T(4,128)}, u32[]{:S(2)}) copy-start(f32[128,4]{0,1:T(4,128)} %copy-done.56) | copy-start | bytes 6148
  732.9 27.6 %copy-start.19 = (bf16[4,128,8,128]{1,3,2,0:T(8,128)(2,1)S(1)}, bf16[4,128,8,128]{1,3,2,0:T(8,128)(2,1)}, u32[]{:S(2)}) copy-start(bf16[4,128,8,128]{1,3,2,0:T(8,128)(2,1)} %get-tuple-element.106) | copy-start | bytes 3145732
  733.9 27.7 %copy-start.35 = (bf16[128,2048]{0,1:T(8,128)(2,1)S(1)}, bf16[128,2048]{0,1:T(8,128)(2,1)}, u32[]{:S(2)}) copy-start(bf16[128,2048]{0,1:T(8,128)(2,1)} %copy.163) | copy-start | bytes 1572868
  734.9 27.5 %copy-start.34 = (bf16[128,2048]{0,1:T(8,128)(2,1)S(1)}, bf16[128,2048]{0,1:T(8,128)(2,1)}, u32[]{:S(2)}) copy-start(bf16[128,2048]{0,1:T(8,128)(2,1)} %copy.164) | copy-start | bytes 1572868
  734.9 28.3 %copy-start.50 = (bf16[128,32]{0,1:T(8,128)(2,1)S(1)}, bf16[128,32]{0,1:T(8,128)(2,1)}, u32[]{:S(2)}) copy-start(bf16[128,32]{0,1:T(8,128)(2,1)} %copy-done.49) | copy-start | bytes 24580
  763.8 252.7 %reduce-scatter.8.cloned.1.call-start = ((), (), s32[]{:S(2)}) async-start(), calls=%async_computation.14 | async-start | bytes 7077888 | tf_op jit(solution)/shard_map/reduce_scatter | solution.py:267
  773.7 263.9 %reduce-scatter.6.cloned.1.call-start = ((), (), s32[]{:S(2)}) async-start(), calls=%async_computation.13 | async-start | bytes 14155776 | tf_op jit(solution)/shard_map/reduce_scatter | solution.py:33
  797.7 353.0 %all-reduce.7.cloned.1.call-start = ((), (), s32[]{:S(2)}) async-start(), calls=%async_computation.16 | async-start | bytes 9437184 | tf_op jit(solution)/shard_map/psum | solution.py:396
  953.3 60.1 %copy-start.6 = (f32[128,2048]{1,0:T(8,128)S(1)}, f32[128,2048]{1,0:T(8,128)}, u32[]{:S(2)}) copy-start(f32[128,2048]{1,0:T(8,128)} %copy-done.5) | copy-start | bytes 3145732
  953.3 60.1 %copy-start.18 = (f32[128,2048]{1,0:T(8,128)S(1)}, f32[128,2048]{1,0:T(8,128)}, u32[]{:S(2)}) copy-start(f32[128,2048]{1,0:T(8,128)} %copy-done.17) | copy-start | bytes 3145732
  953.3 60.1 %copy-start.23 = (bf16[1,128,2048]{2,1,0:T(8,128)(2,1)S(1)}, bf16[1,128,2048]{2,1,0:T(8,128)(2,1)}, u32[]{:S(2)}) copy-start(bf16[1,128,2048]{2,1,0:T(8,128)(2,1)} %param.21) | copy-start | bytes 1572868
  953.3 60.1 %copy-start.48 = (f32[2048]{0:T(1024)S(1)}, f32[2048]{0:T(1024)}, u32[]{:S(2)}) copy-start(f32[2048]{0:T(1024)} %param.25) | copy-start | bytes 24580
  953.4 60.1 %copy-start.66 = (f32[128]{0:T(128)S(1)}, f32[128]{0:T(128)}, u32[]{:S(2)}) copy-start(f32[128]{0:T(128)} %copy-done.65) | copy-start | bytes 1540
  953.4 60.1 %copy-start.72 = (f32[128]{0:T(128)S(1)}, f32[128]{0:T(128)}, u32[]{:S(2)}) copy-start(f32[128]{0:T(128)} %copy-done.71) | copy-start | bytes 1540
  (66 other events, 375.9 us)
Sparse Core Ops, SparseCore 0:
  10.9 105.2 all-gather.6
  126.7 26.1 all-gather.8
  154.6 85.3 all-gather.10
  242.2 67.9 all-gather.12
  311.7 41.3 all-gather.14
  724.6 32.2 reduce-scatter.9
  763.9 152.9 all-gather.16
  919.3 43.6 reduce-scatter.7
  965.4 72.1 reduce-scatter.5
  1042.3 108.3 all-reduce.6
where the time goes:
time: 1180 us; the launch traced here: 1170 us
  waiting for transfers between devices  464 us (39%)
  matrix products  217 us (18%)
  blocking collectives  211 us (18%)
  local copies, waits for them, and re-layouts  151 us (13%)
  other arithmetic  83.7 us (7%)
  starting transfers between devices  23.7 us (2%)
  between operations  15.7 us (1%)
    all_gather x4, waiting for transfers between devices, sent_together(): filled = lax.all_gather(both, axis, axis=dim, tiled=True)  223 us
    psum x1, blocking collectives, local(): lax.psum(local_shares[4].astype(jnp.bfloat16), EXPERT).astype(jnp.float32)  75.1 us
    all_to_all x1, blocking collectives, local(): lax.all_to_all(send_rows, EXPERT, split_axis=0, concat_axis=0, tiled=True)  69.5 us
    all_to_all x1, waiting for transfers between devices, local(): lax.all_to_all(row_grads, EXPERT, split_axis=0, concat_axis=0, tiled=True)  63.5 us
    psum x4, blocking collectives, by_axis(): return functools.reduce(lax.psum, axes, value)  53.6 us
    all_to_all x1, waiting for transfers between devices, local(): lax.all_to_all(expert_out, EXPERT, split_axis=0, concat_axis=0, tiled=True)  50.8 us
    all_to_all x1, waiting for transfers between devices, local(): lax.all_to_all(send_grads, EXPERT, split_axis=0, concat_axis=0, tiled=True)  48.4 us
    dot_general x2, local copies, waits for them, and re-layouts, local(): jnp.dot(first_hidden, query_full, preferred_element_type=jnp.float32)  37.3 us
  transfers between devices with their start and end apart: 13, of which 9 were waited for; matrix products, arithmetic and copies ran while one was open for 24% of the time, Pallas kernels for 0%

commit v1 on v0

v1 whole, which is shorter than its diff:
```python
import functools

import jax
import jax.numpy as jnp
from jax import lax
from jax.experimental import pallas as pl
from jax.experimental.pallas import tpu as pltpu
from jax.sharding import Mesh
from jax.sharding import PartitionSpec as P

MODEL_WIDTH = 2048
QUERY_HEADS = 32
KEY_VALUE_HEADS = 4
HEAD_SIZE = 128
TOPK = 8
EXPERTS = 32
CAP = 40
Z, C, Y, X = "z", "c", "y", "x"
FSDP = (Z, C)
EXPERT = (Y, X)
ALL = (Z, C, Y, X)

bf16 = jnp.bfloat16
f32 = jnp.float32
epsilon = 1e-06
rope_base = 1000000.0


def dot(a, b):
    return jnp.dot(a, b, preferred_element_type=f32)


def es(spec, a, b):
    return jnp.einsum(spec, a, b, preferred_element_type=f32)


def shift(v, axis, by):
    n = 2 if axis == C else 4
    return lax.ppermute(v, axis, [(i, (i + by) % n) for i in range(n)])


def gather_fsdp(p):
    half = p.shape[0] // 2
    up, down, other = shift(p, Z, -1), shift(p, Z, 1), shift(p, C, 1)
    far_low, far_high = shift(down[:half], Z, 1), shift(up[half:], Z, -1)
    far = [(up, 1, 0), (down, 3, 0), (far_low, 2, 0), (far_high, 2, half)]
    return (
        [(p, 0, 0, 0), (other, 0, 1, 0)]
        + [(a, dz, 0, r) for a, dz, r in far]
        + [(shift(a, C, 1), dz, 1, r) for a, dz, r in far]
    )


def scatter_fsdp(keep, send):
    got = shift(send, C, 1)
    half = keep.shape[1] // 2

    def both(d, rows=slice(None)):
        return (keep[d, rows].astype(f32) + got[d, rows].astype(f32)).astype(bf16)

    low, high = slice(None, half), slice(half, None)
    far_low, far_high = both(2, low), both(2, high)
    from_down, from_up = shift(far_low, Z, 1), shift(far_high, Z, -1)
    one, three = both(1), both(3)
    one = jnp.concatenate([(one[low].astype(f32) + from_down.astype(f32)).astype(bf16), one[high]])
    three = jnp.concatenate([three[low], (three[high].astype(f32) + from_up.astype(f32)).astype(bf16)])
    from_down, from_up = shift(one, Z, 1), shift(three, Z, -1)
    own = keep[0].astype(f32) + got[0].astype(f32)
    return own + from_down.astype(f32) + from_up.astype(f32)


def gather_ring(v, axis):
    half = v.shape[0] // 2
    up, down = shift(v, axis, -1), shift(v, axis, 1)
    return v, up, shift(down[:half], axis, 1), shift(up[half:], axis, -1), down


def gather_plane(left, right):
    def stacked(parts):
        a, b, low, high, d = parts
        return jnp.stack([a, b, jnp.concatenate([low, high]), d])

    left, right = gather_ring(left, X), gather_ring(right, Y)
    return gather_ring(stacked(left), Y), gather_ring(stacked(right), X)


def scatter_ring(parts, axis):
    own, one, low, high, three = parts
    k = low.shape[0]
    down, up = shift(low, axis, 1), shift(high, axis, -1)

    def plus(a, b):
        return (a.astype(f32) + b.astype(f32)).astype(bf16)

    one = jnp.concatenate([plus(one[:k], down), one[k:]])
    three = jnp.concatenate([three[:k], plus(three[k:], up)])
    down, up = shift(one, axis, 1), shift(three, axis, -1)
    return own.astype(f32) + down.astype(f32) + up.astype(f32)


def scatter_plane(left, right):
    def halves(v):
        v = v.astype(bf16)
        k = v.shape[1] // 2
        return v[0], v[1], v[2, :k], v[2, k:], v[3]

    left = scatter_ring(halves(scatter_ring(left, Y)), X)
    right = scatter_ring(halves(scatter_ring(right, X)), Y)
    return left, right


def sum_all(v):
    v = v + shift(v, C, 1)
    for axis in (Z, Y, X):
        v = (v + shift(v, axis, 1)) + (shift(v, axis, 2) + shift(v, axis, 3))
    return v


def inv_rms(values):
    return lax.rsqrt(jnp.mean(values * values, axis=-1, keepdims=True) + epsilon)


def norm_back(grad_norm, normed, scale_part):
    return scale_part * (grad_norm - normed * jnp.mean(grad_norm * normed, axis=-1, keepdims=True))


def turned(values):
    middle = values.shape[-1] // 2
    return jnp.concatenate([-values[..., middle:], values[..., :middle]], axis=-1)


def turned_back(values):
    middle = values.shape[-1] // 2
    return jnp.concatenate([values[..., middle:], -values[..., :middle]], axis=-1)


def rope_tables(positions):
    frequency = rope_base ** (-(jnp.arange(HEAD_SIZE // 2).astype(f32) * 2.0 / HEAD_SIZE))
    frequency = jnp.concatenate([frequency, frequency])
    angles = positions[:, None] * frequency[None, :]
    return jnp.cos(angles), jnp.sin(angles)


def mm(a, b, dims=((1,), (0,))):
    return lax.dot_general(a, b, (dims, ((), ())), preferred_element_type=f32)


NT = ((1,), (1,))
TN = ((0,), (0,))
ANY = pl.BlockSpec(memory_space=pl.ANY)
VM = pl.BlockSpec(memory_space=pltpu.VMEM)
SM = pl.BlockSpec(memory_space=pltpu.SMEM)
MIB = 1 << 20


def part_of(outer, inner):
    return {0: (0, inner), 1: (1, inner), 2: (2 + inner // 2, inner % 2), 3: (4, inner)}[outer]


def load_pieces(place, spec, pieces, whole, sems):
    copies = []
    for k, (dz, dc, first, rows) in enumerate(spec):
        at = lax.rem(place[0] + dz, 4) * 256 + lax.rem(place[1] + dc, 2) * 128 + first
        at = pl.multiple_of(at, 64)
        copies.append(pltpu.make_async_copy(pieces[k], whole.at[pl.ds(at, rows)], sems.at[k]))
    for copy in copies:
        copy.start()
    return copies


def attention_kernel(spec, place, w_own, w_other, w_out, q_gain, k_gain, cosine, sine, *rest):
    n = len(spec)
    pieces, rest = rest[:n], rest[n:]
    h1, q_raw, k_raw, v_b, q_b, k_b, a_b, lse, keep, send, sems = rest
    z, c = place[0], place[1]
    for copy in load_pieces(place, spec, pieces, h1, sems):
        copy.wait()

    @pl.loop(0, 4)
    def _(i):
        rows = pl.ds(pl.multiple_of(i * 256, 256), 256)
        t = mm(h1[rows], w_own[...])
        other = mm(h1[rows], w_other[...])
        key = jnp.where(c == 0, t[:, 512:], other)
        q_raw[rows] = t[:, :512]
        k_raw[rows] = key
        v_b[rows] = jnp.where(c == 0, other, t[:, 512:]).astype(bf16)
        co, si = cosine[rows], sine[rows]

        def rotated(u, gain):
            u = u * lax.rsqrt(jnp.mean(u * u, axis=-1, keepdims=True) + epsilon) * gain
            return (u * co + pltpu.roll(u, 64, 1) * si).astype(bf16)

        for h in range(4):
            q_b[h, rows] = rotated(t[:, 128 * h : 128 * h + 128], q_gain[...])
        k_b[rows] = rotated(key, k_gain[...])

    lane = lax.broadcasted_iota(jnp.int32, (256, 128), 1)
    below = lax.broadcasted_iota(jnp.int32, (256, 256), 0) >= lax.broadcasted_iota(
        jnp.int32, (256, 256), 1
    )
    for i in range(4):
        n_keys = 256 * (i + 1)
        rows = slice(256 * i, n_keys)
        logs = jnp.zeros((256, 128), f32)
        for h in range(4):
            s = mm(q_b[h, rows], k_b[:n_keys], NT) * (HEAD_SIZE**-0.5)
            e = jnp.exp(s)
            tail = jnp.where(below, e[:, n_keys - 256 :], 0.0)
            e = tail if i == 0 else jnp.concatenate([e[:, : n_keys - 256], tail], axis=1)
            total = jnp.sum(e, axis=1, keepdims=True)
            a = mm(e.astype(bf16), v_b[:n_keys]) / total
            a_b[rows, 128 * h : 128 * h + 128] = a.astype(bf16)
            logs = jnp.where(lane == h, jnp.log(total), logs)
        lse[rows] = logs
        part = mm(a_b[rows], w_out[...]).astype(bf16)
        dz = lax.rem(i - z + 4, 4)
        first, second = part[:128], part[128:]
        keep[dz] = jnp.where(c == 0, first, second)
        send[dz] = jnp.where(c == 0, second, first)


def attention_forward(pieces, place, w_own, w_other, w_out, q_gain, k_gain, cosine, sine):
    spec = [(dz, dc, first, a.shape[0]) for a, dz, dc, first in pieces]
    seq = 1024
    shapes = [
        ((seq, MODEL_WIDTH), bf16),
        ((seq, 512), f32),
        ((seq, 128), f32),
        ((seq, 128), bf16),
        ((4, seq, 128), bf16),
        ((seq, 128), bf16),
        ((seq, 512), bf16),
        ((seq, 128), f32),
        ((4, 128, MODEL_WIDTH), bf16),
        ((4, 128, MODEL_WIDTH), bf16),
    ]
    return pl.pallas_call(
        functools.partial(attention_kernel, spec),
        out_shape=[jax.ShapeDtypeStruct(*s) for s in shapes],
        in_specs=[SM] + [VM] * 7 + [ANY] * len(spec),
        out_specs=[VM] * len(shapes),
        scratch_shapes=[pltpu.SemaphoreType.DMA((len(spec),))],
        compiler_params=pltpu.CompilerParams(vmem_limit_bytes=56 * MIB),
        cost_estimate=pl.CostEstimate(flops=9 << 30, bytes_accessed=28 << 20, transcendentals=3 << 20),
        name="attention_forward",
    )(place, w_own, w_other, w_out, q_gain, k_gain, cosine, sine, *[p[0] for p in pieces])


def rows_kernel(n_pieces, idx, target, *rest):
    pieces, (out, whole, sems) = rest[:n_pieces], rest[n_pieces:]
    waits = [[] for _ in range(8)]
    k = 0

    def start(r0, source, into):
        nonlocal k
        copy = pltpu.make_async_copy(source, into, sems.at[k])
        copy.start()
        waits[r0 // 2].append(copy)
        k += 1

    width = MODEL_WIDTH // 2
    for r in range(16):
        dy, dx = divmod(r, 4)
        if n_pieces == 1:
            start(r, pieces[0].at[idx[r], :, pl.ds(0, MODEL_WIDTH)], whole.at[r])
            continue
        a, ai = part_of(dy, dx)
        b, bi = part_of(dx, dy)
        start(r, pieces[a].at[ai], whole.at[r, :, pl.ds(0, width)])
        start(r, pieces[5 + b].at[bi], whole.at[r, :, pl.ds(width, width)])
    slots = lax.broadcasted_iota(jnp.int32, (80, 256), 0)
    for p in range(8):
        for copy in waits[p]:
            copy.wait()
        h = whole[2 * p : 2 * p + 2].reshape(256, MODEL_WIDTH)
        both = jnp.concatenate(
            [jnp.where(slots == target[p, e : e + 1], 1.0, 0.0) for e in range(2)], axis=0
        )
        rows = mm(both.astype(bf16), h).astype(bf16)
        out[0, 80 * p : 80 * p + 80] = rows[:80]
        out[1, 80 * p : 80 * p + 80] = rows[80:]


def slot_rows(pieces, idx, target):
    n = len(pieces)
    return pl.pallas_call(
        functools.partial(rows_kernel, n),
        out_shape=jax.ShapeDtypeStruct((2, 640, MODEL_WIDTH), bf16),
        in_specs=[SM, VM] + [ANY] * n,
        out_specs=VM,
        scratch_shapes=[pltpu.VMEM((16, 128, MODEL_WIDTH), bf16), pltpu.SemaphoreType.DMA((32,))],
        compiler_params=pltpu.CompilerParams(vmem_limit_bytes=40 * MIB),
        cost_estimate=pl.CostEstimate(flops=3 << 30, bytes_accessed=14 << 20, transcendentals=0),
        name="slot_rows",
    )(idx, target, *pieces)


def expert_kernel(xs, dys, gate, w_gate, w_up, w_down, dhr, hidden, dgate, dg, du, g_s, u_s, d_s):
    g_s[...] = mm(xs[0], w_gate[0])
    u_s[...] = mm(xs[0], w_up[0])
    d_s[...] = mm(dys[0], w_down[0], NT)

    @pl.loop(0, 10)
    def _(i):
        rows = pl.ds(pl.multiple_of(i * 64, 64), 64)
        g, u, d, s = g_s[rows], u_s[rows], d_s[rows], gate[0, rows][:, 0:1]
        sig = 1.0 / (1.0 + jnp.exp(-g))
        act = g * sig
        hid = act * u
        dgate[0, rows] = jnp.broadcast_to(jnp.sum(d * hid, axis=1, keepdims=True), (64, 128))
        hidden[0, rows] = (hid * s).astype(bf16)
        d = d * s
        du[0, rows] = (d * act).astype(bf16)
        dg[0, rows] = (d * u * sig * (1.0 + g * (1.0 - sig))).astype(bf16)

    dhr[0] = (mm(dg[0], w_gate[0], NT) + mm(du[0], w_up[0], NT)).astype(bf16)


def expert_rows(xs, dys, gate, w_gate, w_up, w_down):
    def one(*dims):
        return pl.BlockSpec((1, *dims), lambda e: (e, 0, 0))

    ff = w_down.shape[1]
    outs = [(MODEL_WIDTH, bf16), (ff, bf16), (128, f32), (ff, bf16), (ff, bf16)]
    return pl.pallas_call(
        expert_kernel,
        grid=(2,),
        out_shape=[jax.ShapeDtypeStruct((2, 640, n), t) for n, t in outs],
        in_specs=[one(640, MODEL_WIDTH)] * 2 + [one(640, 128)] + [one(MODEL_WIDTH, ff)] * 2 + [one(ff, MODEL_WIDTH)],
        out_specs=[one(640, n) for n, _ in outs],
        scratch_shapes=[pltpu.VMEM((640, ff), f32)] * 3,
        compiler_params=pltpu.CompilerParams(vmem_limit_bytes=60 * MIB),
        cost_estimate=pl.CostEstimate(flops=20 << 30, bytes_accessed=44 << 20, transcendentals=1 << 20),
        name="expert_rows",
    )(xs, dys, gate, w_gate, w_up, w_down)


def combine_kernel(target, rows, *outs):
    left, right = outs[:5], outs[5:]
    lane = lax.broadcasted_iota(jnp.int32, (256, 160), 1)
    width = MODEL_WIDTH // 2
    for p in range(8):
        t = target[p]
        pick = (lane == t[:, 0:1]) | (lane == t[:, 1:2])
        part = jnp.concatenate([rows[0, 80 * p : 80 * p + 80], rows[1, 80 * p : 80 * p + 80]], axis=0)
        whole = mm(jnp.where(pick, 1.0, 0.0).astype(bf16), part).astype(bf16)
        dy, dx0 = divmod(2 * p, 4)
        for b in range(2):
            dx = dx0 + b
            one = whole[128 * b : 128 * b + 128]
            a, ai = part_of(dy, dx)
            c, ci = part_of(dx, dy)
            left[a][ai] = one[:, :width]
            right[c][ci] = one[:, width:]


def combine(target, rows):
    width = MODEL_WIDTH // 2
    sizes = [4, 4, 2, 2, 4] * 2
    outs = pl.pallas_call(
        combine_kernel,
        out_shape=[jax.ShapeDtypeStruct((n, 128, width), bf16) for n in sizes],
        in_specs=[VM, VM],
        out_specs=[VM] * 10,
        compiler_params=pltpu.CompilerParams(vmem_limit_bytes=40 * MIB),
        cost_estimate=pl.CostEstimate(flops=2 << 30, bytes_accessed=14 << 20, transcendentals=0),
        name="combine",
    )(target, rows)
    return outs[:5], outs[5:]


def attention_back_kernel(spec, place, w_out, a_b, q_b, k_b, v_b, lse, q_raw, q_gain, cosine, sine, *rest):
    n = len(spec)
    pieces, rest = rest[:n], rest[n:]
    da, dq_raw, dkv, gain, dob, sems = rest
    for copy in load_pieces(place, spec, pieces, da, sems):
        copy.wait()

    @pl.loop(0, 4)
    def _(i):
        rows = pl.ds(pl.multiple_of(i * 256, 256), 256)
        dob[rows] = mm(da[rows], w_out[...], NT).astype(bf16)

    root = HEAD_SIZE**-0.5
    below = lax.broadcasted_iota(jnp.int32, (256, 256), 0) >= lax.broadcasted_iota(
        jnp.int32, (256, 256), 1
    )
    dkv[...] = jnp.zeros(dkv.shape, f32)
    total = jnp.zeros((1, HEAD_SIZE), f32)
    for i in range(4):
        keys = 256 * (i + 1)
        rows = slice(256 * i, keys)
        co, si = cosine[rows], sine[rows]
        for h in range(4):
            cols = slice(128 * h, 128 * h + 128)
            q, do = q_b[h, rows], dob[rows, cols]
            p = jnp.exp(mm(q, k_b[:keys], NT) * root - lse[rows, h : h + 1])
            tail = jnp.where(below, p[:, keys - 256 :], 0.0)
            p = tail if i == 0 else jnp.concatenate([p[:, : keys - 256], tail], axis=1)
            dp = mm(do, v_b[:keys], NT)
            mean = jnp.sum(do.astype(f32) * a_b[rows, cols].astype(f32), axis=1, keepdims=True)
            ds = (p * (dp - mean)).astype(bf16)
            dkv[:keys, :128] += mm(ds, q, TN) * root
            dkv[:keys, 128:] += mm(p.astype(bf16), do, TN)
            dq = (mm(ds, k_b[:keys]) * root).astype(bf16).astype(f32)
            dq_in = dq * co + pltpu.roll(dq * si, 64, 1)
            raw = q_raw[rows, cols]
            scale = lax.rsqrt(jnp.mean(raw * raw, axis=-1, keepdims=True) + epsilon)
            hat = raw * scale
            total = total + jnp.sum(dq_in * hat, axis=0, keepdims=True)
            t = dq_in * q_gain[...]
            back = scale * (t - hat * jnp.mean(t * hat, axis=-1, keepdims=True))
            dq_raw[rows, cols] = back.astype(bf16)
    gain[...] = total


def attention_backward(pieces, place, w_out, a_b, q_b, k_b, v_b, lse, q_raw, q_gain, cosine, sine):
    spec = [(dz, dc, first, a.shape[0]) for a, dz, dc, first in pieces]
    shapes = [((1024, MODEL_WIDTH), bf16), ((1024, 512), bf16), ((1024, 256), f32), ((1, HEAD_SIZE), f32)]
    return pl.pallas_call(
        functools.partial(attention_back_kernel, spec),
        out_shape=[jax.ShapeDtypeStruct(*s) for s in shapes],
        in_specs=[SM] + [VM] * 10 + [ANY] * len(spec),
        out_specs=[VM] * 4,
        scratch_shapes=[pltpu.VMEM((1024, 512), bf16), pltpu.SemaphoreType.DMA((len(spec),))],
        compiler_params=pltpu.CompilerParams(vmem_limit_bytes=56 * MIB),
        cost_estimate=pl.CostEstimate(flops=12 << 30, bytes_accessed=20 << 20, transcendentals=3 << 20),
        name="attention_backward",
    )(place, w_out, a_b, q_b, k_b, v_b, lse, q_raw, q_gain, cosine, sine, *[p[0] for p in pieces])


def grads_kernel(place, idx, dq_raw, own, other, k_raw, k_gain, cosine, sine, h1, low, high, dqkv, gain):
    c = place[1]
    dqkv[:, :512] = dq_raw[...]
    total = jnp.zeros((1, HEAD_SIZE), f32)
    for i in range(4):
        rows = slice(256 * i, 256 * i + 256)
        both = (own[rows] + other[rows]).astype(bf16)
        dk = both[:, :128].astype(f32)
        dk_in = dk * cosine[rows] + pltpu.roll(dk * sine[rows], 64, 1)
        raw = k_raw[rows]
        scale = lax.rsqrt(jnp.mean(raw * raw, axis=-1, keepdims=True) + epsilon)
        hat = raw * scale
        total = total + jnp.sum(dk_in * hat, axis=0, keepdims=True)
        t = dk_in * k_gain[...]
        back = scale * (t - hat * jnp.mean(t * hat, axis=-1, keepdims=True))
        dqkv[rows, 512:] = jnp.where(c == 0, back, both[:, 128:].astype(f32)).astype(bf16)
    gain[...] = total
    for f in range(8):
        out = low if f < 4 else high
        part = mm(h1[:, 256 * f : 256 * f + 256], dqkv[...], TN).astype(bf16)
        for r in range(16):
            dy, dx = idx[r] // 4, lax.rem(idx[r], 4)
            at = (dy, dx) if f < 4 else (dx, dy)
            out[at[0], at[1], f % 4] = part[16 * r : 16 * r + 16]


def projection_grads(place, back, dq_raw, own, other, k_raw, k_gain, cosine, sine, h1):
    half = ((4, 4, 4, 16, 640), bf16)
    shapes = [half, half, ((1024, 640), bf16), ((1, HEAD_SIZE), f32)]
    return pl.pallas_call(
        grads_kernel,
        out_shape=[jax.ShapeDtypeStruct(*s) for s in shapes],
        in_specs=[SM, SM] + [VM] * 8,
        out_specs=[VM] * 4,
        compiler_params=pltpu.CompilerParams(vmem_limit_bytes=48 * MIB),
        cost_estimate=pl.CostEstimate(flops=3 << 30, bytes_accessed=12 << 20, transcendentals=0),
        name="projection_grads",
    )(place, back, dq_raw, own, other, k_raw, k_gain, cosine, sine, h1)


def input_grad_kernel(place, dqkv, w_own, keep, send):
    z, c = place[0], place[1]

    @pl.loop(0, 4)
    def _(i):
        rows = pl.ds(pl.multiple_of(i * 256, 256), 256)
        part = mm(dqkv[rows], w_own[...], NT).astype(bf16)
        dz = lax.rem(i - z + 4, 4)
        first, second = part[:128], part[128:]
        keep[dz] = jnp.where(c == 0, first, second)
        send[dz] = jnp.where(c == 0, second, first)


def input_grad(place, dqkv, w_own):
    return pl.pallas_call(
        input_grad_kernel,
        out_shape=[jax.ShapeDtypeStruct((4, 128, MODEL_WIDTH), bf16)] * 2,
        in_specs=[SM, VM, VM],
        out_specs=[VM] * 2,
        compiler_params=pltpu.CompilerParams(vmem_limit_bytes=40 * MIB),
        cost_estimate=pl.CostEstimate(flops=3 << 30, bytes_accessed=8 << 20, transcendentals=0),
        name="input_grad",
    )(place, dqkv, w_own)


def place_kernel(idx, *refs):
    left, right, (query, key, value) = refs[:5], refs[5:10], refs[10:]
    for r in range(16):
        dy, dx = divmod(r, 4)
        rows = pl.ds(pl.multiple_of(idx[r] * 16, 16), 16)
        a, ai = part_of(dy, dx)
        b, bi = part_of(dx, dy)
        for f in range(8):
            block = (left[a][ai, f] if f < 4 else right[b][bi, f - 4]).astype(f32)
            query[rows, 512 * f : 512 * f + 512] = block[:, :512]
            out = key if f % 2 == 0 else value
            out[rows, 128 * (f // 2) : 128 * (f // 2) + 128] = block[:, 512:]


def place_rows(idx, left, right):
    return pl.pallas_call(
        place_kernel,
        out_shape=[jax.ShapeDtypeStruct((256, n), f32) for n in (4096, 512, 512)],
        in_specs=[SM] + [VM] * 10,
        out_specs=[VM] * 3,
        compiler_params=pltpu.CompilerParams(vmem_limit_bytes=32 * MIB),
        cost_estimate=pl.CostEstimate(flops=0, bytes_accessed=8 << 20, transcendentals=0),
        name="place_rows",
    )(idx, *left, *right)


def place_out_kernel(idx, *refs):
    left, right, out = refs[:5], refs[5:10], refs[10]
    width = MODEL_WIDTH // 2
    for r in range(16):
        dy, dx = divmod(r, 4)
        rows = pl.ds(pl.multiple_of(idx[r] * 32, 32), 32)
        a, ai = part_of(dy, dx)
        b, bi = part_of(dx, dy)
        out[rows, :width] = left[a][ai].astype(f32)
        out[rows, width:] = right[b][bi].astype(f32)


def place_out(idx, left, right):
    return pl.pallas_call(
        place_out_kernel,
        out_shape=jax.ShapeDtypeStruct((512, MODEL_WIDTH), f32),
        in_specs=[SM] + [VM] * 10,
        out_specs=VM,
        compiler_params=pltpu.CompilerParams(vmem_limit_bytes=32 * MIB),
        cost_estimate=pl.CostEstimate(flops=0, bytes_accessed=6 << 20, transcendentals=0),
        name="place_out",
    )(idx, *left, *right)


def out_grads_kernel(idx, a_b, da, low, high):
    width = MODEL_WIDTH // 2
    for f in range(2):
        part = mm(a_b[:, 256 * f : 256 * f + 256], da[...], TN).astype(bf16)
        for r in range(8):
            dy, dx = idx[8 * f + r] // 4, lax.rem(idx[8 * f + r], 4)
            block = part[32 * r : 32 * r + 32]
            low[dy, dx] = block[:, :width]
            high[dx, dy] = block[:, width:]


def out_grads(back, a_b, da):
    return pl.pallas_call(
        out_grads_kernel,
        out_shape=[jax.ShapeDtypeStruct((4, 4, 32, MODEL_WIDTH // 2), bf16)] * 2,
        in_specs=[SM, VM, VM],
        out_specs=[VM] * 2,
        compiler_params=pltpu.CompilerParams(vmem_limit_bytes=40 * MIB),
        cost_estimate=pl.CostEstimate(flops=2 << 30, bytes_accessed=8 << 20, transcendentals=0),
        name="out_grads",
    )(back, a_b, da)


def tied(*values):
    return lax.optimization_barrier(values)


def local(
    layer_input, routes, cotangent, attn_gain, query_gain, key_gain, mlp_gain,
    w_query, key_weight, value_weight, w_out, w_router, w_gate, w_up, w_down,
):
    core = lax.axis_index(C)
    place = lax.axis_index(EXPERT)
    py, px = lax.axis_index(Y), lax.axis_index(X)
    zc = jnp.stack([lax.axis_index(Z), core]).astype(jnp.int32)
    ahead = jnp.arange(16, dtype=jnp.int32)
    idx = (py + ahead // 4) % 4 * 4 + (px + ahead % 4) % 4
    back = (ahead // 4 - py) % 4 * 4 + (ahead % 4 - px) % 4
    residual = layer_input[0].astype(f32)
    dy_low = cotangent[0]
    upstream = dy_low.astype(f32)
    scale_one = inv_rms(residual)
    normed_one = residual * scale_one
    h1 = (normed_one * attn_gain).astype(bf16)
    h1_pieces = gather_fsdp(h1)
    rows = w_query.shape[0]
    key_value = jnp.stack([key_weight.reshape(rows, 4, 128), value_weight.reshape(rows, 4, 128)], axis=2)
    blocks = jnp.concatenate(
        [w_query.reshape(rows, 8, 512), key_value.reshape(rows, 8, 128)], axis=2
    ).transpose(1, 0, 2)
    w_own = lax.all_to_all(blocks, FSDP, 0, 0, tiled=True).reshape(8 * rows, 640)
    w_other = shift(w_own[:, 512:], C, 1)
    seq = 1024
    cosine, sine = rope_tables(jnp.arange(seq).astype(f32))
    sign = jnp.where(jnp.arange(HEAD_SIZE) < HEAD_SIZE // 2, -1.0, 1.0).astype(f32)
    signed = sine * sign
    h1_all, q_raw, k_raw, v_b, q_b, k_b, a_b, lse, keep, send = attention_forward(
        h1_pieces, zc, w_own, w_other, w_out, query_gain[None], key_gain[None], cosine, signed
    )
    beside = jnp.pad(routes[0], ((0, 0), (0, 120))).astype(bf16)
    dy_all = lax.all_gather(jnp.concatenate([dy_low, beside], axis=1), EXPERT, axis=0, tiled=False)
    router_own = jnp.pad(w_router, ((0, 0), (0, 96)))
    gate_all = lax.all_gather(
        jnp.concatenate([w_gate, jnp.stack([router_own, router_own])], axis=2), FSDP, axis=1, tiled=True
    )
    up_all = lax.all_gather(w_up, FSDP, axis=1, tiled=True)
    down_all = lax.all_gather(w_down, FSDP, axis=1, tiled=True)
    router = gate_all[0, :, 768 : 768 + EXPERTS]
    routes_all = dy_all[:, :, MODEL_WIDTH : MODEL_WIDTH + TOPK].astype(jnp.int32)
    routes_rel = routes_all[idx]
    own_ids = 2 * place + jnp.arange(2, dtype=jnp.int32)
    member = jnp.any(routes_rel[:, None, :, :] == own_ids[None, :, None, None], axis=-1)
    rank = jnp.cumsum(member.astype(jnp.int32), axis=2) - 1
    slot = jnp.where(member, rank, -1)
    by_pair = slot.reshape(8, 2, 2, 128)
    shifted = jnp.where(by_pair >= 0, by_pair + CAP * jnp.arange(2, dtype=jnp.int32)[:, None, None], -1)
    target = shifted.transpose(0, 2, 1, 3).reshape(8, 2, 256)
    target_t = jnp.where(
        target >= 0, target + 2 * CAP * jnp.arange(2, dtype=jnp.int32)[:, None], -1
    ).transpose(0, 2, 1)
    pick = slot[:, :, None, :] == jnp.arange(CAP)[None, None, :, None]
    dys = slot_rows([dy_all], idx, target)
    attn = scatter_fsdp(keep, send)
    attn, dys, target_t = tied(attn, dys, target_t)
    resid_two = residual + attn
    scale_two = inv_rms(resid_two)
    normed_two = resid_two * scale_two
    h2 = (normed_two * mlp_gain).astype(bf16)
    half = MODEL_WIDTH // 2
    left, right = gather_plane(h2[:, :half], h2[:, half:])
    ids = jnp.arange(EXPERTS, dtype=jnp.int32)
    logits = dot(h2, router)
    chosen = jnp.any(routes[0][:, :, None] == ids, axis=1)
    logits = jnp.where(chosen, logits, -1e30)
    powers = jnp.where(chosen, jnp.exp(logits - jnp.max(logits, axis=-1, keepdims=True)), 0.0)
    gates_own = powers / jnp.sum(powers, axis=-1, keepdims=True)
    gates_part = gates_own.reshape(128, 16, 2).transpose(1, 2, 0)
    gates_all = lax.all_to_all(gates_part, EXPERT, 0, 0, tiled=True)[idx]
    slot_gate = jnp.sum(jnp.where(pick, gates_all[:, :, None, :], 0.0), axis=-1)
    slot_gate = slot_gate.transpose(1, 0, 2).reshape(2, 640, 1)
    slot_gate = jnp.broadcast_to(slot_gate, (2, 640, 128))
    xs = slot_rows([*left, *right], idx, target)
    dhr, hidden, dgate_slot, dg, du = expert_rows(xs, dys, slot_gate, gate_all, up_all, down_all)
    dh_left, dh_right = scatter_plane(*combine(target_t, dhr))
    dh_sum = jnp.concatenate([dh_left, dh_right], axis=1)
    dgate_slot = dgate_slot[:, :, 0].reshape(2, 16, CAP).transpose(1, 0, 2)
    dgate_part = jnp.sum(jnp.where(pick, dgate_slot[..., None], 0.0), axis=2)[back]
    dgate_all = lax.all_to_all(dgate_part, EXPERT, 0, 0, tiled=True)
    dgate = dgate_all.transpose(2, 0, 1).reshape(128, EXPERTS)
    grad_gate = es("erd,erf->edf", xs, dg).astype(bf16)
    grad_up = es("erd,erf->edf", xs, du).astype(bf16)
    grad_down = es("erf,erd->efd", hidden, dys).astype(bf16)
    ys = es("erf,efd->erd", hidden, down_all).astype(bf16)
    y_left, y_right = combine(target_t, ys)
    dh_sum, grad_gate, grad_up, grad_down, y_left, y_right = tied(
        dh_sum, grad_gate, grad_up, grad_down, y_left, y_right
    )
    expert_grads = [
        lax.psum_scatter(v, FSDP, scatter_dimension=1, tiled=True).astype(f32)
        for v in (grad_gate, grad_up, grad_down)
    ]
    dl = (gates_own * (dgate - jnp.sum(gates_own * dgate, axis=-1, keepdims=True))).astype(bf16)
    dh2 = es("te,de->td", dl, router) + dh_sum
    dx2 = upstream + norm_back(dh2 * mlp_gain, normed_two, scale_two)
    da = dx2.astype(bf16)
    da_pieces = gather_fsdp(da)
    grad_mlp_gain = jnp.sum(dh2 * normed_two, axis=0)
    grad_router = es("te,td->ed", dl, h2)
    early = sum_all(jnp.concatenate([grad_router, grad_mlp_gain[None]], axis=0))
    y_left, y_right = scatter_plane(y_left, y_right)
    output = (resid_two + jnp.concatenate([y_left, y_right], axis=1)).astype(bf16)
    da_all, dq_raw, dkv, q_gain_part = attention_backward(
        da_pieces, zc, w_out, a_b, q_b, k_b, v_b, lse, q_raw, query_gain[None], cosine, signed
    )
    low, high, dqkv, k_gain_part = projection_grads(
        zc, back, dq_raw, dkv, shift(dkv, C, 1), k_raw, key_gain[None], cosine, signed, h1_all
    )

    def halves(v):
        return v[0], v[1], v[2, :2], v[2, 2:], v[3]

    low, high = scatter_plane(halves(low), halves(high))
    keep, send = input_grad(zc, dqkv, w_own)
    dh1 = scatter_fsdp(keep, send)
    grad_input = dx2 + norm_back(dh1 * attn_gain, normed_one, scale_one)
    out_low, out_high = out_grads(back, a_b, da_all)
    out_low, out_high = scatter_plane(halves(out_low), halves(out_high))
    grad_out = place_out(idx, *gather_plane(out_low.astype(bf16), out_high.astype(bf16)))
    parted = jnp.concatenate([low, high]).astype(bf16)
    parted = lax.all_to_all(parted, FSDP, 0, 0, tiled=True)
    grad_query, grad_key, grad_value = place_rows(idx, *gather_plane(parted[:4], parted[4:]))
    grad_attn_gain = jnp.sum(dh1 * normed_one, axis=0)
    late = sum_all(jnp.concatenate([grad_attn_gain, q_gain_part[0], k_gain_part[0] * 0.5]).reshape(18, 128))
    late = late.reshape(-1)
    grad_router = lax.dynamic_slice_in_dim(early[:EXPERTS], 256 * lax.axis_index(FSDP), 256, 1).T
    return (
        output[None],
        grad_input.astype(bf16)[None],
        late[:MODEL_WIDTH],
        late[MODEL_WIDTH : MODEL_WIDTH + HEAD_SIZE],
        late[MODEL_WIDTH + HEAD_SIZE :],
        early[EXPERTS],
        grad_query,
        grad_key,
        grad_value,
        grad_out,
        grad_router,
        *expert_grads,
    )


def solution(mesh):
    torus = Mesh(mesh.devices.reshape(4, 2, 4, 4), ALL)
    tokens, rows, experts = P(EXPERT, FSDP, None), P(FSDP, None), P(EXPERT, FSDP, None)
    return jax.shard_map(
        local,
        mesh=torus,
        in_specs=(tokens,) * 3 + (P(),) * 4 + (rows,) * 5 + (experts,) * 3,
        out_specs=(tokens,) * 2 + (P(),) * 4 + (rows,) * 5 + (experts,) * 3,
        check_vma=False,
    )
```

time: 1180 us -> 791 us (0.67)
  blocking collectives: 211 us -> 0 us
  starting transfers between devices: 23.7 us -> 219 us
  waiting for transfers between devices: 464 us -> 278 us
  matrix products: 217 us -> 35.3 us
  Pallas kernels: 0 us -> 120 us
  local copies, waits for them, and re-layouts: 151 us -> 50.2 us
  other arithmetic: 83.7 us -> 64.7 us
    ppermute x0 -> x162, waiting for transfers between devices: none -> 260 us  [shift(): return lax.ppermute(v, axis, [(i, (i + by) % n) for i in range(n)])]
    all_gather x6 -> x4, waiting for transfers between devices: 226 us -> 0.03 us  [the longest x1 0.02 us: local(): lax.all_gather(jnp.concatenate([dy_low, beside], axis=1), EXPERT, axis=0,...]
    ppermute x0 -> x162, starting transfers between devices: none -> 203 us  [shift(): return lax.ppermute(v, axis, [(i, (i + by) % n) for i in range(n)])]
    dot_general x52 -> x7, matrix products: 217 us -> 35.3 us  [the longest x6 33.8 us: es(): return jnp.einsum(spec, a, b, preferred_element_type=f32)]
    all_to_all x3 -> x4, waiting for transfers between devices: 163 us -> 17.1 us  [the longest x1 7.45 us: local(): gates_all = lax.all_to_all(gates_part, EXPERT, 0, 0, tiled=True)[idx]]
    psum x5 -> x0, blocking collectives: 129 us -> none  [the longest x1 75.1 us: local(): lax.psum(local_shares[4].astype(jnp.bfloat16), EXPERT).astype(jnp.float32)]
    pallas_call x0 -> x12, Pallas kernels: none -> 120 us  [the longest x1 36.5 us: expert_rows(): pl.pallas_call(expert_kernel, grid=(2,), out_shape=[jax.ShapeDtypeStruct(...]
    all_to_all x1 -> x0, blocking collectives: 69.5 us -> none  [local(): lax.all_to_all(send_rows, EXPERT, split_axis=0, concat_axis=0, tiled=True)]
  transfers between devices with their start and end apart: 13 -> 173, of which waited for: 9 -> 66; matrix products, arithmetic and copies ran while one was open for 24% -> 13% of each run, Pallas kernels for 0% -> 10%
where the time goes in v1:
time: 791 us; the launch traced here: 785 us
  waiting for transfers between devices  278 us (35%)
  starting transfers between devices  219 us (28%)
  Pallas kernels  120 us (15%)
  other arithmetic  64.7 us (8%)
  local copies, waits for them, and re-layouts  50.2 us (6%)
  matrix products  35.3 us (4%)
  between operations  16.8 us (2%)
    ppermute x162, waiting for transfers between devices, shift(): return lax.ppermute(v, axis, [(i, (i + by) % n) for i in range(n)])  260 us
    ppermute x162, starting transfers between devices, shift(): return lax.ppermute(v, axis, [(i, (i + by) % n) for i in range(n)])  203 us
    pallas_call x1, Pallas kernels, expert_rows(): pl.pallas_call(expert_kernel, grid=(2,), out_shape=[jax.ShapeDtypeStruct(...  36.5 us
    dot_general x6, matrix products, es(): return jnp.einsum(spec, a, b, preferred_element_type=f32)  33.8 us
    unnamed x192, local copies, waits for them, and re-layouts  28.8 us
    pallas_call x1, Pallas kernels, attention_backward(): pl.pallas_call(functools.partial(attention_back_kernel, spec), out_shape=...  20.8 us
    pallas_call x1, Pallas kernels, attention_forward(): pl.pallas_call(functools.partial(attention_kernel, spec), out_shape=[jax....  19.3 us
  transfers between devices with their start and end apart: 173, of which 66 were waited for; matrix products, arithmetic and copies ran while one was open for 13% of the time, Pallas kernels for 10%

profile of v1, /device:TPU:0, one launch (start us, length us, event | category | flops | bytes accessed | tf_op | source)
XLA Modules:
  0.0 784.7 jit_solution(3512286200155107409)
XLA Ops:
  15.5 5.5 all-to-all-start
  25.6 39.4 %collective-permute-done.3.rest_3_ = bf16[128,2048]{1,0:T(8,128)(2,1)} collective-permute-done((bf16[128,2048]{1,0:T(8,128)(2,1)}, bf16[128,2048]{1,0:T(8,128)(2,1)}, u32[]{:S(2)}, u32[]{:S(2)}) %collective-permute-start.3) | collective-permute-done | bytes 524320 | tf_op jit(solution)/shard_map/ppermute | solution.py:39
  81.2 19.3 %attention_forward.1 = (bf16[1024,2048]{1,0:T(8,128)(2,1)}, f32[1024,512]{1,0:T(8,128)}, f32[1024,128]{1,0:T(8,128)}, bf16[1024,128]{1,0:T(8,128)(2,1)}, bf16[4,...) custom-call(s32[2]{0:T(128)} %pad_add_fusion.place, ...), custom_call_target="tpu_custom_call" | custom-call | flops 9663676416 | bytes 29360128 | tf_op jit(solution)/shard_map/attention_forward/pallas_call | solution.py:238
  111.8 10.4 %collective-permute-done.13 = bf16[64,2048]{1,0:T(8,128)(2,1)S(1)} collective-permute-done((bf16[64,2048]{1,0:T(8,128)(2,1)S(1)}, bf16[64,2048]{1,0:T(8,128)(2,1)S(1)}, u32[]{:S(2)}, u32[]{:S(2)}) %collective-permute-start.13) | collective-permute-done | bytes 262176 | tf_op jit(solution)/shard_map/ppermute | solution.py:39
  126.9 20.5 %collective-permute-done.14 = bf16[128,2048]{1,0:T(8,128)(2,1)S(1)} collective-permute-done((bf16[128,2048]{1,0:T(8,128)(2,1)S(1)}, bf16[128,2048]{1,0:T(8,128)(2,1)S(1)}, u32[]{:S(2)}, u32[]{:S(2)}) %collective-permute-start.14) | collective-permute-done | bytes 524320 | tf_op jit(solution)/shard_map/ppermute | solution.py:39
  159.0 4.5 copy-done
  196.8 17.3 %collective-permute-done.20.rest_4_ = bf16[4,128,1024]{2,1,0:T(8,128)(2,1)S(1)} collective-permute-done((bf16[4,128,1024]{2,1,0:T(8,128)(2,1)S(1)}, bf16[4,128,1024]{2,1,0:T(8,128)(2,1)S(1)}, u32[]{:S(2)}, u32[]{:S(2)}) %collective-permute-start.20) | collective-permute-done | bytes 1048608 | tf_op jit(solution)/shard_map/ppermute | solution.py:39
  230.2 7.5 all-to-all-done.1
  242.3 4.5 slot_rows.3.xs
  250.2 36.5 %expert_rows.1 = (bf16[2,640,2048]{2,1,0:T(8,128)(2,1)}, bf16[2,640,768]{2,1,0:T(8,128)(2,1)}, f32[2,640,128]{2,1,0:T(8,128)}, bf16[2,640,768]{2,1,0:T(8,128)(2,1)}, bf16[2,640,768]{2,1,0:T(8,128)(2,1)}) custom-call(bf16[2,640,2048]{2,1,0:T(8,128)(2,1)} %copy-done.2, bf16[2,640,2048]{2,1,0:T(8,128)(2,1)} %copy-done.1, ...), custom_call_target="tpu_custom_call" | custom-call | flops 21474836480 | bytes 46137344 | tf_op jit(solution)/shard_map/expert_rows/pallas_call | solution.py:326
  286.7 10.1 %convolution_convert_fusion = bf16[2,768,2048]{2,1,0:T(8,128)(2,1)} fusion(bf16[2,640,768]{2,1,0:T(8,128)(2,1)} %get-tuple-element.99, bf16[2,640,2048]{2,1,0:T(8,128)(2,1)} %copy-done.1), kind=kOutput, calls=%fused_computation.3 | convolution fusion | flops 4029677568 | bytes 13500416 | tf_op jit(solution)/shard_map/erf,erd->efd/dot_general | solution.py:34
  296.8 5.9 combine.2
  311.1 7.5 convolution_convert_fusion.3.rows
  318.7 7.3 convolution_convert_fusion.2
  340.5 7.2 convolution_convert_fusion.1
  372.5 5.7 combine.3
  394.1 5.6 all-to-all-done.2
  409.7 7.5 collective-permute-done.49
  429.3 7.1 collective-permute-done.50
  463.7 13.3 %collective-permute-done.65.rest_3_ = bf16[128,2048]{1,0:T(8,128)(2,1)S(1)} collective-permute-done((bf16[128,2048]{1,0:T(8,128)(2,1)S(1)}, bf16[128,2048]{1,0:T(8,128)(2,1)S(1)}, u32[]{:S(2)}, u32[]{:S(2)}) %collective-permute-start.65) | collective-permute-done | bytes 524320 | tf_op jit(solution)/shard_map/ppermute | solution.py:39
  487.4 20.8 %attention_backward.1 = (bf16[1024,2048]{1,0:T(8,128)(2,1)}, bf16[1024,512]{1,0:T(8,128)(2,1)}, f32[1024,256]{1,0:T(8,128)}, f32[1,128]{1,0:T(1,128)}) custom-call(s32[2]{0:T(128)} %pad_add_fusion.place, bf16[512,2048]{1,0:T(8,128)(2,1)} %w_out.3, bf16[1024,512]{1,0:T(8,128)(2,1)} %get-tuple-element.122.a_b, bf16[4,1024,128]{2,1,0:T(8,128)(2,1)} %get-tuple-element.123.q_b, ...), custom_call_target="tpu_custom_call" | custom-call | flops 12884901888 | bytes 20971520 | tf_op jit(solution)/shard_map/attention_backward/pallas_call | solution.py:421
  574.3 8.4 %projection_grads.1 = (bf16[4,4,4,16,640]{4,3,2,1,0:T(8,128)(2,1)S(1)}, bf16[4,4,4,16,640]{4,3,2,1,0:T(8,128)(2,1)}, bf16[1024,640]{1,0:T(8,128)(2,1)}, f32[1,128]{1,0:T(1,128)S(1)}) custom-call(s32[2]{0:T(128)S(1)} %copy-done.37, s32[16]{0:T(128)S(1)} %fusion.79.idx, bf16[1024,512]{1,0:T(8,128)(2,1)S(1)} %copy-done.41, f32[1024,256]{1,0:T(8,128)S(1)} %copy-done.30, ...), custom_call_target="tpu_custom_call" | custom-call | flops 3221225472 | bytes 12582912 | tf_op jit(solution)/shard_map/projection_grads/pallas_call | solution.py:462
  589.6 5.9 input_grad.1
  601.7 7.4 collective-permute-done.101
  612.1 6.3 collective-permute-done.109
  654.0 4.3 collective-permute-done.92
  658.2 4.9 collective-permute-done.143.refs_4_
  679.7 6.6 collective-permute-done.74
  695.1 8.4 %collective-permute-done.117 = bf16[2,16,640]{2,1,0:T(8,128)(2,1)S(1)} collective-permute-done((bf16[2,16,640]{2,1,0:T(8,128)(2,1)S(1)}, bf16[2,16,640]{2,1,0:T(8,128)(2,1)S(1)}, u32[]{:S(2)}, u32[]{:S(2)}) %collective-permute-start.117) | collective-permute-done | bytes 40992 | tf_op jit(solution)/shard_map/ppermute | solution.py:39
  703.4 4.5 collective-permute-start.95
  708.2 7.3 collective-permute-done.96
  727.7 7.5 collective-permute-done.126.refs_6_
  (765 shorter events, 433.1 us)
Async XLA Ops:
  7.2 142.7 %all-gather.12.cloned.1.call-start = ((), (), s32[]{:S(2)}) async-start(), calls=%async_computation.13 | async-start | bytes 9469952 | tf_op jit(solution)/shard_map/all_gather | solution.py:608
  10.0 214.4 %all-gather.6.cloned.1.call-start = ((), (), s32[]{:S(2)}) async-start(), calls=%async_computation.7 | async-start | bytes 8257536 | tf_op jit(solution)/shard_map/all_gather | solution.py:610
  12.0 237.1 %all-gather.8.cloned.1.call-start = ((), (), s32[]{:S(2)}) async-start(), calls=%async_computation.8 | async-start | bytes 7077888 | tf_op jit(solution)/shard_map/all_gather | solution.py:613
  15.5 55.9 %all-to-all-start = ((bf16[8,256,640]{2,1,0:T(8,128)(2,1)}), bf16[8,256,640]{2,1,0:T(8,128)(2,1)S(1)}, u32[]{:S(2)}, u32[]{:S(2)}) async-start(bf16[8,256,640]{2,1,0:T(8,128)(2,1)} %maximum_bitcast_fusion), calls=%async_computation | async-start | bytes 5242880 | tf_op jit(solution)/shard_map/all_to_all | solution.py:598
  21.1 228.0 %all-gather.10.cloned.1.call-start = ((), (), s32[]{:S(2)}) async-start(), calls=%async_computation.9 | async-start | bytes 7077888 | tf_op jit(solution)/shard_map/all_gather | solution.py:614
  22.3 42.6 %collective-permute-start.3 = (bf16[128,2048]{1,0:T(8,128)(2,1)}, bf16[128,2048]{1,0:T(8,128)(2,1)}, u32[]{:S(2)}, u32[]{:S(2)}) collective-permute-start(bf16[128,2048]{1,0:T(8,128)(2,1)} %fusion.5.rest_0_), channel_id=1, source_target_pairs={{0,32},{32,64},{64,96},{96,0},{1,33},{33,65},{65,97},{97,1},{2,34}... | collective-permute-start | bytes 1572872 | tf_op jit(solution)/shard_map/ppermute | solution.py:39
  24.3 41.7 %collective-permute-start.2 = (bf16[128,2048]{1,0:T(8,128)(2,1)}, bf16[128,2048]{1,0:T(8,128)(2,1)}, u32[]{:S(2)}, u32[]{:S(2)}) collective-permute-start(bf16[128,2048]{1,0:T(8,128)(2,1)} %fusion.5.rest_0_), channel_id=1, source_target_pairs={{0,96},{32,0},{64,32},{96,64},{1,97},{33,1},{65,33},{97,65},{2,98}... | collective-permute-start | bytes 1572872 | tf_op jit(solution)/shard_map/ppermute | solution.py:39
  25.5 46.8 %collective-permute-start.1 = (bf16[128,2048]{1,0:T(8,128)(2,1)}, bf16[128,2048]{1,0:T(8,128)(2,1)}, u32[]{:S(2)}, u32[]{:S(2)}) collective-permute-start(bf16[128,2048]{1,0:T(8,128)(2,1)} %fusion.5.rest_0_), channel_id=1, source_target_pairs={{0,16},{16,0},{1,17},{17,1},{2,18},{18,2},{3,19},{19,3},{4,20},{20... | collective-permute-start | bytes 1572872 | tf_op jit(solution)/shard_map/ppermute | solution.py:39
  122.4 25.1 %collective-permute-start.14 = (bf16[128,2048]{1,0:T(8,128)(2,1)S(1)}, bf16[128,2048]{1,0:T(8,128)(2,1)S(1)}, u32[]{:S(2)}, u32[]{:S(2)}) collective-permute-start(bf16[128,2048]{1,0:T(8,128)(2,1)S(1)} %pad_maximum_fusion.13), channel_id=1, source_target_pairs={{0,96},{32,0},{64,32},{96,64},{1,97},{33,1},{65,33},{97,65},{2,98}... | collective-permute-start | bytes 1572872 | tf_op jit(solution)/shard_map/ppermute | solution.py:39
  189.0 25.1 %collective-permute-start.20 = (bf16[4,128,1024]{2,1,0:T(8,128)(2,1)S(1)}, bf16[4,128,1024]{2,1,0:T(8,128)(2,1)S(1)}, u32[]{:S(2)}, u32[]{:S(2)}) collective-permute-start(bf16[4,128,1024]{2,1,0:T(8,128)(2,1)S(1)} %pad_maximum_fusion.rest_0_), channel_id=1, source_target_pairs={{0,4},{4,8},{8,12},{12,0},{1,5},{5,9},{9,13},{13,1},{2,6},{6,10},{... | collective-permute-start | bytes 3145736 | tf_op jit(solution)/shard_map/ppermute | solution.py:39
  190.6 24.4 %collective-permute-start.19 = (bf16[4,128,1024]{2,1,0:T(8,128)(2,1)S(1)}, bf16[4,128,1024]{2,1,0:T(8,128)(2,1)S(1)}, u32[]{:S(2)}, u32[]{:S(2)}) collective-permute-start(bf16[4,128,1024]{2,1,0:T(8,128)(2,1)S(1)} %pad_maximum_fusion.rest_0_), channel_id=1, source_target_pairs={{0,12},{4,0},{8,4},{12,8},{1,13},{5,1},{9,5},{13,9},{2,14},{6,2},{... | collective-permute-start | bytes 3145736 | tf_op jit(solution)/shard_map/ppermute | solution.py:39
  193.3 25.8 %collective-permute-start.28 = (bf16[4,128,1024]{2,1,0:T(8,128)(2,1)S(1)}, bf16[4,128,1024]{2,1,0:T(8,128)(2,1)S(1)}, u32[]{:S(2)}, u32[]{:S(2)}) collective-permute-start(bf16[4,128,1024]{2,1,0:T(8,128)(2,1)S(1)} %pad_maximum_fusion.1.rest_5_), channel_id=1, source_target_pairs={{0,1},{1,2},{2,3},{3,0},{4,5},{5,6},{6,7},{7,4},{8,9},{9,10},{10,1... | collective-permute-start | bytes 3145736 | tf_op jit(solution)/shard_map/ppermute | solution.py:39
  193.5 26.5 %collective-permute-start.27 = (bf16[4,128,1024]{2,1,0:T(8,128)(2,1)S(1)}, bf16[4,128,1024]{2,1,0:T(8,128)(2,1)S(1)}, u32[]{:S(2)}, u32[]{:S(2)}) collective-permute-start(bf16[4,128,1024]{2,1,0:T(8,128)(2,1)S(1)} %pad_maximum_fusion.1.rest_5_), channel_id=1, source_target_pairs={{0,3},{1,0},{2,1},{3,2},{4,7},{5,4},{6,5},{7,6},{8,11},{9,8},{10,9... | collective-permute-start | bytes 3145736 | tf_op jit(solution)/shard_map/ppermute | solution.py:39
  214.9 23.7 %collective-permute-start.21 = (bf16[2,128,1024]{2,1,0:T(8,128)(2,1)}, bf16[2,128,1024]{2,1,0:T(8,128)(2,1)}, u32[]{:S(2)}, u32[]{:S(2)}) collective-permute-start(bf16[2,128,1024]{2,1,0:T(8,128)(2,1)} %slice.922), channel_id=1, source_target_pairs={{0,4},{4,8},{8,12},{12,0},{1,5},{5,9},{9,13},{13,1},{2,6},{6,10},{... | collective-permute-start | bytes 1572872 | tf_op jit(solution)/shard_map/ppermute | solution.py:39
  215.9 22.8 %collective-permute-start.22 = (bf16[2,128,1024]{2,1,0:T(8,128)(2,1)}, bf16[2,128,1024]{2,1,0:T(8,128)(2,1)}, u32[]{:S(2)}, u32[]{:S(2)}) collective-permute-start(bf16[2,128,1024]{2,1,0:T(8,128)(2,1)} %slice.923), channel_id=1, source_target_pairs={{0,12},{4,0},{8,4},{12,8},{1,13},{5,1},{9,5},{13,9},{2,14},{6,2},{... | collective-permute-start | bytes 1572872 | tf_op jit(solution)/shard_map/ppermute | solution.py:39
  230.1 540.3 %reduce-scatter.8.cloned.1.call-start = ((), (), s32[]{:S(2)}) async-start(), calls=%async_computation.12 | async-start | bytes 7077888 | tf_op jit(solution)/shard_map/reduce_scatter | solution.py:666
  304.7 31.5 %collective-permute-start.31 = (bf16[2,128,1024]{2,1,0:T(8,128)(2,1)}, bf16[2,128,1024]{2,1,0:T(8,128)(2,1)}, u32[]{:S(2)}, u32[]{:S(2)}) collective-permute-start(bf16[2,128,1024]{2,1,0:T(8,128)(2,1)} %get-tuple-element.89), channel_id=1, source_target_pairs={{0,4},{4,8},{8,12},{12,0},{1,5},{5,9},{9,13},{13,1},{2,6},{6,10},{... | collective-permute-start | bytes 1572872 | tf_op jit(solution)/shard_map/ppermute | solution.py:39
  305.3 29.4 %collective-permute-start.33 = (bf16[2,128,1024]{2,1,0:T(8,128)(2,1)}, bf16[2,128,1024]{2,1,0:T(8,128)(2,1)}, u32[]{:S(2)}, u32[]{:S(2)}) collective-permute-start(bf16[2,128,1024]{2,1,0:T(8,128)(2,1)} %get-tuple-element.91), channel_id=1, source_target_pairs={{0,12},{4,0},{8,4},{12,8},{1,13},{5,1},{9,5},{13,9},{2,14},{6,2},{... | collective-permute-start | bytes 1572872 | tf_op jit(solution)/shard_map/ppermute | solution.py:39
  336.0 23.6 %collective-permute-start.34 = (bf16[4,128,1024]{2,1,0:T(8,128)(2,1)S(1)}, bf16[4,128,1024]{2,1,0:T(8,128)(2,1)}, u32[]{:S(2)}, u32[]{:S(2)}) collective-permute-start(bf16[4,128,1024]{2,1,0:T(8,128)(2,1)S(1)} %pad_maximum_fusion.3), channel_id=1, source_target_pairs={{0,12},{4,0},{8,4},{12,8},{1,13},{5,1},{9,5},{13,9},{2,14},{6,2},{... | collective-permute-start | bytes 3145736 | tf_op jit(solution)/shard_map/ppermute | solution.py:39
  382.2 390.6 %reduce-scatter.6.cloned.1.call-start = ((), (), s32[]{:S(2)}) async-start(), calls=%async_computation.11 | async-start | bytes 7077888 | tf_op jit(solution)/shard_map/reduce_scatter | solution.py:666
  392.1 383.1 %reduce-scatter.4.cloned.1.call-start = ((), (), s32[]{:S(2)}) async-start(), calls=%async_computation.10 | async-start | bytes 7077888 | tf_op jit(solution)/shard_map/reduce_scatter | solution.py:666
  485.4 64.3 %collective-permute-start.88 = (f32[33,2048]{1,0:T(8,128)S(1)}, f32[33,2048]{1,0:T(8,128)S(1)}, u32[]{:S(2)}, u32[]{:S(2)}) collective-permute-start(f32[33,2048]{1,0:T(8,128)S(1)} %pad_maximum_fusion.16), channel_id=1, source_target_pairs={{0,16},{16,0},{1,17},{17,1},{2,18},{18,2},{3,19},{19,3},{4,20},{20... | collective-permute-start | bytes 811016 | tf_op jit(solution)/shard_map/ppermute | solution.py:39
  520.4 53.9 %collective-permute-start.72 = (f32[1024,256]{1,0:T(8,128)S(1)}, f32[1024,256]{1,0:T(8,128)S(1)}, u32[]{:S(2)}, u32[]{:S(2)}) collective-permute-start(f32[1024,256]{1,0:T(8,128)S(1)} %copy-done.30), channel_id=1, source_target_pairs={{0,16},{16,0},{1,17},{17,1},{2,18},{18,2},{3,19},{19,3},{4,20},{20... | collective-permute-start | bytes 3145736 | tf_op jit(solution)/shard_map/ppermute | solution.py:39
  572.2 80.5 %collective-permute-start.94 = (f32[33,2048]{1,0:T(8,128)S(1)}, f32[33,2048]{1,0:T(8,128)}, u32[]{:S(2)}, u32[]{:S(2)}) collective-permute-start(f32[33,2048]{1,0:T(8,128)S(1)} %add_add_fusion.2), channel_id=1, source_target_pairs={{0,12},{4,0},{8,4},{12,8},{1,13},{5,1},{9,5},{13,9},{2,14},{6,2},{... | collective-permute-start | bytes 811016 | tf_op jit(solution)/shard_map/ppermute | solution.py:39
  572.7 81.2 %collective-permute-start.93 = (f32[33,2048]{1,0:T(8,128)S(1)}, f32[33,2048]{1,0:T(8,128)}, u32[]{:S(2)}, u32[]{:S(2)}) collective-permute-start(f32[33,2048]{1,0:T(8,128)S(1)} %add_add_fusion.2), channel_id=1, source_target_pairs={{0,8},{4,12},{8,0},{12,4},{1,9},{5,13},{9,1},{13,5},{2,10},{6,14},... | collective-permute-start | bytes 811016 | tf_op jit(solution)/shard_map/ppermute | solution.py:39
  598.7 71.3 %collective-permute-start.73 = (bf16[4,128,2048]{2,1,0:T(8,128)(2,1)}, bf16[4,128,2048]{2,1,0:T(8,128)(2,1)}, u32[]{:S(2)}, u32[]{:S(2)}) collective-permute-start(bf16[4,128,2048]{2,1,0:T(8,128)(2,1)} %get-tuple-element.134), channel_id=1, source_target_pairs={{0,16},{16,0},{1,17},{17,1},{2,18},{18,2},{3,19},{19,3},{4,20},{20... | collective-permute-start | bytes 6291464 | tf_op jit(solution)/shard_map/ppermute | solution.py:39
  664.6 24.7 %collective-permute-start.114 = (bf16[4,16,640]{2,1,0:T(8,128)(2,1)S(1)}, bf16[4,16,640]{2,1,0:T(8,128)(2,1)S(1)}, u32[]{:S(2)}, u32[]{:S(2)}) collective-permute-start(bf16[4,16,640]{2,1,0:T(8,128)(2,1)S(1)} %get-tuple-element.244), channel_id=1, source_target_pairs={{0,3},{1,0},{2,1},{3,2},{4,7},{5,4},{6,5},{7,6},{8,11},{9,8},{10,9... | collective-permute-start | bytes 245768 | tf_op jit(solution)/shard_map/ppermute | solution.py:39
  666.5 22.9 %collective-permute-start.115 = (bf16[4,16,640]{2,1,0:T(8,128)(2,1)S(1)}, bf16[4,16,640]{2,1,0:T(8,128)(2,1)S(1)}, u32[]{:S(2)}, u32[]{:S(2)}) collective-permute-start(bf16[4,16,640]{2,1,0:T(8,128)(2,1)S(1)} %get-tuple-element.244), channel_id=1, source_target_pairs={{0,1},{1,2},{2,3},{3,0},{4,5},{5,6},{6,7},{7,4},{8,9},{9,10},{10,1... | collective-permute-start | bytes 245768 | tf_op jit(solution)/shard_map/ppermute | solution.py:39
  666.7 26.2 %collective-permute-start.125 = (bf16[2,16,640]{2,1,0:T(8,128)(2,1)S(1)}, bf16[2,16,640]{2,1,0:T(8,128)(2,1)S(1)}, u32[]{:S(2)}, u32[]{:S(2)}) collective-permute-start(bf16[2,16,640]{2,1,0:T(8,128)(2,1)S(1)} %slice.994), channel_id=1, source_target_pairs={{0,12},{4,0},{8,4},{12,8},{1,13},{5,1},{9,5},{13,9},{2,14},{6,2},{... | collective-permute-start | bytes 122888 | tf_op jit(solution)/shard_map/ppermute | solution.py:39
  669.9 23.1 %collective-permute-start.124 = (bf16[2,16,640]{2,1,0:T(8,128)(2,1)S(1)}, bf16[2,16,640]{2,1,0:T(8,128)(2,1)S(1)}, u32[]{:S(2)}, u32[]{:S(2)}) collective-permute-start(bf16[2,16,640]{2,1,0:T(8,128)(2,1)S(1)} %slice.993), channel_id=1, source_target_pairs={{0,4},{4,8},{8,12},{12,0},{1,5},{5,9},{9,13},{13,1},{2,6},{6,10},{... | collective-permute-start | bytes 122888 | tf_op jit(solution)/shard_map/ppermute | solution.py:39
  686.4 29.2 %collective-permute-start.77 = (bf16[128,2048]{1,0:T(8,128)(2,1)S(1)}, bf16[128,2048]{1,0:T(8,128)(2,1)S(1)}, u32[]{:S(2)}, u32[]{:S(2)}) collective-permute-start(bf16[128,2048]{1,0:T(8,128)(2,1)S(1)} %pad_maximum_fusion.15), channel_id=1, source_target_pairs={{0,96},{32,0},{64,32},{96,64},{1,97},{33,1},{65,33},{97,65},{2,98}... | collective-permute-start | bytes 1572872 | tf_op jit(solution)/shard_map/ppermute | solution.py:39
  689.3 29.4 %collective-permute-start.75 = (bf16[128,2048]{1,0:T(8,128)(2,1)S(1)}, bf16[128,2048]{1,0:T(8,128)(2,1)S(1)}, u32[]{:S(2)}, u32[]{:S(2)}) collective-permute-start(bf16[128,2048]{1,0:T(8,128)(2,1)S(1)} %pad_maximum_fusion.14), channel_id=1, source_target_pairs={{0,32},{32,64},{64,96},{96,0},{1,33},{33,65},{65,97},{97,1},{2,34}... | collective-permute-start | bytes 1572872 | tf_op jit(solution)/shard_map/ppermute | solution.py:39
  (236 other events, 2284.9 us)
Sparse Core Ops, SparseCore 0:
  10.7 75.4 all-gather.11
  87.9 60.9 all-gather.5
  150.6 41.4 all-gather.7
  193.7 41.0 all-gather.9
  382.4 40.0 reduce-scatter.7
  424.8 56.1 reduce-scatter.5
  554.6 43.1 reduce-scatter.3

commit v2 on v1

v2 whole, which is shorter than its diff:
```python
import functools

import jax
import jax.numpy as jnp
from jax import lax
from jax.experimental import pallas as pl
from jax.experimental.pallas import tpu as pltpu
from jax.sharding import Mesh
from jax.sharding import PartitionSpec as P

MODEL_WIDTH = 2048
QUERY_HEADS = 32
KEY_VALUE_HEADS = 4
HEAD_SIZE = 128
TOPK = 8
EXPERTS = 32
CAP = 40
Z, C, Y, X = "z", "c", "y", "x"
FSDP = (Z, C)
EXPERT = (Y, X)
ALL = (Z, C, Y, X)

bf16 = jnp.bfloat16
f32 = jnp.float32
epsilon = 1e-06
rope_base = 1000000.0


def dot(a, b):
    return jnp.dot(a, b, preferred_element_type=f32)


def es(spec, a, b):
    return jnp.einsum(spec, a, b, preferred_element_type=f32)


def shift(v, axis, by):
    n = 2 if axis == C else 4
    return lax.ppermute(v, axis, [(i, (i + by) % n) for i in range(n)])


def gather_fsdp(p, join=lambda *values: values):
    half = p.shape[0] // 2
    up, down = join(shift(p, Z, -1), shift(p, Z, 1))
    other = shift(p, C, 1)
    far_low, far_high = shift(down[:half], Z, 1), shift(up[half:], Z, -1)
    far = [(up, 1, 0), (down, 3, 0), (far_low, 2, 0), (far_high, 2, half)]
    return (
        [(p, 0, 0, 0), (other, 0, 1, 0)]
        + [(a, dz, 0, r) for a, dz, r in far]
        + [(shift(a, C, 1), dz, 1, r) for a, dz, r in far]
    )


def scatter_fsdp(keep, send, join=lambda *values: values):
    got = shift(send, C, 1)
    half = keep.shape[1] // 2

    def both(d, rows=slice(None)):
        return (keep[d, rows].astype(f32) + got[d, rows].astype(f32)).astype(bf16)

    low, high = slice(None, half), slice(half, None)
    far_low, far_high = both(2, low), both(2, high)
    from_down, from_up = shift(far_low, Z, 1), shift(far_high, Z, -1)
    one, three = both(1), both(3)
    one = jnp.concatenate([(one[low].astype(f32) + from_down.astype(f32)).astype(bf16), one[high]])
    three = jnp.concatenate([three[low], (three[high].astype(f32) + from_up.astype(f32)).astype(bf16)])
    one, three = join(one, three)
    from_down, from_up = shift(one, Z, 1), shift(three, Z, -1)
    own = keep[0].astype(f32) + got[0].astype(f32)
    return own + from_down.astype(f32) + from_up.astype(f32)


def gather_ring(v, axis):
    half = v.shape[0] // 2
    up, down = shift(v, axis, -1), shift(v, axis, 1)
    return v, up, shift(down[:half], axis, 1), shift(up[half:], axis, -1), down


def gather_plane(left, right):
    def stacked(parts):
        a, b, low, high, d = parts
        return jnp.stack([a, b, jnp.concatenate([low, high]), d])

    left, right = gather_ring(left, X), gather_ring(right, Y)
    return gather_ring(stacked(left), Y), gather_ring(stacked(right), X)


def sum_all(v):
    v = v + shift(v, C, 1)
    for axis in (Z, Y, X):
        v = (v + shift(v, axis, 2)) + (shift(v, axis, 1) + shift(v, axis, 3))
    return v


def inv_rms(values):
    return lax.rsqrt(jnp.mean(values * values, axis=-1, keepdims=True) + epsilon)


def norm_back(grad_norm, normed, scale_part):
    return scale_part * (grad_norm - normed * jnp.mean(grad_norm * normed, axis=-1, keepdims=True))


def rope_tables(positions):
    frequency = rope_base ** (-(jnp.arange(HEAD_SIZE // 2).astype(f32) * 2.0 / HEAD_SIZE))
    frequency = jnp.concatenate([frequency, frequency])
    angles = positions[:, None] * frequency[None, :]
    return jnp.cos(angles), jnp.sin(angles)


def mm(a, b, dims=((1,), (0,))):
    return lax.dot_general(a, b, (dims, ((), ())), preferred_element_type=f32)


NT = ((1,), (1,))
TN = ((0,), (0,))
ANY = pl.BlockSpec(memory_space=pl.ANY)
VM = pl.BlockSpec(memory_space=pltpu.VMEM)
SM = pl.BlockSpec(memory_space=pltpu.SMEM)
MIB = 1 << 20


def load_pieces(place, spec, pieces, whole, sems):
    copies = []
    for k, (dz, dc, first, rows) in enumerate(spec):
        at = lax.rem(place[0] + dz, 4) * 256 + lax.rem(place[1] + dc, 2) * 128 + first
        at = pl.multiple_of(at, 64)
        copies.append(pltpu.make_async_copy(pieces[k], whole.at[pl.ds(at, rows)], sems.at[k]))
    for copy in copies:
        copy.start()
    return copies


def load_weights(place, parts, w, sems):
    copies = []
    width = w.shape[3] // 2
    own, from_x, from_y = parts
    for k in range(8):
        source = lax.rem(place[0] + 4 - k % 4, 4) * 2 + lax.rem(place[1] + k // 4, 2)
        for side, (at, other) in enumerate(((place[3], from_x), (place[2], from_y))):
            cols = pl.ds(side * width, width)
            for j, piece in enumerate((own.at[k, :, cols], other.at[k])):
                into = w.at[source, lax.rem(at + j, 2), :, cols]
                copies.append(pltpu.make_async_copy(piece, into, sems.at[4 * k + 2 * side + j]))
    for copy in copies:
        copy.start()
    return copies


def attention_kernel(spec, place, w_out, q_gain, k_gain, cosine, sine, *rest):
    n = len(spec)
    pieces, parts, rest = rest[:n], rest[n : n + 3], rest[n + 3 :]
    w, h1, q_raw, k_raw, v_b, q_b, k_b, a_b, lse, keep, send, sems, w_sems = rest
    z, c = place[0], place[1]
    copies = load_weights(place, parts, w, w_sems)
    for copy in load_pieces(place, spec, pieces, h1, sems) + copies:
        copy.wait()

    @pl.loop(0, 4)
    def _(i):
        rows = pl.ds(pl.multiple_of(i * 256, 256), 256)
        t = mm(h1[rows, :MODEL_WIDTH], w[...].reshape(MODEL_WIDTH, 768))
        q_raw[rows] = t[:, :512]
        k_raw[rows] = t[:, 512:640]
        v_b[rows] = t[:, 640:].astype(bf16)
        co, si = cosine[rows], sine[rows]

        def rotated(u, gain):
            u = u * lax.rsqrt(jnp.mean(u * u, axis=-1, keepdims=True) + epsilon) * gain
            return (u * co + pltpu.roll(u, 64, 1) * si).astype(bf16)

        for h in range(4):
            q_b[h, rows] = rotated(t[:, 128 * h : 128 * h + 128], q_gain[...])
        k_b[rows] = rotated(t[:, 512:640], k_gain[...])

    lane = lax.broadcasted_iota(jnp.int32, (256, 128), 1)
    below = lax.broadcasted_iota(jnp.int32, (256, 256), 0) >= lax.broadcasted_iota(
        jnp.int32, (256, 256), 1
    )
    for i in range(4):
        n_keys = 256 * (i + 1)
        rows = slice(256 * i, n_keys)
        logs = jnp.zeros((256, 128), f32)
        for h in range(4):
            s = mm(q_b[h, rows], k_b[:n_keys], NT) * (HEAD_SIZE**-0.5)
            e = jnp.exp(s)
            tail = jnp.where(below, e[:, n_keys - 256 :], 0.0)
            e = tail if i == 0 else jnp.concatenate([e[:, : n_keys - 256], tail], axis=1)
            total = jnp.sum(e, axis=1, keepdims=True)
            a = mm(e.astype(bf16), v_b[:n_keys]) / total
            a_b[rows, 128 * h : 128 * h + 128] = a.astype(bf16)
            logs = jnp.where(lane == h, jnp.log(total), logs)
        lse[rows] = logs
        part = mm(a_b[rows], w_out[...]).astype(bf16)
        dz = lax.rem(i - z + 4, 4)
        first, second = part[:128], part[128:]
        keep[dz] = jnp.where(c == 0, first, second)
        send[dz] = jnp.where(c == 0, second, first)


def attention_forward(pieces, parts, place, w_out, q_gain, k_gain, cosine, sine):
    spec = [(dz, dc, first, a.shape[0]) for a, dz, dc, first in pieces]
    seq = 1024
    shapes = [
        ((8, 2, 128, 768), bf16),
        ((seq, MODEL_WIDTH + 128), bf16),
        ((seq, 512), f32),
        ((seq, 128), f32),
        ((seq, 128), bf16),
        ((4, seq, 128), bf16),
        ((seq, 128), bf16),
        ((seq, 512), bf16),
        ((seq, 128), f32),
        ((4, 128, MODEL_WIDTH), bf16),
        ((4, 128, MODEL_WIDTH), bf16),
    ]
    return pl.pallas_call(
        functools.partial(attention_kernel, spec),
        out_shape=[jax.ShapeDtypeStruct(*s) for s in shapes],
        in_specs=[SM] + [VM] * 5 + [ANY] * (len(spec) + 3),
        out_specs=[VM] * len(shapes),
        scratch_shapes=[pltpu.SemaphoreType.DMA((len(spec),)), pltpu.SemaphoreType.DMA((32,))],
        compiler_params=pltpu.CompilerParams(vmem_limit_bytes=56 * MIB),
        cost_estimate=pl.CostEstimate(flops=9 << 30, bytes_accessed=28 << 20, transcendentals=3 << 20),
        name="attention_forward",
    )(place, w_out, q_gain, k_gain, cosine, sine, *[p[0] for p in pieces], *parts)


def expert_kernel(e, xs_in, dys_in, w_in, w_down, back, hid, dg, du, xs, dys, wg, wu, wd, sems):
    loads = []
    for k, (source, into) in enumerate(
        (
            (xs_in.at[:, pl.ds(0, MODEL_WIDTH)], xs), (w_in.at[e], wg), (w_in.at[2 + e], wu), (dys_in, dys), (w_down.at[e], wd),
        )
    ):
        loads.append(pltpu.make_async_copy(source, into, sems.at[k]))
        loads[-1].start()
    total = jnp.zeros((640, 1), f32)
    for k in range(3):
        loads[k].wait()
    for i in range(3):
        cols = slice(256 * i, 256 * i + 256)
        g, u = mm(xs[...], wg[:, cols]), mm(xs[...], wu[:, cols])
        if i == 0:
            loads[3].wait()
            loads[4].wait()
        d = mm(dys[...], wd[cols], NT)
        sig = 0.5 + 0.5 * jnp.tanh(0.5 * g)
        act = g * sig
        h = act * u
        total = total + jnp.sum(d * h, axis=1, keepdims=True)
        hid[:, cols] = h.astype(bf16)
        du[:, cols] = (d * act).astype(bf16)
        dg[:, cols] = (d * u * (sig + act * (1.0 - sig))).astype(bf16)
    back[:, :MODEL_WIDTH] = (mm(dg[...], wg[...], NT) + mm(du[...], wu[...], NT)).astype(bf16)
    high = total.astype(bf16).astype(f32)
    lane = lax.broadcasted_iota(jnp.int32, (640, 128), 1)
    back[:, MODEL_WIDTH:] = jnp.where(lane == 0, high, jnp.where(lane == 1, total - high, 0.0)).astype(bf16)


def expert_rows(e, xs, dys, w_in, w_down):
    row, act = (640, MODEL_WIDTH), (640, 768)
    scratch = [row, row, (MODEL_WIDTH, 768), (MODEL_WIDTH, 768), (768, MODEL_WIDTH)]
    return pl.pallas_call(
        functools.partial(expert_kernel, e),
        out_shape=[jax.ShapeDtypeStruct(s, bf16) for s in ((640, MODEL_WIDTH + 128), act, act, act)],
        in_specs=[ANY] * 4,
        out_specs=[VM] * 4,
        scratch_shapes=[pltpu.VMEM(s, bf16) for s in scratch] + [pltpu.SemaphoreType.DMA((5,))],
        compiler_params=pltpu.CompilerParams(vmem_limit_bytes=48 * MIB),
        cost_estimate=pl.CostEstimate(flops=10 << 30, bytes_accessed=20 << 20, transcendentals=1 << 20),
        name="expert_rows",
    )(xs, dys, w_in, w_down)


def weight_grads_kernel(*refs):
    rows, w_down, grads, ys = refs[:12], refs[12], refs[14:17], refs[17:19]
    first = pl.program_id(0) == 0
    for e in range(2):
        xs, dys, hid, dg, du, gate = rows[6 * e : 6 * e + 6]

        @pl.when(first if e == 0 else jnp.logical_not(first))
        def _(xs=xs, dys=dys, hid=hid, dg=dg, du=du, gate=gate, out=ys[e]):
            s = gate[:, 0:1]

            def scaled(v):
                return (v[...].astype(f32) * s).astype(bf16)

            out[...] = mm(hid[...], w_down[0]).astype(bf16)
            grads[0][0] = mm(xs[:, :MODEL_WIDTH], scaled(dg), TN).astype(bf16)
            grads[1][0] = mm(xs[:, :MODEL_WIDTH], scaled(du), TN).astype(bf16)
            grads[2][0] = mm(scaled(hid), dys[...], TN).astype(bf16)


def weight_grads(rows, w_down, event):
    def per_expert(*dims):
        return pl.BlockSpec((1, *dims), lambda e: (e, 0, 0))

    sizes = [(MODEL_WIDTH, 768), (MODEL_WIDTH, 768), (768, MODEL_WIDTH)]
    return pl.pallas_call(
        weight_grads_kernel,
        grid=(2,),
        out_shape=[jax.ShapeDtypeStruct((2, *s), bf16) for s in sizes]
        + [jax.ShapeDtypeStruct((640, MODEL_WIDTH), bf16)] * 2,
        in_specs=[VM] * 12 + [per_expert(768, MODEL_WIDTH), ANY],
        out_specs=[per_expert(*s) for s in sizes] + [VM] * 2,
        compiler_params=pltpu.CompilerParams(vmem_limit_bytes=60 * MIB),
        cost_estimate=pl.CostEstimate(flops=16 << 30, bytes_accessed=48 << 20, transcendentals=0),
        name="weight_grads",
    )(*rows, w_down, event)


def out_back_kernel(spec, place, w_out, a_b, *rest):
    n = len(spec)
    pieces, (dob, shares, da, sems) = rest[:n], rest[n:]
    for copy in load_pieces(place, spec, pieces, da, sems):
        copy.wait()

    @pl.loop(0, 4)
    def _(i):
        rows = pl.ds(pl.multiple_of(i * 256, 256), 256)
        dob[rows] = mm(da[rows], w_out[...], NT).astype(bf16)

    shares[...] = mm(a_b[...], da[...], TN).astype(bf16)


def out_back(pieces, place, w_out, a_b):
    spec = [(dz, dc, first, a.shape[0]) for a, dz, dc, first in pieces]
    shapes = [((1024, 512), bf16), ((512, MODEL_WIDTH), bf16)]
    return pl.pallas_call(
        functools.partial(out_back_kernel, spec),
        out_shape=[jax.ShapeDtypeStruct(*s) for s in shapes],
        in_specs=[SM] + [VM] * 2 + [ANY] * len(spec),
        out_specs=[VM] * 2,
        scratch_shapes=[pltpu.VMEM((1024, MODEL_WIDTH), bf16), pltpu.SemaphoreType.DMA((len(spec),))],
        compiler_params=pltpu.CompilerParams(vmem_limit_bytes=40 * MIB),
        cost_estimate=pl.CostEstimate(flops=5 << 30, bytes_accessed=12 << 20, transcendentals=0),
        name="out_back",
    )(place, w_out, a_b, *[p[0] for p in pieces])


def attention_back_kernel(dob, a_b, q_b, k_b, v_b, lse, q_raw, q_gain, cosine, sine, dq_raw, dkv, gain):
    root = HEAD_SIZE**-0.5
    below = lax.broadcasted_iota(jnp.int32, (256, 256), 0) >= lax.broadcasted_iota(
        jnp.int32, (256, 256), 1
    )
    dkv[...] = jnp.zeros(dkv.shape, f32)
    total = jnp.zeros((1, HEAD_SIZE), f32)
    for i in range(4):
        keys = 256 * (i + 1)
        rows = slice(256 * i, keys)
        co, si = cosine[rows], sine[rows]
        for h in range(4):
            cols = slice(128 * h, 128 * h + 128)
            q, do = q_b[h, rows], dob[rows, cols]
            p = jnp.exp(mm(q, k_b[:keys], NT) * root - lse[rows, h : h + 1])
            tail = jnp.where(below, p[:, keys - 256 :], 0.0)
            p = tail if i == 0 else jnp.concatenate([p[:, : keys - 256], tail], axis=1)
            dp = mm(do, v_b[:keys], NT)
            mean = jnp.sum(do.astype(f32) * a_b[rows, cols].astype(f32), axis=1, keepdims=True)
            ds = (p * (dp - mean)).astype(bf16)
            dkv[:keys, :128] += mm(ds, q, TN) * root
            dkv[:keys, 128:] += mm(p.astype(bf16), do, TN)
            dq = (mm(ds, k_b[:keys]) * root).astype(bf16).astype(f32)
            dq_in = dq * co + pltpu.roll(dq * si, 64, 1)
            raw = q_raw[rows, cols]
            scale = lax.rsqrt(jnp.mean(raw * raw, axis=-1, keepdims=True) + epsilon)
            hat = raw * scale
            total = total + jnp.sum(dq_in * hat, axis=0, keepdims=True)
            t = dq_in * q_gain[...]
            back = scale * (t - hat * jnp.mean(t * hat, axis=-1, keepdims=True))
            dq_raw[rows, cols] = back.astype(bf16)
    gain[...] = total


def attention_backward(dob, a_b, q_b, k_b, v_b, lse, q_raw, q_gain, cosine, sine):
    shapes = [((1024, 512), bf16), ((1024, 256), f32), ((1, HEAD_SIZE), f32)]
    return pl.pallas_call(
        attention_back_kernel,
        out_shape=[jax.ShapeDtypeStruct(*s) for s in shapes],
        in_specs=[VM] * 10,
        out_specs=[VM] * 3,
        compiler_params=pltpu.CompilerParams(vmem_limit_bytes=48 * MIB),
        cost_estimate=pl.CostEstimate(flops=10 << 30, bytes_accessed=12 << 20, transcendentals=3 << 20),
        name="attention_backward",
    )(dob, a_b, q_b, k_b, v_b, lse, q_raw, q_gain, cosine, sine)


def grads_kernel(
    place, dq_raw, own, other, k_raw, q_part, k_gain, cosine, sine, h1, w, aux, _,
    shares, dqkv, along_out, k_part,
):
    c = place[1]
    dqkv[:, :512] = dq_raw[...]
    total = jnp.zeros((1, HEAD_SIZE), f32)
    for i in range(4):
        rows = slice(256 * i, 256 * i + 256)
        both = (own[rows] + other[rows]).astype(bf16)
        dk = both[:, :128].astype(f32)
        dk_in = dk * cosine[rows] + pltpu.roll(dk * sine[rows], 64, 1)
        raw = k_raw[rows]
        scale = lax.rsqrt(jnp.mean(raw * raw, axis=-1, keepdims=True) + epsilon)
        hat = raw * scale
        total = total + jnp.sum(dk_in * hat, axis=0, keepdims=True)
        t = dk_in * k_gain[...]
        grad = scale * (t - hat * jnp.mean(t * hat, axis=-1, keepdims=True))
        dqkv[rows, 512:] = jnp.where(c == 0, grad, both[:, 128:].astype(f32)).astype(bf16)
    k_part[...] = total * 0.5
    for f in range(8):
        shard = slice(256 * f, 256 * f + 256)
        part = mm(h1[:, shard], dqkv[...], TN)
        last = jnp.where(c == 0, w[shard, 512:640], w[shard, 640:])
        along = jnp.sum(part[:, :512] * w[shard, :512].astype(f32), axis=1, keepdims=True)
        along = along + jnp.sum(part[:, 512:] * last.astype(f32), axis=1, keepdims=True)
        along_out[shard] = jnp.broadcast_to(along, (256, 128))
        part = jnp.concatenate([part.astype(bf16), aux[shard].astype(bf16)], axis=1)
        for r in range(16):
            shares[r, 16 * f : 16 * f + 16] = part[16 * r : 16 * r + 16]


def projection_grads(place, dq_raw, own, other, k_raw, q_part, k_gain, cosine, sine, h1, w, aux, event):
    shapes = [((16, 128, 768), bf16), ((1024, 640), bf16), ((MODEL_WIDTH, 128), f32), ((1, HEAD_SIZE), f32)]
    return pl.pallas_call(
        grads_kernel,
        out_shape=[jax.ShapeDtypeStruct(*s) for s in shapes],
        in_specs=[SM] + [VM] * 11 + [ANY],
        out_specs=[VM] * 4,
        compiler_params=pltpu.CompilerParams(vmem_limit_bytes=48 * MIB),
        cost_estimate=pl.CostEstimate(flops=3 << 30, bytes_accessed=16 << 20, transcendentals=0),
        name="projection_grads",
    )(place, dq_raw, own, other, k_raw, q_part, k_gain, cosine, sine, h1, w, aux, event)


def input_grad_kernel(place, dqkv, w, keep, send, w_own):
    z, c = place[0], place[1]
    w_own[:, :512] = w[:, :512]
    w_own[:, 512:] = jnp.where(c == 0, w[:, 512:640], w[:, 640:])

    @pl.loop(0, 4)
    def _(i):
        rows = pl.ds(pl.multiple_of(i * 256, 256), 256)
        part = mm(dqkv[rows], w_own[...], NT).astype(bf16)
        dz = lax.rem(i - z + 4, 4)
        first, second = part[:128], part[128:]
        keep[dz] = jnp.where(c == 0, first, second)
        send[dz] = jnp.where(c == 0, second, first)


def input_grad(place, dqkv, w):
    return pl.pallas_call(
        input_grad_kernel,
        out_shape=[jax.ShapeDtypeStruct((4, 128, MODEL_WIDTH), bf16)] * 2,
        in_specs=[SM, VM, VM],
        out_specs=[VM] * 2,
        scratch_shapes=[pltpu.VMEM((MODEL_WIDTH, 640), bf16)],
        compiler_params=pltpu.CompilerParams(vmem_limit_bytes=40 * MIB),
        cost_estimate=pl.CostEstimate(flops=3 << 30, bytes_accessed=8 << 20, transcendentals=0),
        name="input_grad",
    )(place, dqkv, w)


def part_of(outer, inner):
    return {0: (0, inner), 1: (1, inner), 2: (2 + inner // 2, inner % 2), 3: (4, inner)}[outer]


def place_kernel(idx, *refs):
    left, right, (query, key, value, aux, out) = refs[:5], refs[5:10], refs[-5:]
    for r in range(16):
        dy, dx = divmod(r, 4)
        rows = pl.ds(pl.multiple_of(idx[r] * 16, 16), 16)
        a, ai = part_of(dy, dx)
        b, bi = part_of(dx, dy)
        total = jnp.zeros((16, 128), f32)
        for f in range(8):
            block = (left[a][ai, f] if f < 4 else right[b][bi, f - 4]).astype(f32)
            query[rows, 512 * f : 512 * f + 512] = block[:, :512]
            to = key if f % 2 == 0 else value
            to[rows, 128 * (f // 2) : 128 * (f // 2) + 128] = block[:, 512:640]
            total = total + block[:, 640:768]
            out_rows = pl.ds(pl.multiple_of(idx[r] * 32 + 16 * (f % 2), 16), 16)
            out[out_rows, 512 * (f // 2) : 512 * (f // 2) + 512] = block[:, 768:]
        aux[rows] = total


def place_rows(idx, left, right, *events):
    shapes = [(256, 4096), (256, 512), (256, 512), (256, 128), (512, MODEL_WIDTH)]
    return pl.pallas_call(
        place_kernel,
        out_shape=[jax.ShapeDtypeStruct(s, f32) for s in shapes],
        in_specs=[SM] + [VM] * 10 + [ANY] * len(events),
        out_specs=[VM] * 5,
        compiler_params=pltpu.CompilerParams(vmem_limit_bytes=40 * MIB),
        cost_estimate=pl.CostEstimate(flops=0, bytes_accessed=16 << 20, transcendentals=0),
        name="place_rows",
    )(idx, *left, *right, *events)


def nothing(*refs):
    pass


def after(values, *events):
    n = len(values)
    return pl.pallas_call(
        nothing,
        out_shape=[jax.ShapeDtypeStruct(v.shape, v.dtype) for v in values],
        in_specs=[ANY] * (n + len(events)),
        out_specs=[ANY] * n,
        input_output_aliases={i: i for i in range(n)},
        cost_estimate=pl.CostEstimate(flops=0, bytes_accessed=0, transcendentals=0),
        name="after",
    )(*values, *events)


def local(
    layer_input, routes, cotangent, attn_gain, query_gain, key_gain, mlp_gain,
    w_query, key_weight, value_weight, w_out, w_router, w_gate, w_up, w_down,
):
    core = lax.axis_index(C)
    py, px = lax.axis_index(Y), lax.axis_index(X)
    zc = jnp.stack([lax.axis_index(Z), core, py, px]).astype(jnp.int32)
    ahead = jnp.arange(16, dtype=jnp.int32)
    idx = (py + ahead // 4) % 4 * 4 + (px + ahead % 4) % 4
    residual = layer_input[0].astype(f32)
    dy_low = cotangent[0]
    upstream = dy_low.astype(f32)
    scale_one = inv_rms(residual)
    normed_one = residual * scale_one
    h1 = (normed_one * attn_gain).astype(bf16)
    beside = jnp.pad(w_router.reshape(128, 64), ((0, 0), (0, 64)))
    h1 = jnp.concatenate([h1, beside], axis=1)
    seq = 1024
    cosine, sine = rope_tables(jnp.arange(seq).astype(f32))
    sign = jnp.where(jnp.arange(HEAD_SIZE) < HEAD_SIZE // 2, -1.0, 1.0).astype(f32)
    signed = sine * sign
    ids = jnp.arange(EXPERTS, dtype=jnp.int32)
    chosen = jnp.any(routes[0][:, :, None] == ids, axis=1)
    before = jnp.tril(jnp.ones((128, 128), bf16), -1)
    rank = dot(before, chosen.astype(bf16)).astype(jnp.int32)
    slot = jnp.where(chosen, rank, -1).T.reshape(16, 2, 128).transpose(1, 0, 2)
    picks = (slot[:, :, None, :] == jnp.arange(CAP)[:, None]).reshape(2, 640, 128)

    def sent(e, v):
        packed = dot(picks[e].astype(bf16), v).astype(bf16)
        return packed.reshape(16, CAP, MODEL_WIDTH)

    def exchanged(v):
        return lax.all_to_all(v, EXPERT, 0, 0, tiled=True)

    dy_all = lax.all_gather(dy_low, EXPERT, axis=0, tiled=False)
    tokens = jnp.arange(128, dtype=jnp.int32)
    slot_token = jnp.max(jnp.where(picks, tokens, -1), axis=-1).reshape(2, 16, CAP).transpose(1, 0, 2)
    slot_token = exchanged(slot_token.astype(f32)).astype(jnp.int32)
    taken = (slot_token.transpose(1, 0, 2)[..., None] == tokens).astype(bf16)
    dys = [es("sct,std->scd", taken[e], dy_all).astype(bf16).reshape(640, MODEL_WIDTH) for e in range(2)]
    in_own = jnp.concatenate([w_gate, w_up])
    rows = w_query.shape[0]

    def per_head(w, n):
        return jnp.repeat(w.reshape(rows, 4, 128), 2, axis=1) if n == 2 else w.reshape(rows, 8, 512)

    blocks = jnp.concatenate([per_head(w_query, 1), per_head(key_weight, 2), per_head(value_weight, 2)], axis=2)
    blocks = blocks.reshape(2, 128, 8, 768)
    halved = jnp.concatenate(
        [
            jnp.where(px % 2 == 0, blocks[0, :, :, :384], blocks[1, :, :, :384]),
            jnp.where(py % 2 == 0, blocks[0, :, :, 384:], blocks[1, :, :, 384:]),
        ],
        axis=2,
    ).transpose(1, 0, 2)
    halved = halved.reshape(4, 2, 128, 768)
    halved = jnp.where(core == 0, halved, halved[:, ::-1])
    place_z = lax.axis_index(Z)

    def meant_for(ahead):
        return lax.dynamic_index_in_dim(halved, (place_z + ahead) % 4, 0, keepdims=False)

    arrived = [shift(meant_for(d), Z, d) for d in range(1, 4)]
    h1_pieces = gather_fsdp(h1, lambda up, down: after([up, down], *arrived, slot_token, cosine, signed, in_own))
    arrived = jnp.stack([meant_for(0)] + arrived, axis=1)
    arrived = jnp.concatenate([arrived[0], shift(arrived[1], C, 1)])
    swap = [(0, 1), (1, 0), (2, 3), (3, 2)]
    w_parts = [
        arrived, lax.ppermute(arrived[:, :, :384], X, swap), lax.ppermute(arrived[:, :, 384:], Y, swap)
    ]
    in_own, down_own = after(
        [in_own, w_down], arrived, h1_pieces[4][0], h1_pieces[5][0]
    )
    in_all = lax.all_gather(in_own, FSDP, axis=1, tiled=True)
    down_all = lax.all_gather(down_own, FSDP, axis=1, tiled=True)
    w, h1_all, q_raw, k_raw, v_b, q_b, k_b, a_b, lse, keep, send = attention_forward(
        h1_pieces, w_parts, zc, w_out, query_gain[None], key_gain[None], cosine, signed
    )
    router = h1_all[:, MODEL_WIDTH : MODEL_WIDTH + 64].reshape(MODEL_WIDTH, EXPERTS)
    w = w.reshape(MODEL_WIDTH, 768)
    attn = scatter_fsdp(keep, send)
    resid_two = residual + attn
    scale_two = inv_rms(resid_two)
    normed_two = resid_two * scale_two
    h2 = (normed_two * mlp_gain).astype(bf16)
    xs_first = exchanged(sent(0, h2))
    logits = jnp.where(chosen, dot(h2, router), -1e30)
    powers = jnp.where(chosen, jnp.exp(logits - jnp.max(logits, axis=-1, keepdims=True)), 0.0)
    gates = powers / jnp.sum(powers, axis=-1, keepdims=True)
    gates_slot = gates.T.reshape(16, 2, 128).transpose(1, 0, 2)
    weighted = jnp.where(picks.reshape(2, 16, CAP, 128), gates_slot[:, :, None, :], 0.0)
    slot_gate = jnp.sum(weighted, axis=-1)
    high = slot_gate.astype(bf16)
    low = (slot_gate - high.astype(f32)).astype(bf16)
    beside = jnp.stack([high[0], low[0], high[1], low[1]], axis=-1)
    beside = jnp.pad(beside, ((0, 0), (0, 0), (0, 124)))
    second = jnp.concatenate([sent(1, h2), beside], axis=-1)
    (second,) = after([second], xs_first)
    xs_second = exchanged(second)
    xs = [xs_first.reshape(640, MODEL_WIDTH), xs_second.reshape(640, MODEL_WIDTH + 128)]
    back_first, *kept_first = expert_rows(0, xs[0], dys[0], in_all, down_all)
    wide = (16, CAP, MODEL_WIDTH + 128)
    (back_first,) = after([back_first.reshape(wide)], xs_second)
    from_first = exchanged(back_first)
    back_second, *kept_second = expert_rows(1, xs[1], dys[1], in_all, down_all)
    (back_second,) = after([back_second.reshape(wide)], from_first)
    from_second = exchanged(back_second)
    got = xs[1][:, MODEL_WIDTH : MODEL_WIDTH + 4].astype(f32)
    slot_gate = [jnp.broadcast_to(got[:, 2 * e : 2 * e + 1] + got[:, 2 * e + 1 : 2 * e + 2], (640, 128)) for e in range(2)]
    weighted = weighted.reshape(2, 640, 128).astype(bf16)

    def combined(parts):
        return sum(es("rt,rd->td", weighted[e], parts[e].reshape(640, -1)[:, :MODEL_WIDTH]) for e in range(2))

    kept = [
        (xs[e], dys[e], *kept, slot_gate[e]) for e, kept in enumerate((kept_first, kept_second))
    ]
    grad_gate, grad_up, grad_down, *ys = weight_grads([*kept[0], *kept[1]], down_all, from_first)
    grad_gate, grad_up, grad_down = after([grad_gate, grad_up, grad_down], from_second)
    (from_second,) = after([from_second], ys[0])
    backs = [from_first, from_second]
    dh_sum = combined(backs)
    dgate = [v.reshape(640, -1)[:, MODEL_WIDTH : MODEL_WIDTH + 2].astype(f32).sum(axis=1) for v in backs]
    dgate = jnp.stack(dgate).reshape(2, 16, CAP, 1)
    dgate = jnp.sum(jnp.where(picks.reshape(2, 16, CAP, 128), dgate, 0.0), axis=2)
    dgate = dgate.transpose(2, 1, 0).reshape(128, EXPERTS)
    dl = (gates * (dgate - jnp.sum(gates * dgate, axis=-1, keepdims=True))).astype(bf16)
    dh2 = es("te,de->td", dl, router) + dh_sum
    dx2 = upstream + norm_back(dh2 * mlp_gain, normed_two, scale_two)
    da = dx2.astype(bf16)
    y_first, y_second = (v.reshape(16, CAP, MODEL_WIDTH) for v in ys)
    y_first = exchanged(y_first)
    da_pieces = gather_fsdp(da, lambda up, down: after([up, down], y_first))
    (y_second,) = after([y_second], da_pieces[2][0])
    y_second = exchanged(y_second)
    output = (resid_two + combined([y_first, y_second])).astype(bf16)
    aux = jnp.pad(es("td,te->de", h2, dl), ((0, 0), (0, 128 - EXPERTS)))
    grad_mlp_gain = jnp.sum(dh2 * normed_two, axis=0)
    def scattered(v):
        return lax.psum_scatter(v, FSDP, scatter_dimension=1, tiled=True)

    def summed(v):
        return jnp.sum(exchanged(v).astype(f32), axis=0).astype(bf16)

    grad_gate, grad_up, grad_down = scattered(grad_gate), scattered(grad_up), scattered(grad_down)
    dob, out_shares = out_back(da_pieces, zc, w_out, a_b)
    (out_shares,) = after([out_shares.reshape(16, 32, MODEL_WIDTH)], y_second)
    grad_out = summed(out_shares)
    dq_raw, dkv, q_part = attention_backward(
        dob, a_b, q_b, k_b, v_b, lse, q_raw, query_gain[None], cosine, signed
    )
    shares, dqkv, along, k_part = projection_grads(
        zc, dq_raw, dkv, shift(dkv, C, 1), k_raw, q_part, key_gain[None], cosine, signed, h1_all, w, aux,
        grad_out,
    )
    keep, send = input_grad(zc, dqkv, w)
    dh1 = scatter_fsdp(keep, send)
    gains = jnp.concatenate([along[:, 0], grad_mlp_gain, q_part[0], k_part[0]]).reshape(34, 128)
    gains = sum_all(gains).reshape(-1)
    (shares,) = after([summed(shares).reshape(8, 16, 768)], dh1)
    parted = lax.all_to_all(shares, FSDP, 0, 0, tiled=True)
    grad_out = grad_out.reshape(2, 16, 4, 512).transpose(2, 0, 1, 3).reshape(8, 16, 512)
    parted = jnp.concatenate([parted, grad_out], axis=2)
    grad_input = dx2 + norm_back(dh1 * attn_gain, normed_one, scale_one)
    expert_grads = [v.astype(f32) for v in (grad_gate, grad_up, grad_down)]
    grad_query, grad_key, grad_value, aux, grad_out = place_rows(
        idx, *gather_plane(parted[:4], parted[4:]), gains, *expert_grads
    )
    return (
        output[None],
        grad_input.astype(bf16)[None],
        gains[:MODEL_WIDTH] / attn_gain,
        gains[2 * MODEL_WIDTH : 2 * MODEL_WIDTH + HEAD_SIZE],
        gains[2 * MODEL_WIDTH + HEAD_SIZE :],
        gains[MODEL_WIDTH : 2 * MODEL_WIDTH],
        grad_query,
        grad_key,
        grad_value,
        grad_out,
        aux[:, :EXPERTS],
        *expert_grads,
    )


def solution(mesh):
    torus = Mesh(mesh.devices.reshape(4, 2, 4, 4), ALL)
    tokens, rows, experts = P(EXPERT, FSDP, None), P(FSDP, None), P(EXPERT, FSDP, None)
    return jax.shard_map(
        local,
        mesh=torus,
        in_specs=(tokens,) * 3 + (P(),) * 4 + (rows,) * 5 + (experts,) * 3,
        out_specs=(tokens,) * 2 + (P(),) * 4 + (rows,) * 5 + (experts,) * 3,
        check_vma=False,
    )
```

time: 791 us -> 623 us (0.79)
  starting transfers between devices: 219 us -> 129 us
  waiting for transfers between devices: 278 us -> 210 us
  other arithmetic: 64.7 us -> 43.5 us
  Pallas kernels: 120 us -> 129 us
    ppermute x162 -> x59, waiting for transfers between devices: 260 us -> 62.3 us  [shift(): return lax.ppermute(v, axis, [(i, (i + by) % n) for i in range(n)])]
    ppermute x162 -> x59, starting transfers between devices: 203 us -> 75.9 us  [shift(): return lax.ppermute(v, axis, [(i, (i + by) % n) for i in range(n)])]
    all_to_all x4 -> x10, waiting for transfers between devices: 17.1 us -> 125 us  [the longest x9 122 us: exchanged(): return lax.all_to_all(v, EXPERT, 0, 0, tiled=True)]
    all_to_all x4 -> x10, starting transfers between devices: 16 us -> 49.9 us  [the longest x9 45.8 us: exchanged(): return lax.all_to_all(v, EXPERT, 0, 0, tiled=True)]
    ppermute x0 -> x2, waiting for transfers between devices: none -> 21.1 us  [the longest x1 21.1 us: local(): lax.ppermute(arrived[:, :, :384], X, swap)]
    convert_element_type x36 -> x8, other arithmetic: 24 us -> 6.02 us  [the longest x3 4.9 us: local(): expert_grads = [v.astype(f32) for v in (grad_gate, grad_up, grad_down)]]
    unnamed x192 -> x191, local copies, waits for them, and re-layouts: 28.8 us -> 41.1 us
    dot_general x6 -> x8, matrix products: 33.8 us -> 23.6 us  [es(): return jnp.einsum(spec, a, b, preferred_element_type=f32)]
  transfers between devices with their start and end apart: 173 -> 77, of which waited for: 66 -> 25; matrix products, arithmetic and copies ran while one was open for 13% -> 15% of each run, Pallas kernels for 10% -> 20%
where the time goes in v2:
time: 623 us; the launch traced here: 613 us
  waiting for transfers between devices  210 us (34%)
  starting transfers between devices  129 us (21%)
  Pallas kernels  129 us (21%)
  local copies, waits for them, and re-layouts  57.4 us (9%)
  other arithmetic  43.5 us (7%)
  matrix products  28.3 us (5%)
  between operations  16.1 us (3%)
    all_to_all x9, waiting for transfers between devices, exchanged(): return lax.all_to_all(v, EXPERT, 0, 0, tiled=True)  122 us
    ppermute x59, starting transfers between devices, shift(): return lax.ppermute(v, axis, [(i, (i + by) % n) for i in range(n)])  75.9 us
    ppermute x59, waiting for transfers between devices, shift(): return lax.ppermute(v, axis, [(i, (i + by) % n) for i in range(n)])  62.3 us
    all_to_all x9, starting transfers between devices, exchanged(): return lax.all_to_all(v, EXPERT, 0, 0, tiled=True)  45.8 us
    unnamed x191, local copies, waits for them, and re-layouts  41.1 us
    pallas_call x2, Pallas kernels, expert_rows(): pl.pallas_call(functools.partial(expert_kernel, e), out_shape=[jax.ShapeD...  35.4 us
    pallas_call x1, Pallas kernels, weight_grads(): pl.pallas_call(weight_grads_kernel, grid=(2,), out_shape=[jax.ShapeDtypeS...  31.7 us
    dot_general x8, matrix products, es(): return jnp.einsum(spec, a, b, preferred_element_type=f32)  23.6 us
  transfers between devices with their start and end apart: 77, of which 25 were waited for; matrix products, arithmetic and copies ran while one was open for 15% of the time, Pallas kernels for 20%

profile of v2, /device:TPU:0, one launch (start us, length us, event | category | flops | bytes accessed | tf_op | source)
XLA Modules:
  0.0 613.1 jit_solution(1155436322827152186)
XLA Ops:
  21.5 4.7 collective-permute-start.4
  27.7 7.0 %all-to-all-start = ((f32[16,2,40]{2,1,0:T(2,128)}), f32[16,2,40]{2,1,0:T(2,128)S(1)}, u32[]{:S(2)}, u32[]{:S(2)}) async-start(f32[16,2,40]{2,1,0:T(2,128)} %bitcast.226), calls=%async_computation | async-start | bytes 32768 | tf_op jit(solution)/shard_map/all_to_all | solution.py:548
  36.1 12.0 %collective-permute-done.3.refs_2_ = bf16[2,128,768]{2,1,0:T(8,128)(2,1)S(1)} collective-permute-done((bf16[2,128,768]{2,1,0:T(8,128)(2,1)}, bf16[2,128,768]{2,1,0:T(8,128)(2,1)S(1)}, u32[]{:S(2)}, u32[]{:S(2)}) %collective-permute-start.3) | collective-permute-done | bytes 393248 | tf_op jit(solution)/shard_map/ppermute | solution.py:39
  77.3 21.1 %collective-permute-done.13.rest_11_ = bf16[8,128,384]{2,1,0:T(8,128)(2,1)S(1)} collective-permute-done((bf16[8,128,384]{2,1,0:T(8,128)(2,1)S(1)}, bf16[8,128,384]{2,1,0:T(8,128)(2,1)S(1)}, u32[]{:S(2)}, u32[]{:S(2)}) %collective-permute-start.13) | collective-permute-done | bytes 786464 | tf_op jit(solution)/shard_map/ppermute | solution.py:584
  99.6 19.2 %attention_forward.1 = (bf16[8,2,128,768]{3,2,1,0:T(8,128)(2,1)}, bf16[1024,2176]{1,0:T(8,128)(2,1)}, f32[1024,512]{1,0:T(8,128)}, f32[1024,128]{1,0:T(8,128)}, ...) custom-call(s32[4]{0:T(128)} %pad_add_fusion.place, ...), custom_call_target="tpu_custom_call" | custom-call | flops 9663676416 | bytes 29360128 | tf_op jit(solution)/shard_map/attention_forward/pallas_call | solution.py:217
  129.4 9.1 %collective-permute-done.16 = bf16[64,2048]{1,0:T(8,128)(2,1)S(1)} collective-permute-done((bf16[64,2048]{1,0:T(8,128)(2,1)S(1)}, bf16[64,2048]{1,0:T(8,128)(2,1)S(1)}, u32[]{:S(2)}, u32[]{:S(2)}) %collective-permute-start.16) | collective-permute-done | bytes 262176 | tf_op jit(solution)/shard_map/ppermute | solution.py:39
  142.2 11.3 %collective-permute-done.17 = bf16[128,2048]{1,0:T(8,128)(2,1)S(1)} collective-permute-done((bf16[128,2048]{1,0:T(8,128)(2,1)S(1)}, bf16[128,2048]{1,0:T(8,128)(2,1)S(1)}, u32[]{:S(2)}, u32[]{:S(2)}) %collective-permute-start.17) | collective-permute-done | bytes 524320 | tf_op jit(solution)/shard_map/ppermute | solution.py:39
  158.5 7.0 %all-to-all-start.1 = ((bf16[16,40,2048]{2,1,0:T(8,128)(2,1)}), bf16[16,40,2048]{2,1,0:T(8,128)(2,1)S(1)}, u32[]{:S(2)}, u32[]{:S(2)}) async-start(bf16[16,40,2048]{2,1,0:T(8,128)(2,1)} %bitcast.253), calls=%async_computation.1 | async-start | bytes 5242880 | tf_op jit(solution)/shard_map/all_to_all | solution.py:548
  172.2 30.3 %all-to-all-done.1.refs_1_ = bf16[16,40,2048]{2,1,0:T(8,128)(2,1)S(1)} async-done(((bf16[16,40,2048]{2,1,0:T(8,128)(2,1)}), bf16[16,40,2048]{2,1,0:T(8,128)(2,1)S(1)}, u32[]{:S(2)}, u32[]{:S(2)}) %all-to-all-start.1) | async-done | bytes 2621472 | tf_op jit(solution)/shard_map/all_to_all | solution.py:548
  208.8 6.2 %convolution_convert_fusion.2 = bf16[16,40,2048]{2,1,0:T(8,128)(2,1)} fusion(bf16[16,128,2048]{2,1,0:T(8,128)(2,1)} %all-gather.4.cloned.1.call-done, pred[2,16,40,128]{3,2,1,0:T(8,128)(4,1)S(1)} %iota_compare_fusion.2), kind=kOutput, calls=%fused_computation.4 | convolution fusion | flops 336855040 | bytes 11091968 | tf_op jit(solution)/shard_map/sct,std->scd/dot_general | solution.py:34
  215.0 16.9 %expert_rows.2 = (bf16[640,2176]{1,0:T(8,128)(2,1)}, bf16[640,768]{1,0:T(8,128)(2,1)S(1)}, bf16[640,768]{1,0:T(8,128)(2,1)S(1)}, bf16[640,768]{1,0:T(8,128)(2,1)S(1)}) custom-call(bf16[640,2048]{1,0:T(8,128)(2,1)S(1)} %bitcast.229, bf16[640,2048]{1,0:T(8,128)(2,1)} %bitcast.255, bf16[4,2048,768]{2,1,0:T(8,128)(2,1)} %all-gather.6.cloned.1.call-done.w_in, ...), custom_call_target="tpu_custom_call" | custom-call | flops 10737418240 | bytes 20971520 | tf_op jit(solution)/shard_map/expert_rows/pallas_call | solution.py:264
  234.8 11.9 %all-to-all-done.2.refs_1_ = bf16[16,40,2176]{2,1,0:T(8,128)(2,1)} async-done(((bf16[16,40,2176]{2,1,0:T(8,128)(2,1)}), bf16[16,40,2176]{2,1,0:T(8,128)(2,1)}, u32[]{:S(2)}, u32[]{:S(2)}) %all-to-all-start.2) | async-done | bytes 2785312 | tf_op jit(solution)/shard_map/all_to_all | solution.py:548
  246.7 5.0 all-to-all-start.3
  251.6 4.6 convolution_convert_fusion
  256.3 18.5 %expert_rows.3 = (bf16[640,2176]{1,0:T(8,128)(2,1)}, bf16[640,768]{1,0:T(8,128)(2,1)S(1)}, bf16[640,768]{1,0:T(8,128)(2,1)S(1)}, bf16[640,768]{1,0:T(8,128)(2,1)S(1)}) custom-call(bf16[640,2176]{1,0:T(8,128)(2,1)} %bitcast.53.xs_in.refs_6_, bf16[640,2048]{1,0:T(8,128)(2,1)S(1)} %bitcast.231, bf16[4,2048,768]{2,1,0:T(8,128)(2,1)} %all-gather.6.cloned.1.call-done.w_in, ...), custom_call_target="tpu_custom_call" | custom-call | flops 10737418240 | bytes 20971520 | tf_op jit(solution)/shard_map/expert_rows/pallas_call | solution.py:264
  277.7 12.1 %all-to-all-done.3.refs_13_.refs_1_ = bf16[16,40,2176]{2,1,0:T(8,128)(2,1)} async-done(((bf16[16,40,2176]{2,1,0:T(8,128)(2,1)}), bf16[16,40,2176]{2,1,0:T(8,128)(2,1)}, u32[]{:S(2)}, u32[]{:S(2)}) %all-to-all-start.3) | async-done | bytes 2785312 | tf_op jit(solution)/shard_map/all_to_all | solution.py:548
  296.8 31.7 %weight_grads.1 = (bf16[2,2048,768]{2,1,0:T(8,128)(2,1)}, bf16[2,2048,768]{2,1,0:T(8,128)(2,1)}, bf16[2,768,2048]{2,1,0:T(8,128)(2,1)}, bf16[640,2048]{1,0:T(8,128)(2,1)}, bf16[640,2048]{1,0:T(8,128)(2,1)}) custom-call(bf16[640,2048]{1,0:T(8,128)(2,1)} %bitcast.228, bf16[640,2048]{1,0:T(8,128)(2,1)} %bitcast.256, bf16[640,768]{1,0:T(8,128)(2,1)} %copy-done.39, ...), custom_call_target="tpu_custom_call" | custom-call | flops 17179869184 | bytes 50331648 | tf_op jit(solution)/shard_map/weight_grads/pallas_call | solution.py:300
  328.5 5.2 all-to-all-done.5.refs_0_.refs_3_
  353.2 23.8 %all-to-all-done.4.refs_2_ = bf16[16,40,2048]{2,1,0:T(8,128)(2,1)} async-done(((bf16[16,40,2048]{2,1,0:T(8,128)(2,1)}), bf16[16,40,2048]{2,1,0:T(8,128)(2,1)}, u32[]{:S(2)}, u32[]{:S(2)}) %all-to-all-start.4) | async-done | bytes 2621472 | tf_op jit(solution)/shard_map/all_to_all | solution.py:548
  378.6 4.6 all-to-all-start.6
  387.3 6.1 collective-permute-done.23.rest_4_
  398.6 7.2 %out_back.1 = (bf16[1024,512]{1,0:T(8,128)(2,1)S(1)}, bf16[512,2048]{1,0:T(8,128)(2,1)S(1)}) custom-call(s32[4]{0:T(128)S(1)} %copy-done.28, bf16[512,2048]{1,0:T(8,128)(2,1)S(1)} %copy-done.30, bf16[1024,512]{1,0:T(8,128)(2,1)S(1)} %copy-done.33, bf16[128,2048]{1,0:T(8,128)(2,1)S(1)} %fusion.70.rest_0_, ...), custom_call_target="tpu_custom_call" | custom-call | flops 5368709120 | bytes 12582912 | tf_op jit(solution)/shard_map/out_back/pallas_call | solution.py:330
  408.2 11.3 %all-to-all-done.6.refs_1_ = bf16[16,40,2048]{2,1,0:T(8,128)(2,1)} async-done(((bf16[16,40,2048]{2,1,0:T(8,128)(2,1)}), bf16[16,40,2048]{2,1,0:T(8,128)(2,1)}, u32[]{:S(2)}, u32[]{:S(2)}) %all-to-all-start.6) | async-done | bytes 2621472 | tf_op jit(solution)/shard_map/all_to_all | solution.py:548
  419.5 5.0 all-to-all-start.7
  427.8 13.2 %attention_backward.1 = (bf16[1024,512]{1,0:T(8,128)(2,1)S(1)}, f32[1024,256]{1,0:T(8,128)S(1)}, f32[1,128]{1,0:T(1,128)S(1)}) custom-call(bf16[1024,512]{1,0:T(8,128)(2,1)S(1)} %copy-done.35, bf16[1024,512]{1,0:T(8,128)(2,1)} %get-tuple-element.81.a_b, bf16[4,1024,128]{2,1,0:T(8,128)(2,1)} %get-tuple-element.84.q_b, bf16[1024,128]{1,0:T(8,128)(2,1)S(1)} %copy-done.44, ...), custom_call_target="tpu_custom_call" | custom-call | flops 10737418240 | bytes 12582912 | tf_op jit(solution)/shard_map/attention_backward/pallas_call | solution.py:378
  442.6 11.4 %all-to-all-done.7 = bf16[16,32,2048]{2,1,0:T(8,128)(2,1)} async-done(((bf16[16,32,2048]{2,1,0:T(8,128)(2,1)}), bf16[16,32,2048]{2,1,0:T(8,128)(2,1)}, u32[]{:S(2)}, u32[]{:S(2)}) %all-to-all-start.7) | async-done | bytes 2097184 | tf_op jit(solution)/shard_map/all_to_all | solution.py:548
  457.2 10.3 %projection_grads.1 = (bf16[16,128,768]{2,1,0:T(8,128)(2,1)}, bf16[1024,640]{1,0:T(8,128)(2,1)}, f32[2048,128]{1,0:T(8,128)S(1)}, f32[1,128]{1,0:T(1,128)S(1)}) custom-call(s32[4]{0:T(128)S(1)} %copy-done.28, bf16[1024,512]{1,0:T(8,128)(2,1)S(1)} %get-tuple-element.89.dq_raw, f32[1024,256]{1,0:T(8,128)S(1)} %get-tuple-element.90.own, ...), custom_call_target="tpu_custom_call" | custom-call | flops 3221225472 | bytes 16777216 | tf_op jit(solution)/shard_map/projection_grads/pallas_call | solution.py:423
  468.9 6.2 %input_grad.1 = (bf16[4,128,2048]{2,1,0:T(8,128)(2,1)S(1)}, bf16[4,128,2048]{2,1,0:T(8,128)(2,1)}) custom-call(s32[4]{0:T(128)S(1)} %copy-done.28, bf16[1024,640]{1,0:T(8,128)(2,1)S(1)} %copy-done.31, bf16[2048,768]{1,0:T(8,128)(2,1)S(1)} %bitcast.234), custom_call_target="tpu_custom_call" | custom-call | flops 3221225472 | bytes 8388608 | tf_op jit(solution)/shard_map/input_grad/pallas_call | solution.py:450
  479.4 4.5 all-to-all-start.8
  517.0 15.7 %all-to-all-done.8 = bf16[16,128,768]{2,1,0:T(8,128)(2,1)} async-done(((bf16[16,128,768]{2,1,0:T(8,128)(2,1)}), bf16[16,128,768]{2,1,0:T(8,128)(2,1)}, u32[]{:S(2)}, u32[]{:S(2)}) %all-to-all-start.8) | async-done | bytes 3145760 | tf_op jit(solution)/shard_map/all_to_all | solution.py:548
  569.9 7.5 %collective-permute-done.58.refs_9_ = bf16[4,4,16,1280]{3,2,1,0:T(8,128)(2,1)S(1)} collective-permute-done((bf16[4,4,16,1280]{3,2,1,0:T(8,128)(2,1)S(1)}, bf16[4,4,16,1280]{3,2,1,0:T(8,128)(2,1)S(1)}, u32[]{:S(2)}, u32[]{:S(2)}) %collective-permute-start.58) | collective-permute-done | bytes 655392 | tf_op jit(solution)/shard_map/ppermute | solution.py:39
  598.2 5.5 place_rows.1
  (473 shorter events, 230.9 us)
Async XLA Ops:
  7.2 201.5 %all-gather.4.cloned.1.call-start = ((), (), s32[]{:S(2)}) async-start(), calls=%async_computation.13 | async-start | bytes 8912896 | tf_op jit(solution)/shard_map/all_gather | solution.py:550
  11.6 43.5 %collective-permute-start.1 = (bf16[128,2176]{1,0:T(8,128)(2,1)}, bf16[128,2176]{1,0:T(8,128)(2,1)}, u32[]{:S(2)}, u32[]{:S(2)}) collective-permute-start(bf16[128,2176]{1,0:T(8,128)(2,1)} %fusion.32.rest_0_), channel_id=1, source_target_pairs={{0,96},{32,0},{64,32},{96,64},{1,97},{33,1},{65,33},{97,65},{2,98}... | collective-permute-start | bytes 1671176 | tf_op jit(solution)/shard_map/ppermute | solution.py:39
  15.8 39.4 %collective-permute-start.2 = (bf16[128,2176]{1,0:T(8,128)(2,1)}, bf16[128,2176]{1,0:T(8,128)(2,1)}, u32[]{:S(2)}, u32[]{:S(2)}) collective-permute-start(bf16[128,2176]{1,0:T(8,128)(2,1)} %fusion.32.rest_0_), channel_id=1, source_target_pairs={{0,32},{32,64},{64,96},{96,0},{1,33},{33,65},{65,97},{97,1},{2,34}... | collective-permute-start | bytes 1671176 | tf_op jit(solution)/shard_map/ppermute | solution.py:39
  21.5 26.6 %collective-permute-start.3 = (bf16[2,128,768]{2,1,0:T(8,128)(2,1)}, bf16[2,128,768]{2,1,0:T(8,128)(2,1)S(1)}, u32[]{:S(2)}, u32[]{:S(2)}) collective-permute-start(bf16[2,128,768]{2,1,0:T(8,128)(2,1)} %get-tuple-element.251), channel_id=1, source_target_pairs={{0,32},{32,64},{64,96},{96,0},{1,33},{33,65},{65,97},{97,1},{2,34}... | collective-permute-start | bytes 1179656 | tf_op jit(solution)/shard_map/ppermute | solution.py:39
  21.5 26.6 %collective-permute-start.4 = (bf16[2,128,768]{2,1,0:T(8,128)(2,1)}, bf16[2,128,768]{2,1,0:T(8,128)(2,1)S(1)}, u32[]{:S(2)}, u32[]{:S(2)}) collective-permute-start(bf16[2,128,768]{2,1,0:T(8,128)(2,1)} %get-tuple-element.250), channel_id=1, source_target_pairs={{0,64},{32,96},{64,0},{96,32},{1,65},{33,97},{65,1},{97,33},{2,66}... | collective-permute-start | bytes 1179656 | tf_op jit(solution)/shard_map/ppermute | solution.py:39
  26.2 21.9 %collective-permute-start.5 = (bf16[2,128,768]{2,1,0:T(8,128)(2,1)}, bf16[2,128,768]{2,1,0:T(8,128)(2,1)S(1)}, u32[]{:S(2)}, u32[]{:S(2)}) collective-permute-start(bf16[2,128,768]{2,1,0:T(8,128)(2,1)} %get-tuple-element.249), channel_id=1, source_target_pairs={{0,96},{32,0},{64,32},{96,64},{1,97},{33,1},{65,33},{97,65},{2,98}... | collective-permute-start | bytes 1179656 | tf_op jit(solution)/shard_map/ppermute | solution.py:39
  27.7 26.7 %all-to-all-start = ((f32[16,2,40]{2,1,0:T(2,128)}), f32[16,2,40]{2,1,0:T(2,128)S(1)}, u32[]{:S(2)}, u32[]{:S(2)}) async-start(f32[16,2,40]{2,1,0:T(2,128)} %bitcast.226), calls=%async_computation | async-start | bytes 32768 | tf_op jit(solution)/shard_map/all_to_all | solution.py:548
  34.8 180.2 %all-gather.8.cloned.1.call-start = ((), (), s32[]{:S(2)}) async-start(), calls=%async_computation.15 | async-start | bytes 7077888 | tf_op jit(solution)/shard_map/all_gather | solution.py:590
  68.3 146.6 %all-gather.6.cloned.1.call-start = ((), (), s32[]{:S(2)}) async-start(), calls=%async_computation.14 | async-start | bytes 14155776 | tf_op jit(solution)/shard_map/all_gather | solution.py:589
  70.5 27.9 %collective-permute-start.13 = (bf16[8,128,384]{2,1,0:T(8,128)(2,1)S(1)}, bf16[8,128,384]{2,1,0:T(8,128)(2,1)S(1)}, u32[]{:S(2)}, u32[]{:S(2)}) collective-permute-start(bf16[8,128,384]{2,1,0:T(8,128)(2,1)S(1)} %get-tuple-element.245), channel_id=1, source_target_pairs={{0,1},{1,0},{2,3},{3,2},{4,5},{5,4},{6,7},{7,6},{8,9},{9,8},{10,11... | collective-permute-start | bytes 2359304 | tf_op jit(solution)/shard_map/ppermute | solution.py:584
  72.1 26.3 %collective-permute-start.14 = (bf16[8,128,384]{2,1,0:T(8,128)(2,1)S(1)}, bf16[8,128,384]{2,1,0:T(8,128)(2,1)S(1)}, u32[]{:S(2)}, u32[]{:S(2)}) collective-permute-start(bf16[8,128,384]{2,1,0:T(8,128)(2,1)S(1)} %get-tuple-element.244), channel_id=1, source_target_pairs={{0,4},{4,0},{8,12},{12,8},{1,5},{5,1},{9,13},{13,9},{2,6},{6,2},{1... | collective-permute-start | bytes 2359304 | tf_op jit(solution)/shard_map/ppermute | solution.py:584
  158.5 44.0 %all-to-all-start.1 = ((bf16[16,40,2048]{2,1,0:T(8,128)(2,1)}), bf16[16,40,2048]{2,1,0:T(8,128)(2,1)S(1)}, u32[]{:S(2)}, u32[]{:S(2)}) async-start(bf16[16,40,2048]{2,1,0:T(8,128)(2,1)} %bitcast.253), calls=%async_computation.1 | async-start | bytes 5242880 | tf_op jit(solution)/shard_map/all_to_all | solution.py:548
  204.0 42.7 %all-to-all-start.2 = ((bf16[16,40,2176]{2,1,0:T(8,128)(2,1)}), bf16[16,40,2176]{2,1,0:T(8,128)(2,1)}, u32[]{:S(2)}, u32[]{:S(2)}) async-start(bf16[16,40,2176]{2,1,0:T(8,128)(2,1)} %after.13), calls=%async_computation.2 | async-start | bytes 5570560 | tf_op jit(solution)/shard_map/all_to_all | solution.py:548
  246.7 43.1 %all-to-all-start.3 = ((bf16[16,40,2176]{2,1,0:T(8,128)(2,1)}), bf16[16,40,2176]{2,1,0:T(8,128)(2,1)}, u32[]{:S(2)}, u32[]{:S(2)}) async-start(bf16[16,40,2176]{2,1,0:T(8,128)(2,1)} %after.14), calls=%async_computation.3 | async-start | bytes 5570560 | tf_op jit(solution)/shard_map/all_to_all | solution.py:548
  289.8 43.9 %all-to-all-start.5 = ((bf16[16,40,2176]{2,1,0:T(8,128)(2,1)}), bf16[16,40,2176]{2,1,0:T(8,128)(2,1)S(1)}, u32[]{:S(2)}, u32[]{:S(2)}) async-start(bf16[16,40,2176]{2,1,0:T(8,128)(2,1)} %after.15), calls=%async_computation.5 | async-start | bytes 5570560 | tf_op jit(solution)/shard_map/all_to_all | solution.py:548
  293.6 295.8 %reduce-scatter.4.cloned.1.call-start = ((), (), s32[]{:S(2)}) async-start(), calls=%async_computation.16 | async-start | bytes 7077888 | tf_op jit(solution)/shard_map/reduce_scatter | solution.py:655
  335.3 255.4 %reduce-scatter.6.cloned.1.call-start = ((), (), s32[]{:S(2)}) async-start(), calls=%async_computation.17 | async-start | bytes 7077888 | tf_op jit(solution)/shard_map/reduce_scatter | solution.py:655
  337.4 39.6 %all-to-all-start.4 = ((bf16[16,40,2048]{2,1,0:T(8,128)(2,1)}), bf16[16,40,2048]{2,1,0:T(8,128)(2,1)}, u32[]{:S(2)}, u32[]{:S(2)}) async-start(bf16[16,40,2048]{2,1,0:T(8,128)(2,1)} %bitcast.57), calls=%async_computation.4 | async-start | bytes 5242880 | tf_op jit(solution)/shard_map/all_to_all | solution.py:548
  350.4 26.6 %collective-permute-start.20 = (bf16[128,2048]{1,0:T(8,128)(2,1)S(1)}, bf16[128,2048]{1,0:T(8,128)(2,1)S(1)}, u32[]{:S(2)}, u32[]{:S(2)}) collective-permute-start(bf16[128,2048]{1,0:T(8,128)(2,1)S(1)} %fusion.70.rest_0_), channel_id=1, source_target_pairs={{0,96},{32,0},{64,32},{96,64},{1,97},{33,1},{65,33},{97,65},{2,98}... | collective-permute-start | bytes 1572872 | tf_op jit(solution)/shard_map/ppermute | solution.py:39
  353.2 23.8 %collective-permute-start.21 = (bf16[128,2048]{1,0:T(8,128)(2,1)S(1)}, bf16[128,2048]{1,0:T(8,128)(2,1)S(1)}, u32[]{:S(2)}, u32[]{:S(2)}) collective-permute-start(bf16[128,2048]{1,0:T(8,128)(2,1)S(1)} %fusion.70.rest_0_), channel_id=1, source_target_pairs={{0,32},{32,64},{64,96},{96,0},{1,33},{33,65},{65,97},{97,1},{2,34}... | collective-permute-start | bytes 1572872 | tf_op jit(solution)/shard_map/ppermute | solution.py:39
  378.6 40.8 %all-to-all-start.6 = ((bf16[16,40,2048]{2,1,0:T(8,128)(2,1)}), bf16[16,40,2048]{2,1,0:T(8,128)(2,1)}, u32[]{:S(2)}, u32[]{:S(2)}) async-start(bf16[16,40,2048]{2,1,0:T(8,128)(2,1)} %after.18), calls=%async_computation.6 | async-start | bytes 5242880 | tf_op jit(solution)/shard_map/all_to_all | solution.py:548
  383.3 209.2 %reduce-scatter.8.cloned.1.call-start = ((), (), s32[]{:S(2)}) async-start(), calls=%async_computation.18 | async-start | bytes 7077888 | tf_op jit(solution)/shard_map/reduce_scatter | solution.py:655
  419.5 34.6 %all-to-all-start.7 = ((bf16[16,32,2048]{2,1,0:T(8,128)(2,1)}), bf16[16,32,2048]{2,1,0:T(8,128)(2,1)}, u32[]{:S(2)}, u32[]{:S(2)}) async-start(bf16[16,32,2048]{2,1,0:T(8,128)(2,1)} %after.19), calls=%async_computation.7 | async-start | bytes 4194304 | tf_op jit(solution)/shard_map/all_to_all | solution.py:548
  479.4 53.2 %all-to-all-start.8 = ((bf16[16,128,768]{2,1,0:T(8,128)(2,1)}), bf16[16,128,768]{2,1,0:T(8,128)(2,1)}, u32[]{:S(2)}, u32[]{:S(2)}) async-start(bf16[16,128,768]{2,1,0:T(8,128)(2,1)} %get-tuple-element.100), calls=%async_computation.8 | async-start | bytes 6291456 | tf_op jit(solution)/shard_map/all_to_all | solution.py:548
  483.9 23.5 %collective-permute-start.36 = (f32[34,128]{1,0:T(8,128)S(1)}, f32[34,128]{1,0:T(8,128)S(1)}, u32[]{:S(2)}, u32[]{:S(2)}) collective-permute-start(f32[34,128]{1,0:T(8,128)S(1)} %fusion.69), channel_id=1, source_target_pairs={{0,64},{32,96},{64,0},{96,32},{1,65},{33,97},{65,1},{97,33},{2,66}... | collective-permute-start | bytes 52232 | tf_op jit(solution)/shard_map/ppermute | solution.py:39
  485.4 22.0 %collective-permute-start.37 = (f32[34,128]{1,0:T(8,128)S(1)}, f32[34,128]{1,0:T(8,128)S(1)}, u32[]{:S(2)}, u32[]{:S(2)}) collective-permute-start(f32[34,128]{1,0:T(8,128)S(1)} %fusion.69), channel_id=1, source_target_pairs={{0,32},{32,64},{64,96},{96,0},{1,33},{33,65},{65,97},{97,1},{2,34}... | collective-permute-start | bytes 52232 | tf_op jit(solution)/shard_map/ppermute | solution.py:39
  487.6 19.9 %collective-permute-start.38 = (f32[34,128]{1,0:T(8,128)S(1)}, f32[34,128]{1,0:T(8,128)S(1)}, u32[]{:S(2)}, u32[]{:S(2)}) collective-permute-start(f32[34,128]{1,0:T(8,128)S(1)} %fusion.69), channel_id=1, source_target_pairs={{0,96},{32,0},{64,32},{96,64},{1,97},{33,1},{65,33},{97,65},{2,98}... | collective-permute-start | bytes 52232 | tf_op jit(solution)/shard_map/ppermute | solution.py:39
  507.5 32.3 %collective-permute-start.39 = (f32[34,128]{1,0:T(8,128)S(1)}, f32[34,128]{1,0:T(8,128)S(1)}, u32[]{:S(2)}, u32[]{:S(2)}) collective-permute-start(f32[34,128]{1,0:T(8,128)S(1)} %add_add_fusion.2), channel_id=1, source_target_pairs={{0,8},{4,12},{8,0},{12,4},{1,9},{5,13},{9,1},{13,5},{2,10},{6,14},... | collective-permute-start | bytes 52232 | tf_op jit(solution)/shard_map/ppermute | solution.py:39
  510.6 29.3 %collective-permute-start.40 = (f32[34,128]{1,0:T(8,128)S(1)}, f32[34,128]{1,0:T(8,128)S(1)}, u32[]{:S(2)}, u32[]{:S(2)}) collective-permute-start(f32[34,128]{1,0:T(8,128)S(1)} %add_add_fusion.2), channel_id=1, source_target_pairs={{0,4},{4,8},{8,12},{12,0},{1,5},{5,9},{9,13},{13,1},{2,6},{6,10},{... | collective-permute-start | bytes 52232 | tf_op jit(solution)/shard_map/ppermute | solution.py:39
  511.4 28.5 %collective-permute-start.41 = (f32[34,128]{1,0:T(8,128)S(1)}, f32[34,128]{1,0:T(8,128)S(1)}, u32[]{:S(2)}, u32[]{:S(2)}) collective-permute-start(f32[34,128]{1,0:T(8,128)S(1)} %add_add_fusion.2), channel_id=1, source_target_pairs={{0,12},{4,0},{8,4},{12,8},{1,13},{5,1},{9,5},{13,9},{2,14},{6,2},{... | collective-permute-start | bytes 52232 | tf_op jit(solution)/shard_map/ppermute | solution.py:39
  561.3 16.9 %collective-permute-start.57 = (bf16[4,4,16,1280]{3,2,1,0:T(8,128)(2,1)S(1)}, bf16[4,4,16,1280]{3,2,1,0:T(8,128)(2,1)S(1)}, u32[]{:S(2)}, u32[]{:S(2)}) collective-permute-start(bf16[4,4,16,1280]{3,2,1,0:T(8,128)(2,1)S(1)} %pad_maximum_fusion.5.refs_5_), channel_id=1, source_target_pairs={{0,3},{1,0},{2,1},{3,2},{4,7},{5,4},{6,5},{7,6},{8,11},{9,8},{10,9... | collective-permute-start | bytes 1966088 | tf_op jit(solution)/shard_map/ppermute | solution.py:39
  565.5 17.5 %collective-permute-start.49 = (bf16[4,4,16,1280]{3,2,1,0:T(8,128)(2,1)S(1)}, bf16[4,4,16,1280]{3,2,1,0:T(8,128)(2,1)S(1)}, u32[]{:S(2)}, u32[]{:S(2)}) collective-permute-start(bf16[4,4,16,1280]{3,2,1,0:T(8,128)(2,1)S(1)} %pad_maximum_fusion.4.refs_0_), channel_id=1, source_target_pairs={{0,12},{4,0},{8,4},{12,8},{1,13},{5,1},{9,5},{13,9},{2,14},{6,2},{... | collective-permute-start | bytes 1966088 | tf_op jit(solution)/shard_map/ppermute | solution.py:39
  (138 other events, 1307.8 us)
Sparse Core Ops, SparseCore 0:
  10.2 79.7 all-gather.3
  91.6 47.2 all-gather.7
  141.2 66.8 all-gather.5
  335.4 51.4 reduce-scatter.3
  389.2 42.5 reduce-scatter.5
  434.0 42.5 reduce-scatter.7

commit v3 on v2

--- a/solution.py
+++ b/solution.py
@@ -77,20 +77,30 @@
     return v, up, shift(down[:half], axis, 1), shift(up[half:], axis, -1), down
 
 
-def gather_plane(left, right):
-    def stacked(parts):
-        a, b, low, high, d = parts
-        return jnp.stack([a, b, jnp.concatenate([low, high]), d])
-
-    left, right = gather_ring(left, X), gather_ring(right, Y)
-    return gather_ring(stacked(left), Y), gather_ring(stacked(right), X)
-
-
-def sum_all(v):
-    v = v + shift(v, C, 1)
-    for axis in (Z, Y, X):
-        v = (v + shift(v, axis, 2)) + (shift(v, axis, 1) + shift(v, axis, 3))
-    return v
+def scatter_ring(parts, axis):
+    own, one, low, high, three = parts
+    k = low.shape[0]
+    down, up = shift(low, axis, 1), shift(high, axis, -1)
+    first = down
+
+    def plus(a, b):
+        return (a.astype(f32) + b.astype(f32)).astype(bf16)
+
+    one = jnp.concatenate([plus(one[:k], down), one[k:]])
+    three = jnp.concatenate([three[:k], plus(three[k:], up)])
+    down, up = shift(one, axis, 1), shift(three, axis, -1)
+    return own.astype(f32) + down.astype(f32) + up.astype(f32), first
+
+
+def scatter_plane(left, right):
+    def halves(v):
+        v = v.astype(bf16)
+        k = v.shape[1] // 2
+        return v[0], v[1], v[2, :k], v[2, k:], v[3]
+
+    left, first = scatter_ring(left, Y)
+    right, _ = scatter_ring(right, X)
+    return scatter_ring(halves(left), X)[0], scatter_ring(halves(right), Y)[0], first
 
 
 def inv_rms(values):
@@ -133,15 +143,11 @@
 
 def load_weights(place, parts, w, sems):
     copies = []
-    width = w.shape[3] // 2
-    own, from_x, from_y = parts
     for k in range(8):
         source = lax.rem(place[0] + 4 - k % 4, 4) * 2 + lax.rem(place[1] + k // 4, 2)
-        for side, (at, other) in enumerate(((place[3], from_x), (place[2], from_y))):
-            cols = pl.ds(side * width, width)
-            for j, piece in enumerate((own.at[k, :, cols], other.at[k])):
-                into = w.at[source, lax.rem(at + j, 2), :, cols]
-                copies.append(pltpu.make_async_copy(piece, into, sems.at[4 * k + 2 * side + j]))
+        rows = pl.ds(pl.multiple_of(source * 256, 256), 256)
+        piece = parts[k].at[0] if k < 4 else parts[4].at[k - 4]
+        copies.append(pltpu.make_async_copy(piece, w.at[rows], sems.at[k]))
     for copy in copies:
         copy.start()
     return copies
@@ -149,7 +155,7 @@
 
 def attention_kernel(spec, place, w_out, q_gain, k_gain, cosine, sine, *rest):
     n = len(spec)
-    pieces, parts, rest = rest[:n], rest[n : n + 3], rest[n + 3 :]
+    pieces, parts, rest = rest[:n], rest[n : n + 5], rest[n + 5 :]
     w, h1, q_raw, k_raw, v_b, q_b, k_b, a_b, lse, keep, send, sems, w_sems = rest
     z, c = place[0], place[1]
     copies = load_weights(place, parts, w, w_sems)
@@ -159,7 +165,7 @@
     @pl.loop(0, 4)
     def _(i):
         rows = pl.ds(pl.multiple_of(i * 256, 256), 256)
-        t = mm(h1[rows, :MODEL_WIDTH], w[...].reshape(MODEL_WIDTH, 768))
+        t = mm(h1[rows, :MODEL_WIDTH], w[...])
         q_raw[rows] = t[:, :512]
         k_raw[rows] = t[:, 512:640]
         v_b[rows] = t[:, 640:].astype(bf16)
@@ -202,7 +208,7 @@
     spec = [(dz, dc, first, a.shape[0]) for a, dz, dc, first in pieces]
     seq = 1024
     shapes = [
-        ((8, 2, 128, 768), bf16),
+        ((MODEL_WIDTH, 768), bf16),
         ((seq, MODEL_WIDTH + 128), bf16),
         ((seq, 512), f32),
         ((seq, 128), f32),
@@ -217,9 +223,9 @@
     return pl.pallas_call(
         functools.partial(attention_kernel, spec),
         out_shape=[jax.ShapeDtypeStruct(*s) for s in shapes],
-        in_specs=[SM] + [VM] * 5 + [ANY] * (len(spec) + 3),
+        in_specs=[SM] + [VM] * 5 + [ANY] * (len(spec) + 5),
         out_specs=[VM] * len(shapes),
-        scratch_shapes=[pltpu.SemaphoreType.DMA((len(spec),)), pltpu.SemaphoreType.DMA((32,))],
+        scratch_shapes=[pltpu.SemaphoreType.DMA((len(spec),)), pltpu.SemaphoreType.DMA((8,))],
         compiler_params=pltpu.CompilerParams(vmem_limit_bytes=56 * MIB),
         cost_estimate=pl.CostEstimate(flops=9 << 30, bytes_accessed=28 << 20, transcendentals=3 << 20),
         name="attention_forward",
@@ -274,19 +280,21 @@
 
 
 def weight_grads_kernel(*refs):
-    rows, w_down, grads, ys = refs[:12], refs[12], refs[14:17], refs[17:19]
+    rows, w_down, grads, ys = refs[:12], refs[12], refs[14:17], refs[17]
     first = pl.program_id(0) == 0
     for e in range(2):
         xs, dys, hid, dg, du, gate = rows[6 * e : 6 * e + 6]
 
         @pl.when(first if e == 0 else jnp.logical_not(first))
-        def _(xs=xs, dys=dys, hid=hid, dg=dg, du=du, gate=gate, out=ys[e]):
+        def _(e=e, xs=xs, dys=dys, hid=hid, dg=dg, du=du, gate=gate):
             s = gate[:, 0:1]
 
             def scaled(v):
                 return (v[...].astype(f32) * s).astype(bf16)
 
-            out[...] = mm(hid[...], w_down[0]).astype(bf16)
+            y = mm(hid[...], w_down[0])
+            for o in range(16):
+                ys[o, CAP * e : CAP * e + CAP] = y[CAP * o : CAP * o + CAP].astype(bf16)
             grads[0][0] = mm(xs[:, :MODEL_WIDTH], scaled(dg), TN).astype(bf16)
             grads[1][0] = mm(xs[:, :MODEL_WIDTH], scaled(du), TN).astype(bf16)
             grads[2][0] = mm(scaled(hid), dys[...], TN).astype(bf16)
@@ -301,9 +309,9 @@
         weight_grads_kernel,
         grid=(2,),
         out_shape=[jax.ShapeDtypeStruct((2, *s), bf16) for s in sizes]
-        + [jax.ShapeDtypeStruct((640, MODEL_WIDTH), bf16)] * 2,
+        + [jax.ShapeDtypeStruct((16, 2 * CAP, MODEL_WIDTH), bf16)],
         in_specs=[VM] * 12 + [per_expert(768, MODEL_WIDTH), ANY],
-        out_specs=[per_expert(*s) for s in sizes] + [VM] * 2,
+        out_specs=[per_expert(*s) for s in sizes] + [VM],
         compiler_params=pltpu.CompilerParams(vmem_limit_bytes=60 * MIB),
         cost_estimate=pl.CostEstimate(flops=16 << 30, bytes_accessed=48 << 20, transcendentals=0),
         name="weight_grads",
@@ -321,12 +329,17 @@
         rows = pl.ds(pl.multiple_of(i * 256, 256), 256)
         dob[rows] = mm(da[rows], w_out[...], NT).astype(bf16)
 
-    shares[...] = mm(a_b[...], da[...], TN).astype(bf16)
+    for h in range(4):
+        grads = mm(a_b[:, 128 * h : 128 * h + 128], da[...], TN).astype(bf16)
+        for r in range(4):
+            for k in range(4):
+                block = grads[32 * r : 32 * r + 32, 512 * k : 512 * k + 512]
+                shares[4 * h + r, 32 * k : 32 * k + 32] = block
 
 
 def out_back(pieces, place, w_out, a_b):
     spec = [(dz, dc, first, a.shape[0]) for a, dz, dc, first in pieces]
-    shapes = [((1024, 512), bf16), ((512, MODEL_WIDTH), bf16)]
+    shapes = [((1024, 512), bf16), ((16, 128, 512), bf16)]
     return pl.pallas_call(
         functools.partial(out_back_kernel, spec),
         out_shape=[jax.ShapeDtypeStruct(*s) for s in shapes],
@@ -381,15 +394,15 @@
         in_specs=[VM] * 10,
         out_specs=[VM] * 3,
         compiler_params=pltpu.CompilerParams(vmem_limit_bytes=48 * MIB),
-        cost_estimate=pl.CostEstimate(flops=10 << 30, bytes_accessed=12 << 20, transcendentals=3 << 20),
+        cost_estimate=pl.CostEstimate(flops=10 << 30, bytes_accessed=12 << 20, transcendentals=0),
         name="attention_backward",
     )(dob, a_b, q_b, k_b, v_b, lse, q_raw, q_gain, cosine, sine)
 
 
 def grads_kernel(
-    place, dq_raw, own, other, k_raw, q_part, k_gain, cosine, sine, h1, w, aux, _,
-    shares, dqkv, along_out, k_part,
+    place, idx, dq_raw, own, other, k_raw, q_part, k_gain, cosine, sine, h1, w, aux, out_shares, _, *outs
 ):
+    left, right, (dqkv, along_out, k_part, shares) = outs[:5], outs[5:10], outs[10:]
     c = place[1]
     dqkv[:, :512] = dq_raw[...]
     total = jnp.zeros((1, HEAD_SIZE), f32)
@@ -413,25 +426,37 @@
         along = jnp.sum(part[:, :512] * w[shard, :512].astype(f32), axis=1, keepdims=True)
         along = along + jnp.sum(part[:, 512:] * last.astype(f32), axis=1, keepdims=True)
         along_out[shard] = jnp.broadcast_to(along, (256, 128))
-        part = jnp.concatenate([part.astype(bf16), aux[shard].astype(bf16)], axis=1)
-        for r in range(16):
-            shares[r, 16 * f : 16 * f + 16] = part[16 * r : 16 * r + 16]
-
-
-def projection_grads(place, dq_raw, own, other, k_raw, q_part, k_gain, cosine, sine, h1, w, aux, event):
-    shapes = [((16, 128, 768), bf16), ((1024, 640), bf16), ((MODEL_WIDTH, 128), f32), ((1, HEAD_SIZE), f32)]
-    return pl.pallas_call(
+        shares[f, :, :640] = part.astype(bf16)
+        shares[f, :, 640:] = aux[shard].astype(bf16)
+    for r in range(16):
+        dy, dx = divmod(r, 4)
+        rows = pl.ds(pl.multiple_of(idx[r] * 16, 16), 16)
+        a, ai = part_of(dy, dx)
+        b, bi = part_of(dx, dy)
+        for f in range(4):
+            left[a][ai, 16 * f : 16 * f + 16, :768] = shares[f, rows]
+            right[b][bi, 16 * f : 16 * f + 16, :768] = shares[f + 4, rows]
+        left[a][ai, :, 768:] = out_shares[idx[r], :64]
+        right[b][bi, :, 768:] = out_shares[idx[r], 64:]
+
+
+def projection_grads(place, idx, dq_raw, own, other, k_raw, q_part, k_gain, cosine, sine, h1, w, aux, out_shares, event):
+    shapes = [((n, 64, 1280), bf16) for n in [4, 4, 2, 2, 4] * 2]
+    shapes += [((1024, 640), bf16), ((MODEL_WIDTH, 128), f32), ((1, HEAD_SIZE), f32)]
+    outs = pl.pallas_call(
         grads_kernel,
         out_shape=[jax.ShapeDtypeStruct(*s) for s in shapes],
-        in_specs=[SM] + [VM] * 11 + [ANY],
-        out_specs=[VM] * 4,
-        compiler_params=pltpu.CompilerParams(vmem_limit_bytes=48 * MIB),
+        in_specs=[SM, SM] + [VM] * 12 + [ANY],
+        out_specs=[VM] * len(shapes),
+        scratch_shapes=[pltpu.VMEM((8, 256, 768), bf16)],
+        compiler_params=pltpu.CompilerParams(vmem_limit_bytes=52 * MIB),
         cost_estimate=pl.CostEstimate(flops=3 << 30, bytes_accessed=16 << 20, transcendentals=0),
         name="projection_grads",
-    )(place, dq_raw, own, other, k_raw, q_part, k_gain, cosine, sine, h1, w, aux, event)
-
-
-def input_grad_kernel(place, dqkv, w, keep, send, w_own):
+    )(place, idx, dq_raw, own, other, k_raw, q_part, k_gain, cosine, sine, h1, w, aux, out_shares, event)
+    return outs[:5], outs[5:10], *outs[10:]
+
+
+def input_grad_kernel(place, dqkv, w, _, keep, send, w_own):
     z, c = place[0], place[1]
     w_own[:, :512] = w[:, :512]
     w_own[:, 512:] = jnp.where(c == 0, w[:, 512:640], w[:, 640:])
@@ -446,53 +471,51 @@
         send[dz] = jnp.where(c == 0, second, first)
 
 
-def input_grad(place, dqkv, w):
+def input_grad(place, dqkv, w, event):
     return pl.pallas_call(
         input_grad_kernel,
         out_shape=[jax.ShapeDtypeStruct((4, 128, MODEL_WIDTH), bf16)] * 2,
-        in_specs=[SM, VM, VM],
+        in_specs=[SM, VM, VM, ANY],
         out_specs=[VM] * 2,
         scratch_shapes=[pltpu.VMEM((MODEL_WIDTH, 640), bf16)],
         compiler_params=pltpu.CompilerParams(vmem_limit_bytes=40 * MIB),
         cost_estimate=pl.CostEstimate(flops=3 << 30, bytes_accessed=8 << 20, transcendentals=0),
         name="input_grad",
-    )(place, dqkv, w)
+    )(place, dqkv, w, event)
 
 
 def part_of(outer, inner):
     return {0: (0, inner), 1: (1, inner), 2: (2 + inner // 2, inner % 2), 3: (4, inner)}[outer]
 
 
-def place_kernel(idx, *refs):
-    left, right, (query, key, value, aux, out) = refs[:5], refs[5:10], refs[-5:]
+def place_kernel(parts, *refs):
+    query, key, value, aux, gains, out = refs[-6:]
     for r in range(16):
-        dy, dx = divmod(r, 4)
-        rows = pl.ds(pl.multiple_of(idx[r] * 16, 16), 16)
-        a, ai = part_of(dy, dx)
-        b, bi = part_of(dx, dy)
+        rows = slice(16 * r, 16 * r + 16)
         total = jnp.zeros((16, 128), f32)
         for f in range(8):
-            block = (left[a][ai, f] if f < 4 else right[b][bi, f - 4]).astype(f32)
+            block = parts[r, f].astype(f32)
             query[rows, 512 * f : 512 * f + 512] = block[:, :512]
             to = key if f % 2 == 0 else value
             to[rows, 128 * (f // 2) : 128 * (f // 2) + 128] = block[:, 512:640]
             total = total + block[:, 640:768]
-            out_rows = pl.ds(pl.multiple_of(idx[r] * 32 + 16 * (f % 2), 16), 16)
-            out[out_rows, 512 * (f // 2) : 512 * (f // 2) + 512] = block[:, 768:]
+            gains[f] = block[:, 640:768] if r == 0 else gains[f] + block[:, 640:768]
+            first = 32 * r + 16 * (f % 2)
+            out[first : first + 16, 512 * (f // 2) : 512 * (f // 2) + 512] = block[:, 768:]
         aux[rows] = total
 
 
-def place_rows(idx, left, right, *events):
-    shapes = [(256, 4096), (256, 512), (256, 512), (256, 128), (512, MODEL_WIDTH)]
+def place_rows(parts, *events):
+    shapes = [(256, 4096), (256, 512), (256, 512), (256, 128), (8, 16, 128), (512, MODEL_WIDTH)]
     return pl.pallas_call(
         place_kernel,
         out_shape=[jax.ShapeDtypeStruct(s, f32) for s in shapes],
-        in_specs=[SM] + [VM] * 10 + [ANY] * len(events),
-        out_specs=[VM] * 5,
+        in_specs=[VM] + [ANY] * len(events),
+        out_specs=[VM] * 6,
         compiler_params=pltpu.CompilerParams(vmem_limit_bytes=40 * MIB),
         cost_estimate=pl.CostEstimate(flops=0, bytes_accessed=16 << 20, transcendentals=0),
         name="place_rows",
-    )(idx, *left, *right, *events)
+    )(parts, *events)
 
 
 def nothing(*refs):
@@ -549,10 +572,7 @@
 
     dy_all = lax.all_gather(dy_low, EXPERT, axis=0, tiled=False)
     tokens = jnp.arange(128, dtype=jnp.int32)
-    slot_token = jnp.max(jnp.where(picks, tokens, -1), axis=-1).reshape(2, 16, CAP).transpose(1, 0, 2)
-    slot_token = exchanged(slot_token.astype(f32)).astype(jnp.int32)
-    taken = (slot_token.transpose(1, 0, 2)[..., None] == tokens).astype(bf16)
-    dys = [es("sct,std->scd", taken[e], dy_all).astype(bf16).reshape(640, MODEL_WIDTH) for e in range(2)]
+    slot_token = jnp.max(jnp.where(picks, tokens, -1), axis=-1).reshape(2, 16, CAP)
     in_own = jnp.concatenate([w_gate, w_up])
     rows = w_query.shape[0]
 
@@ -560,45 +580,35 @@
         return jnp.repeat(w.reshape(rows, 4, 128), 2, axis=1) if n == 2 else w.reshape(rows, 8, 512)
 
     blocks = jnp.concatenate([per_head(w_query, 1), per_head(key_weight, 2), per_head(value_weight, 2)], axis=2)
-    blocks = blocks.reshape(2, 128, 8, 768)
-    halved = jnp.concatenate(
-        [
-            jnp.where(px % 2 == 0, blocks[0, :, :, :384], blocks[1, :, :, :384]),
-            jnp.where(py % 2 == 0, blocks[0, :, :, 384:], blocks[1, :, :, 384:]),
-        ],
-        axis=2,
-    ).transpose(1, 0, 2)
-    halved = halved.reshape(4, 2, 128, 768)
-    halved = jnp.where(core == 0, halved, halved[:, ::-1])
+    blocks = blocks.transpose(1, 0, 2).reshape(4, 2, rows, 768)
+    blocks = jnp.where(core == 0, blocks, blocks[:, ::-1])
     place_z = lax.axis_index(Z)
 
     def meant_for(ahead):
-        return lax.dynamic_index_in_dim(halved, (place_z + ahead) % 4, 0, keepdims=False)
-
-    arrived = [shift(meant_for(d), Z, d) for d in range(1, 4)]
-    h1_pieces = gather_fsdp(h1, lambda up, down: after([up, down], *arrived, slot_token, cosine, signed, in_own))
-    arrived = jnp.stack([meant_for(0)] + arrived, axis=1)
-    arrived = jnp.concatenate([arrived[0], shift(arrived[1], C, 1)])
-    swap = [(0, 1), (1, 0), (2, 3), (3, 2)]
-    w_parts = [
-        arrived, lax.ppermute(arrived[:, :, :384], X, swap), lax.ppermute(arrived[:, :, 384:], Y, swap)
-    ]
+        return lax.dynamic_index_in_dim(blocks, (place_z + ahead) % 4, 0, keepdims=False)
+
+    w_parts = [meant_for(0)] + [shift(meant_for(d), Z, d) for d in range(1, 4)]
+    h1_pieces = gather_fsdp(h1, lambda up, down: after([up, down], cosine, signed, in_own, *w_parts[1:]))
+    from_other = shift(jnp.stack([v[1] for v in w_parts]), C, 1)
     in_own, down_own = after(
-        [in_own, w_down], arrived, h1_pieces[4][0], h1_pieces[5][0]
+        [in_own, w_down], *w_parts[1:], h1_pieces[4][0], h1_pieces[5][0]
     )
     in_all = lax.all_gather(in_own, FSDP, axis=1, tiled=True)
     down_all = lax.all_gather(down_own, FSDP, axis=1, tiled=True)
     w, h1_all, q_raw, k_raw, v_b, q_b, k_b, a_b, lse, keep, send = attention_forward(
-        h1_pieces, w_parts, zc, w_out, query_gain[None], key_gain[None], cosine, signed
+        h1_pieces, [*w_parts, from_other], zc, w_out, query_gain[None], key_gain[None], cosine, signed
     )
     router = h1_all[:, MODEL_WIDTH : MODEL_WIDTH + 64].reshape(MODEL_WIDTH, EXPERTS)
-    w = w.reshape(MODEL_WIDTH, 768)
     attn = scatter_fsdp(keep, send)
     resid_two = residual + attn
     scale_two = inv_rms(resid_two)
     normed_two = resid_two * scale_two
     h2 = (normed_two * mlp_gain).astype(bf16)
-    xs_first = exchanged(sent(0, h2))
+    beside = jnp.pad(jnp.stack([slot_token[0], slot_token[1]], axis=-1).astype(bf16), ((0, 0), (0, 0), (0, 126)))
+    xs_first = exchanged(jnp.concatenate([sent(0, h2), beside], axis=-1))
+    slot_token = xs_first[:, :, MODEL_WIDTH : MODEL_WIDTH + 2].astype(jnp.int32)
+    taken = (slot_token[..., None] == tokens).astype(bf16)
+    dys = [es("sct,std->scd", taken[:, :, e], dy_all).astype(bf16).reshape(640, MODEL_WIDTH) for e in range(2)]
     logits = jnp.where(chosen, dot(h2, router), -1e30)
     powers = jnp.where(chosen, jnp.exp(logits - jnp.max(logits, axis=-1, keepdims=True)), 0.0)
     gates = powers / jnp.sum(powers, axis=-1, keepdims=True)
@@ -612,7 +622,7 @@
     second = jnp.concatenate([sent(1, h2), beside], axis=-1)
     (second,) = after([second], xs_first)
     xs_second = exchanged(second)
-    xs = [xs_first.reshape(640, MODEL_WIDTH), xs_second.reshape(640, MODEL_WIDTH + 128)]
+    xs = [v.reshape(640, MODEL_WIDTH + 128) for v in (xs_first, xs_second)]
     back_first, *kept_first = expert_rows(0, xs[0], dys[0], in_all, down_all)
     wide = (16, CAP, MODEL_WIDTH + 128)
     (back_first,) = after([back_first.reshape(wide)], xs_second)
@@ -630,60 +640,60 @@
     kept = [
         (xs[e], dys[e], *kept, slot_gate[e]) for e, kept in enumerate((kept_first, kept_second))
     ]
-    grad_gate, grad_up, grad_down, *ys = weight_grads([*kept[0], *kept[1]], down_all, from_first)
-    grad_gate, grad_up, grad_down = after([grad_gate, grad_up, grad_down], from_second)
-    (from_second,) = after([from_second], ys[0])
+    grad_gate, grad_up, grad_down, ys = weight_grads([*kept[0], *kept[1]], down_all, from_first)
+    (from_second,) = after([from_second], ys)
     backs = [from_first, from_second]
     dh_sum = combined(backs)
     dgate = [v.reshape(640, -1)[:, MODEL_WIDTH : MODEL_WIDTH + 2].astype(f32).sum(axis=1) for v in backs]
     dgate = jnp.stack(dgate).reshape(2, 16, CAP, 1)
     dgate = jnp.sum(jnp.where(picks.reshape(2, 16, CAP, 128), dgate, 0.0), axis=2)
     dgate = dgate.transpose(2, 1, 0).reshape(128, EXPERTS)
+    expert_grads = after([grad_gate, grad_up, grad_down], from_second)
     dl = (gates * (dgate - jnp.sum(gates * dgate, axis=-1, keepdims=True))).astype(bf16)
     dh2 = es("te,de->td", dl, router) + dh_sum
     dx2 = upstream + norm_back(dh2 * mlp_gain, normed_two, scale_two)
     da = dx2.astype(bf16)
-    y_first, y_second = (v.reshape(16, CAP, MODEL_WIDTH) for v in ys)
-    y_first = exchanged(y_first)
-    da_pieces = gather_fsdp(da, lambda up, down: after([up, down], y_first))
-    (y_second,) = after([y_second], da_pieces[2][0])
-    y_second = exchanged(y_second)
-    output = (resid_two + combined([y_first, y_second])).astype(bf16)
+    da_pieces = gather_fsdp(da)
+    (ys,) = after([ys], from_second)
+    ys = exchanged(ys).reshape(1280, MODEL_WIDTH)
+    by_owner = weighted.reshape(2, 16, CAP, 128).transpose(1, 0, 2, 3).reshape(1280, 128)
+    output = (resid_two + es("rt,rd->td", by_owner, ys)).astype(bf16)
     aux = jnp.pad(es("td,te->de", h2, dl), ((0, 0), (0, 128 - EXPERTS)))
     grad_mlp_gain = jnp.sum(dh2 * normed_two, axis=0)
     def scattered(v):
         return lax.psum_scatter(v, FSDP, scatter_dimension=1, tiled=True)
 
-    def summed(v):
-        return jnp.sum(exchanged(v).astype(f32), axis=0).astype(bf16)
-
-    grad_gate, grad_up, grad_down = scattered(grad_gate), scattered(grad_up), scattered(grad_down)
+    grad_gate, grad_up, grad_down = (scattered(v) for v in expert_grads)
     dob, out_shares = out_back(da_pieces, zc, w_out, a_b)
-    (out_shares,) = after([out_shares.reshape(16, 32, MODEL_WIDTH)], y_second)
-    grad_out = summed(out_shares)
     dq_raw, dkv, q_part = attention_backward(
         dob, a_b, q_b, k_b, v_b, lse, q_raw, query_gain[None], cosine, signed
     )
-    shares, dqkv, along, k_part = projection_grads(
-        zc, dq_raw, dkv, shift(dkv, C, 1), k_raw, q_part, key_gain[None], cosine, signed, h1_all, w, aux,
-        grad_out,
-    )
-    keep, send = input_grad(zc, dqkv, w)
+    left, right, dqkv, along, k_part = projection_grads(
+        zc, idx, dq_raw, dkv, shift(dkv, C, 1), k_raw, q_part, key_gain[None], cosine, signed, h1_all, w, aux,
+        out_shares, ys,
+    )
+    left, right, first = scatter_plane(left, right)
+    keep, send = input_grad(zc, dqkv, w, first)
     dh1 = scatter_fsdp(keep, send)
     gains = jnp.concatenate([along[:, 0], grad_mlp_gain, q_part[0], k_part[0]]).reshape(34, 128)
-    gains = sum_all(gains).reshape(-1)
-    (shares,) = after([summed(shares).reshape(8, 16, 768)], dh1)
-    parted = lax.all_to_all(shares, FSDP, 0, 0, tiled=True)
-    grad_out = grad_out.reshape(2, 16, 4, 512).transpose(2, 0, 1, 3).reshape(8, 16, 512)
-    parted = jnp.concatenate([parted, grad_out], axis=2)
+    (gains,) = after([gains], first)
+    gains = gains + shift(gains, C, 1)
+    gains = (gains + shift(gains, Z, 2)) + (shift(gains, Z, 1) + shift(gains, Z, 3))
+    high = gains.astype(bf16)
+    gains = jnp.stack([high, (gains - high.astype(f32)).astype(bf16)]).reshape(8, 16, 68)
+    gains = jnp.pad(gains, ((0, 0), (0, 0), (0, 28)))
+    shares = jnp.concatenate([left, right]).astype(bf16)
+    parted = lax.all_to_all(shares[:, :768].reshape(8, 16, 768), FSDP, 0, 0, tiled=True)
+    expert_grads = [v.astype(f32) for v in (grad_gate, grad_up, grad_down)]
+    parted = jnp.concatenate([parted[:, :, : 640 + EXPERTS], gains, shares[:, 768:].reshape(8, 16, 512)], axis=2)
     grad_input = dx2 + norm_back(dh1 * attn_gain, normed_one, scale_one)
-    expert_grads = [v.astype(f32) for v in (grad_gate, grad_up, grad_down)]
-    grad_query, grad_key, grad_value, aux, grad_out = place_rows(
-        idx, *gather_plane(parted[:4], parted[4:]), gains, *expert_grads
-    )
+    grad_input = grad_input.astype(bf16)
+    parted = lax.all_gather(parted, EXPERT, axis=0, tiled=False)
+    grad_query, grad_key, grad_value, aux, gains, grad_out = place_rows(parted, grad_input, *expert_grads)
+    gains = (gains[:4] + gains[4:])[:, :, EXPERTS : EXPERTS + 68].reshape(-1)
     return (
         output[None],
-        grad_input.astype(bf16)[None],
+        grad_input[None],
         gains[:MODEL_WIDTH] / attn_gain,
         gains[2 * MODEL_WIDTH : 2 * MODEL_WIDTH + HEAD_SIZE],
         gains[2 * MODEL_WIDTH + HEAD_SIZE :],

time: 623 us -> 579 us (0.929)
  starting transfers between devices: 129 us -> 95.5 us
  waiting for transfers between devices: 210 us -> 202 us
  matrix products: 28.3 us -> 21.5 us
    ppermute x59 -> x53, waiting for transfers between devices: 62.3 us -> 124 us  [shift(): return lax.ppermute(v, axis, [(i, (i + by) % n) for i in range(n)])]
    all_to_all x9 -> x5, waiting for transfers between devices: 122 us -> 61.4 us  [exchanged(): return lax.all_to_all(v, EXPERT, 0, 0, tiled=True)]
    all_to_all x9 -> x5, starting transfers between devices: 45.8 us -> 24.1 us  [exchanged(): return lax.all_to_all(v, EXPERT, 0, 0, tiled=True)]
    ppermute x2 -> x0, waiting for transfers between devices: 21.1 us -> none  [the longest x1 21.1 us: local(): lax.ppermute(arrived[:, :, :384], X, swap)]
    all_gather x0 -> x1, waiting for transfers between devices: none -> 12.2 us  [local(): parted = lax.all_gather(parted, EXPERT, axis=0, tiled=False)]
    ppermute x59 -> x53, starting transfers between devices: 75.9 us -> 67.2 us  [shift(): return lax.ppermute(v, axis, [(i, (i + by) % n) for i in range(n)])]
    unnamed x191 -> x180, local copies, waits for them, and re-layouts: 41.1 us -> 33.9 us
    convert_element_type x1 -> x10, other arithmetic: 0.01 us -> 6.92 us  [the longest x6 2.55 us: plus(): return (a.astype(f32) + b.astype(f32)).astype(bf16)]
  transfers between devices with their start and end apart: 77 -> 66, of which waited for: 25 -> 30; matrix products, arithmetic and copies ran while one was open for 15% -> 16% of each run, Pallas kernels for 20% -> 22%
where the time goes in v3:
time: 579 us; the launch traced here: 570 us
  waiting for transfers between devices  202 us (35%)
  Pallas kernels  130 us (22%)
  starting transfers between devices  95.5 us (16%)
  local copies, waits for them, and re-layouts  60.9 us (11%)
  other arithmetic  44.2 us (8%)
  matrix products  21.5 us (4%)
  between operations  16 us (3%)
    ppermute x53, waiting for transfers between devices, shift(): return lax.ppermute(v, axis, [(i, (i + by) % n) for i in range(n)])  124 us
    ppermute x53, starting transfers between devices, shift(): return lax.ppermute(v, axis, [(i, (i + by) % n) for i in range(n)])  67.2 us
    all_to_all x5, waiting for transfers between devices, exchanged(): return lax.all_to_all(v, EXPERT, 0, 0, tiled=True)  61.4 us
    pallas_call x2, Pallas kernels, expert_rows(): pl.pallas_call(functools.partial(expert_kernel, e), out_shape=[jax.ShapeD...  36.9 us
    unnamed x180, local copies, waits for them, and re-layouts  33.9 us
    pallas_call x1, Pallas kernels, weight_grads(): pl.pallas_call(weight_grads_kernel, grid=(2,), out_shape=[jax.ShapeDtypeS...  31.8 us
    all_to_all x5, starting transfers between devices, exchanged(): return lax.all_to_all(v, EXPERT, 0, 0, tiled=True)  24.1 us
    pallas_call x1, Pallas kernels, attention_forward(): pl.pallas_call(functools.partial(attention_kernel, spec), out_shape=[jax....  19.4 us
  transfers between devices with their start and end apart: 66, of which 30 were waited for; matrix products, arithmetic and copies ran while one was open for 16% of the time, Pallas kernels for 22%

profile of v3, /device:TPU:0, one launch (start us, length us, event | category | flops | bytes accessed | tf_op | source)
XLA Modules:
  0.0 569.8 jit_solution(17444851545768344116)
XLA Ops:
  24.4 4.7 collective-permute-start.4
  32.4 14.5 %collective-permute-done.1.refs_0_ = bf16[128,2176]{1,0:T(8,128)(2,1)S(1)} collective-permute-done((bf16[128,2176]{1,0:T(8,128)(2,1)}, bf16[128,2176]{1,0:T(8,128)(2,1)S(1)}, u32[]{:S(2)}, u32[]{:S(2)}) %collective-permute-start.1) | collective-permute-done | bytes 557088 | tf_op jit(solution)/shard_map/ppermute | solution.py:39
  47.0 19.2 %collective-permute-done.3.refs_5_.rest_11_.refs_2_ = bf16[2,256,768]{2,1,0:T(8,128)(2,1)S(1)} collective-permute-done((bf16[2,256,768]{2,1,0:T(8,128)(2,1)S(1)}, bf16[2,256,768]{2,1,0:T(8,128)(2,1)S(1)}, u32[]{:S(2)}, u32[]{:S(2)}) %collective-permute-start.3) | collective-permute-done | bytes 786464 | tf_op jit(solution)/shard_map/ppermute | solution.py:39
  83.6 4.3 collective-permute-done.rest_1_
  91.0 19.4 %attention_forward.1 = (bf16[2048,768]{1,0:T(8,128)(2,1)}, bf16[1024,2176]{1,0:T(8,128)(2,1)}, f32[1024,512]{1,0:T(8,128)}, f32[1024,128]{1,0:T(8,128)}, bf16[10...) custom-call(s32[4]{0:T(128)} %pad_add_fusion.place, ...), custom_call_target="tpu_custom_call" | custom-call | flops 9663676416 | bytes 29360128 | tf_op jit(solution)/shard_map/attention_forward/pallas_call | solution.py:223
  122.1 7.6 %collective-permute-done.14 = bf16[64,2048]{1,0:T(8,128)(2,1)S(1)} collective-permute-done((bf16[64,2048]{1,0:T(8,128)(2,1)S(1)}, bf16[64,2048]{1,0:T(8,128)(2,1)S(1)}, u32[]{:S(2)}, u32[]{:S(2)}) %collective-permute-start.14) | collective-permute-done | bytes 262176 | tf_op jit(solution)/shard_map/ppermute | solution.py:39
  134.3 10.6 %collective-permute-done.15 = bf16[128,2048]{1,0:T(8,128)(2,1)S(1)} collective-permute-done((bf16[128,2048]{1,0:T(8,128)(2,1)S(1)}, bf16[128,2048]{1,0:T(8,128)(2,1)S(1)}, u32[]{:S(2)}, u32[]{:S(2)}) %collective-permute-start.15) | collective-permute-done | bytes 524320 | tf_op jit(solution)/shard_map/ppermute | solution.py:39
  152.5 6.6 %all-to-all-start = ((bf16[16,40,2176]{2,1,0:T(8,128)(2,1)}), bf16[16,40,2176]{2,1,0:T(8,128)(2,1)S(1)}, u32[]{:S(2)}, u32[]{:S(2)}) async-start(bf16[16,40,2176]{2,1,0:T(8,128)(2,1)} %fusion.2), calls=%async_computation | async-start | bytes 5570560 | tf_op jit(solution)/shard_map/all_to_all | solution.py:571
  170.1 25.0 %all-to-all-done.refs_1_ = bf16[16,40,2176]{2,1,0:T(8,128)(2,1)S(1)} async-done(((bf16[16,40,2176]{2,1,0:T(8,128)(2,1)}), bf16[16,40,2176]{2,1,0:T(8,128)(2,1)S(1)}, u32[]{:S(2)}, u32[]{:S(2)}) %all-to-all-start) | async-done | bytes 2785312 | tf_op jit(solution)/shard_map/all_to_all | solution.py:571
  196.7 4.5 all-to-all-start.1
  202.6 4.6 convolution_convert_fusion.2
  207.3 18.4 %expert_rows.2 = (bf16[640,2176]{1,0:T(8,128)(2,1)}, bf16[640,768]{1,0:T(8,128)(2,1)S(1)}, bf16[640,768]{1,0:T(8,128)(2,1)S(1)}, bf16[640,768]{1,0:T(8,128)(2,1)S(1)}) custom-call(bf16[640,2176]{1,0:T(8,128)(2,1)} %bitcast.268, bf16[640,2048]{1,0:T(8,128)(2,1)S(1)} %bitcast.252, bf16[4,2048,768]{2,1,0:T(8,128)(2,1)} %all-gather.8.cloned.1.call-done.w_in, ...), custom_call_target="tpu_custom_call" | custom-call | flops 10737418240 | bytes 20971520 | tf_op jit(solution)/shard_map/expert_rows/pallas_call | solution.py:270
  228.6 11.7 %all-to-all-done.1.refs_1_ = bf16[16,40,2176]{2,1,0:T(8,128)(2,1)} async-done(((bf16[16,40,2176]{2,1,0:T(8,128)(2,1)}), bf16[16,40,2176]{2,1,0:T(8,128)(2,1)}, u32[]{:S(2)}, u32[]{:S(2)}) %all-to-all-start.1) | async-done | bytes 2785312 | tf_op jit(solution)/shard_map/all_to_all | solution.py:571
  240.3 4.6 all-to-all-start.2
  244.9 4.6 convolution_convert_fusion
  249.5 18.5 %expert_rows.3 = (bf16[640,2176]{1,0:T(8,128)(2,1)}, bf16[640,768]{1,0:T(8,128)(2,1)S(1)}, bf16[640,768]{1,0:T(8,128)(2,1)S(1)}, bf16[640,768]{1,0:T(8,128)(2,1)S(1)}) custom-call(bf16[640,2176]{1,0:T(8,128)(2,1)} %bitcast.46.xs_in.refs_6_, bf16[640,2048]{1,0:T(8,128)(2,1)S(1)} %bitcast.254, bf16[4,2048,768]{2,1,0:T(8,128)(2,1)} %all-gather.8.cloned.1.call-done.w_in, ...), custom_call_target="tpu_custom_call" | custom-call | flops 10737418240 | bytes 20971520 | tf_op jit(solution)/shard_map/expert_rows/pallas_call | solution.py:270
  271.0 11.7 %all-to-all-done.2.refs_13_.refs_1_ = bf16[16,40,2176]{2,1,0:T(8,128)(2,1)} async-done(((bf16[16,40,2176]{2,1,0:T(8,128)(2,1)}), bf16[16,40,2176]{2,1,0:T(8,128)(2,1)}, u32[]{:S(2)}, u32[]{:S(2)}) %all-to-all-start.2) | async-done | bytes 2785312 | tf_op jit(solution)/shard_map/all_to_all | solution.py:571
  289.7 31.8 %weight_grads.1 = (bf16[2,2048,768]{2,1,0:T(8,128)(2,1)}, bf16[2,2048,768]{2,1,0:T(8,128)(2,1)}, bf16[2,768,2048]{2,1,0:T(8,128)(2,1)}, bf16[16,80,2048]{2,1,0:T(8,128)(2,1)}) custom-call(bf16[640,2176]{1,0:T(8,128)(2,1)} %bitcast.269, bf16[640,2048]{1,0:T(8,128)(2,1)} %bitcast.253, bf16[640,768]{1,0:T(8,128)(2,1)} %copy-done.24, ...), custom_call_target="tpu_custom_call" | custom-call | flops 17179869184 | bytes 50331648 | tf_op jit(solution)/shard_map/weight_grads/pallas_call | solution.py:308
  321.5 5.3 all-to-all-done.3.refs_0_
  332.7 4.6 all-to-all-start.4
  345.6 16.8 %collective-permute-done.20.rest_3_ = bf16[128,2048]{1,0:T(8,128)(2,1)S(1)} collective-permute-done((bf16[128,2048]{1,0:T(8,128)(2,1)S(1)}, bf16[128,2048]{1,0:T(8,128)(2,1)S(1)}, u32[]{:S(2)}, u32[]{:S(2)}) %collective-permute-start.20) | collective-permute-done | bytes 524320 | tf_op jit(solution)/shard_map/ppermute | solution.py:39
  366.3 7.5 %collective-permute-done.21.rest_4_ = bf16[64,2048]{1,0:T(8,128)(2,1)S(1)} collective-permute-done((bf16[64,2048]{1,0:T(8,128)(2,1)S(1)}, bf16[64,2048]{1,0:T(8,128)(2,1)S(1)}, u32[]{:S(2)}, u32[]{:S(2)}) %collective-permute-start.21) | collective-permute-done | bytes 262176 | tf_op jit(solution)/shard_map/ppermute | solution.py:39
  378.8 6.3 %out_back.1 = (bf16[1024,512]{1,0:T(8,128)(2,1)S(1)}, bf16[16,128,512]{2,1,0:T(8,128)(2,1)S(1)}) custom-call(s32[4]{0:T(128)S(1)} %copy-done.18, bf16[512,2048]{1,0:T(8,128)(2,1)S(1)} %copy-done.20, bf16[1024,512]{1,0:T(8,128)(2,1)S(1)} %copy-done.23, bf16[128,2048]{1,0:T(8,128)(2,1)S(1)} %fusion.72.rest_0_, ...), custom_call_target="tpu_custom_call" | custom-call | flops 5368709120 | bytes 12582912 | tf_op jit(solution)/shard_map/out_back/pallas_call | solution.py:343
  386.4 13.6 %attention_backward.1 = (bf16[1024,512]{1,0:T(8,128)(2,1)S(1)}, f32[1024,256]{1,0:T(8,128)S(1)}, f32[1,128]{1,0:T(1,128)S(1)}) custom-call(bf16[1024,512]{1,0:T(8,128)(2,1)S(1)} %get-tuple-element.87.dob, bf16[1024,512]{1,0:T(8,128)(2,1)} %get-tuple-element.86.a_b, bf16[4,1024,128]{2,1,0:T(8,128)(2,1)} %get-tuple-element.88.q_b, ...), custom_call_target="tpu_custom_call" | custom-call | flops 10737418240 | bytes 12582912 | tf_op jit(solution)/shard_map/attention_backward/pallas_call | solution.py:391
  403.9 7.6 %all-to-all-done.4 = bf16[16,80,2048]{2,1,0:T(8,128)(2,1)} async-done(((bf16[16,80,2048]{2,1,0:T(8,128)(2,1)}), bf16[16,80,2048]{2,1,0:T(8,128)(2,1)}, u32[]{:S(2)}, u32[]{:S(2)}) %all-to-all-start.4) | async-done | bytes 5242912 | tf_op jit(solution)/shard_map/all_to_all | solution.py:571
  411.5 13.0 %projection_grads.1 = (bf16[4,64,1280]{2,1,0:T(8,128)(2,1)}, bf16[4,64,1280]{2,1,0:T(8,128)(2,1)}, bf16[2,64,1280]{2,1,0:T(8,128)(2,1)S(1)}, bf16[2,64,1280]{2,1...) custom-call(s32[4]{0:T(128)S(1)} %copy-done.18, ...), custom_call_target="tpu_custom_call" | custom-call | flops 3221225472 | bytes 16777216 | tf_op jit(solution)/shard_map/projection_grads/pallas_call | solution.py:446
  460.3 8.4 %collective-permute-done.34 = bf16[4,64,1280]{2,1,0:T(8,128)(2,1)S(1)} collective-permute-done((bf16[4,64,1280]{2,1,0:T(8,128)(2,1)S(1)}, bf16[4,64,1280]{2,1,0:T(8,128)(2,1)S(1)}, u32[]{:S(2)}, u32[]{:S(2)}) %collective-permute-start.34) | collective-permute-done | bytes 655392 | tf_op jit(solution)/shard_map/ppermute | solution.py:39
  497.6 4.9 input_grad.1
  510.6 5.9 %collective-permute-done.30 = bf16[64,2048]{1,0:T(8,128)(2,1)S(1)} collective-permute-done((bf16[64,2048]{1,0:T(8,128)(2,1)S(1)}, bf16[64,2048]{1,0:T(8,128)(2,1)S(1)}, u32[]{:S(2)}, u32[]{:S(2)}) %collective-permute-start.30) | collective-permute-done | bytes 262176 | tf_op jit(solution)/shard_map/ppermute | solution.py:39
  520.2 4.2 fusion.12
  524.4 6.6 %collective-permute-done.31 = bf16[128,2048]{1,0:T(8,128)(2,1)S(1)} collective-permute-done((bf16[128,2048]{1,0:T(8,128)(2,1)S(1)}, bf16[128,2048]{1,0:T(8,128)(2,1)S(1)}, u32[]{:S(2)}, u32[]{:S(2)}) %collective-permute-start.31) | collective-permute-done | bytes 524320 | tf_op jit(solution)/shard_map/ppermute | solution.py:39
  539.4 12.2 %all-gather.12.cloned.1.call-done = bf16[128,16,1280]{2,1,0:T(8,128)(2,1)} async-done(((bf16[8,16,1280]{2,1,0:T(8,128)(2,1)}), bf16[128,16,1280]{2,1,0:T(8,128)(2,1)}) %all-gather.12.cloned.1.call-update) | async-done | bytes 5242896 | tf_op jit(solution)/shard_map/all_gather | solution.py:691
  (457 shorter events, 214.5 us)
Async XLA Ops:
  7.2 195.4 %all-gather.6.cloned.1.call-start = ((), (), s32[]{:S(2)}) async-start(), calls=%async_computation.9 | async-start | bytes 8912896 | tf_op jit(solution)/shard_map/all_gather | solution.py:573
  9.4 197.8 %all-gather.10.cloned.1.call-start = ((), (), s32[]{:S(2)}) async-start(), calls=%async_computation.11 | async-start | bytes 7077888 | tf_op jit(solution)/shard_map/all_gather | solution.py:597
  12.8 34.2 %collective-permute-start.1 = (bf16[128,2176]{1,0:T(8,128)(2,1)}, bf16[128,2176]{1,0:T(8,128)(2,1)S(1)}, u32[]{:S(2)}, u32[]{:S(2)}) collective-permute-start(bf16[128,2176]{1,0:T(8,128)(2,1)} %fusion.29.rest_0_), channel_id=1, source_target_pairs={{0,96},{32,0},{64,32},{96,64},{1,97},{33,1},{65,33},{97,65},{2,98}... | collective-permute-start | bytes 1671176 | tf_op jit(solution)/shard_map/ppermute | solution.py:39
  16.9 30.1 %collective-permute-start.2 = (bf16[128,2176]{1,0:T(8,128)(2,1)}, bf16[128,2176]{1,0:T(8,128)(2,1)}, u32[]{:S(2)}, u32[]{:S(2)}) collective-permute-start(bf16[128,2176]{1,0:T(8,128)(2,1)} %fusion.29.rest_0_), channel_id=1, source_target_pairs={{0,32},{32,64},{64,96},{96,0},{1,33},{33,65},{65,97},{97,1},{2,34}... | collective-permute-start | bytes 1671176 | tf_op jit(solution)/shard_map/ppermute | solution.py:39
  24.4 41.7 %collective-permute-start.3 = (bf16[2,256,768]{2,1,0:T(8,128)(2,1)S(1)}, bf16[2,256,768]{2,1,0:T(8,128)(2,1)S(1)}, u32[]{:S(2)}, u32[]{:S(2)}) collective-permute-start(bf16[2,256,768]{2,1,0:T(8,128)(2,1)S(1)} %get-tuple-element.259), channel_id=1, source_target_pairs={{0,32},{32,64},{64,96},{96,0},{1,33},{33,65},{65,97},{97,1},{2,34}... | collective-permute-start | bytes 2359304 | tf_op jit(solution)/shard_map/ppermute | solution.py:39
  24.4 41.7 %collective-permute-start.4 = (bf16[2,256,768]{2,1,0:T(8,128)(2,1)S(1)}, bf16[2,256,768]{2,1,0:T(8,128)(2,1)}, u32[]{:S(2)}, u32[]{:S(2)}) collective-permute-start(bf16[2,256,768]{2,1,0:T(8,128)(2,1)S(1)} %get-tuple-element.258), channel_id=1, source_target_pairs={{0,64},{32,96},{64,0},{96,32},{1,65},{33,97},{65,1},{97,33},{2,66}... | collective-permute-start | bytes 2359304 | tf_op jit(solution)/shard_map/ppermute | solution.py:39
  29.1 37.0 %collective-permute-start.5 = (bf16[2,256,768]{2,1,0:T(8,128)(2,1)S(1)}, bf16[2,256,768]{2,1,0:T(8,128)(2,1)}, u32[]{:S(2)}, u32[]{:S(2)}) collective-permute-start(bf16[2,256,768]{2,1,0:T(8,128)(2,1)S(1)} %get-tuple-element.257), channel_id=1, source_target_pairs={{0,96},{32,0},{64,32},{96,64},{1,97},{33,1},{65,33},{97,65},{2,98}... | collective-permute-start | bytes 2359304 | tf_op jit(solution)/shard_map/ppermute | solution.py:39
  77.3 130.0 %all-gather.8.cloned.1.call-start = ((), (), s32[]{:S(2)}) async-start(), calls=%async_computation.10 | async-start | bytes 14155776 | tf_op jit(solution)/shard_map/all_gather | solution.py:596
  116.4 13.4 %collective-permute-start.14 = (bf16[64,2048]{1,0:T(8,128)(2,1)S(1)}, bf16[64,2048]{1,0:T(8,128)(2,1)S(1)}, u32[]{:S(2)}, u32[]{:S(2)}) collective-permute-start(bf16[64,2048]{1,0:T(8,128)(2,1)S(1)} %get-tuple-element.252), channel_id=1, source_target_pairs={{0,32},{32,64},{64,96},{96,0},{1,33},{33,65},{65,97},{97,1},{2,34}... | collective-permute-start | bytes 786440 | tf_op jit(solution)/shard_map/ppermute | solution.py:39
  116.5 13.5 %collective-permute-start.16 = (bf16[64,2048]{1,0:T(8,128)(2,1)S(1)}, bf16[64,2048]{1,0:T(8,128)(2,1)S(1)}, u32[]{:S(2)}, u32[]{:S(2)}) collective-permute-start(bf16[64,2048]{1,0:T(8,128)(2,1)S(1)} %get-tuple-element.253), channel_id=1, source_target_pairs={{0,96},{32,0},{64,32},{96,64},{1,97},{33,1},{65,33},{97,65},{2,98}... | collective-permute-start | bytes 786440 | tf_op jit(solution)/shard_map/ppermute | solution.py:39
  129.9 15.1 %collective-permute-start.15 = (bf16[128,2048]{1,0:T(8,128)(2,1)S(1)}, bf16[128,2048]{1,0:T(8,128)(2,1)S(1)}, u32[]{:S(2)}, u32[]{:S(2)}) collective-permute-start(bf16[128,2048]{1,0:T(8,128)(2,1)S(1)} %pad_maximum_fusion.6), channel_id=1, source_target_pairs={{0,32},{32,64},{64,96},{96,0},{1,33},{33,65},{65,97},{97,1},{2,34}... | collective-permute-start | bytes 1572872 | tf_op jit(solution)/shard_map/ppermute | solution.py:39
  130.1 17.0 %collective-permute-start.17 = (bf16[128,2048]{1,0:T(8,128)(2,1)S(1)}, bf16[128,2048]{1,0:T(8,128)(2,1)S(1)}, u32[]{:S(2)}, u32[]{:S(2)}) collective-permute-start(bf16[128,2048]{1,0:T(8,128)(2,1)S(1)} %pad_maximum_fusion.7), channel_id=1, source_target_pairs={{0,96},{32,0},{64,32},{96,64},{1,97},{33,1},{65,33},{97,65},{2,98}... | collective-permute-start | bytes 1572872 | tf_op jit(solution)/shard_map/ppermute | solution.py:39
  152.5 42.7 %all-to-all-start = ((bf16[16,40,2176]{2,1,0:T(8,128)(2,1)}), bf16[16,40,2176]{2,1,0:T(8,128)(2,1)S(1)}, u32[]{:S(2)}, u32[]{:S(2)}) async-start(bf16[16,40,2176]{2,1,0:T(8,128)(2,1)} %fusion.2), calls=%async_computation | async-start | bytes 5570560 | tf_op jit(solution)/shard_map/all_to_all | solution.py:571
  196.7 43.5 %all-to-all-start.1 = ((bf16[16,40,2176]{2,1,0:T(8,128)(2,1)}), bf16[16,40,2176]{2,1,0:T(8,128)(2,1)}, u32[]{:S(2)}, u32[]{:S(2)}) async-start(bf16[16,40,2176]{2,1,0:T(8,128)(2,1)} %after.11), calls=%async_computation.1 | async-start | bytes 5570560 | tf_op jit(solution)/shard_map/all_to_all | solution.py:571
  240.3 42.4 %all-to-all-start.2 = ((bf16[16,40,2176]{2,1,0:T(8,128)(2,1)}), bf16[16,40,2176]{2,1,0:T(8,128)(2,1)}, u32[]{:S(2)}, u32[]{:S(2)}) async-start(bf16[16,40,2176]{2,1,0:T(8,128)(2,1)} %after.12), calls=%async_computation.2 | async-start | bytes 5570560 | tf_op jit(solution)/shard_map/all_to_all | solution.py:571
  282.7 44.1 %all-to-all-start.3 = ((bf16[16,40,2176]{2,1,0:T(8,128)(2,1)}), bf16[16,40,2176]{2,1,0:T(8,128)(2,1)S(1)}, u32[]{:S(2)}, u32[]{:S(2)}) async-start(bf16[16,40,2176]{2,1,0:T(8,128)(2,1)} %after.13), calls=%async_computation.3 | async-start | bytes 5570560 | tf_op jit(solution)/shard_map/all_to_all | solution.py:571
  286.4 246.9 %reduce-scatter.4.cloned.1.call-start = ((), (), s32[]{:S(2)}) async-start(), calls=%async_computation.12 | async-start | bytes 7077888 | tf_op jit(solution)/shard_map/reduce_scatter | solution.py:664
  328.4 206.2 %reduce-scatter.6.cloned.1.call-start = ((), (), s32[]{:S(2)}) async-start(), calls=%async_computation.13 | async-start | bytes 7077888 | tf_op jit(solution)/shard_map/reduce_scatter | solution.py:664
  332.7 78.8 %all-to-all-start.4 = ((bf16[16,80,2048]{2,1,0:T(8,128)(2,1)}), bf16[16,80,2048]{2,1,0:T(8,128)(2,1)}, u32[]{:S(2)}, u32[]{:S(2)}) async-start(bf16[16,80,2048]{2,1,0:T(8,128)(2,1)} %after.15), calls=%async_computation.4 | async-start | bytes 10485760 | tf_op jit(solution)/shard_map/all_to_all | solution.py:571
  337.3 199.1 %reduce-scatter.8.cloned.1.call-start = ((), (), s32[]{:S(2)}) async-start(), calls=%async_computation.14 | async-start | bytes 7077888 | tf_op jit(solution)/shard_map/reduce_scatter | solution.py:664
  342.2 20.2 %collective-permute-start.20 = (bf16[128,2048]{1,0:T(8,128)(2,1)S(1)}, bf16[128,2048]{1,0:T(8,128)(2,1)S(1)}, u32[]{:S(2)}, u32[]{:S(2)}) collective-permute-start(bf16[128,2048]{1,0:T(8,128)(2,1)S(1)} %fusion.72.rest_0_), channel_id=1, source_target_pairs={{0,32},{32,64},{64,96},{96,0},{1,33},{33,65},{65,97},{97,1},{2,34}... | collective-permute-start | bytes 1572872 | tf_op jit(solution)/shard_map/ppermute | solution.py:39
  342.2 20.3 %collective-permute-start.19 = (bf16[128,2048]{1,0:T(8,128)(2,1)S(1)}, bf16[128,2048]{1,0:T(8,128)(2,1)S(1)}, u32[]{:S(2)}, u32[]{:S(2)}) collective-permute-start(bf16[128,2048]{1,0:T(8,128)(2,1)S(1)} %fusion.72.rest_0_), channel_id=1, source_target_pairs={{0,96},{32,0},{64,32},{96,64},{1,97},{33,1},{65,33},{97,65},{2,98}... | collective-permute-start | bytes 1572872 | tf_op jit(solution)/shard_map/ppermute | solution.py:39
  345.5 28.8 %collective-permute-start.18 = (bf16[128,2048]{1,0:T(8,128)(2,1)S(1)}, bf16[128,2048]{1,0:T(8,128)(2,1)S(1)}, u32[]{:S(2)}, u32[]{:S(2)}) collective-permute-start(bf16[128,2048]{1,0:T(8,128)(2,1)S(1)} %fusion.72.rest_0_), channel_id=1, source_target_pairs={{0,16},{16,0},{1,17},{17,1},{2,18},{18,2},{3,19},{19,3},{4,20},{20... | collective-permute-start | bytes 1572872 | tf_op jit(solution)/shard_map/ppermute | solution.py:39
  437.3 18.0 %collective-permute-start.42 = (bf16[4,64,1280]{2,1,0:T(8,128)(2,1)}, bf16[4,64,1280]{2,1,0:T(8,128)(2,1)}, u32[]{:S(2)}, u32[]{:S(2)}) collective-permute-start(bf16[4,64,1280]{2,1,0:T(8,128)(2,1)} %pad_maximum_fusion.4), channel_id=1, source_target_pairs={{0,1},{1,2},{2,3},{3,0},{4,5},{5,6},{6,7},{7,4},{8,9},{9,10},{10,1... | collective-permute-start | bytes 1966088 | tf_op jit(solution)/shard_map/ppermute | solution.py:39
  438.2 17.0 %collective-permute-start.44 = (bf16[4,64,1280]{2,1,0:T(8,128)(2,1)}, bf16[4,64,1280]{2,1,0:T(8,128)(2,1)}, u32[]{:S(2)}, u32[]{:S(2)}) collective-permute-start(bf16[4,64,1280]{2,1,0:T(8,128)(2,1)} %pad_maximum_fusion.5), channel_id=1, source_target_pairs={{0,3},{1,0},{2,1},{3,2},{4,7},{5,4},{6,5},{7,6},{8,11},{9,8},{10,9... | collective-permute-start | bytes 1966088 | tf_op jit(solution)/shard_map/ppermute | solution.py:39
  450.4 18.3 %collective-permute-start.34 = (bf16[4,64,1280]{2,1,0:T(8,128)(2,1)S(1)}, bf16[4,64,1280]{2,1,0:T(8,128)(2,1)S(1)}, u32[]{:S(2)}, u32[]{:S(2)}) collective-permute-start(bf16[4,64,1280]{2,1,0:T(8,128)(2,1)S(1)} %pad_maximum_fusion.2), channel_id=1, source_target_pairs={{0,4},{4,8},{8,12},{12,0},{1,5},{5,9},{9,13},{13,1},{2,6},{6,10},{... | collective-permute-start | bytes 1966088 | tf_op jit(solution)/shard_map/ppermute | solution.py:39
  451.9 17.0 %collective-permute-start.36 = (bf16[4,64,1280]{2,1,0:T(8,128)(2,1)S(1)}, bf16[4,64,1280]{2,1,0:T(8,128)(2,1)S(1)}, u32[]{:S(2)}, u32[]{:S(2)}) collective-permute-start(bf16[4,64,1280]{2,1,0:T(8,128)(2,1)S(1)} %pad_maximum_fusion.3), channel_id=1, source_target_pairs={{0,12},{4,0},{8,4},{12,8},{1,13},{5,1},{9,5},{13,9},{2,14},{6,2},{... | collective-permute-start | bytes 1966088 | tf_op jit(solution)/shard_map/ppermute | solution.py:39
  456.8 15.7 %collective-permute-start.45 = (bf16[32,1280]{1,0:T(8,128)(2,1)S(1)}, bf16[32,1280]{1,0:T(8,128)(2,1)S(1)}, u32[]{:S(2)}, u32[]{:S(2)}) collective-permute-start(bf16[32,1280]{1,0:T(8,128)(2,1)S(1)} %get-tuple-element.262), channel_id=1, source_target_pairs={{0,4},{4,8},{8,12},{12,0},{1,5},{5,9},{9,13},{13,1},{2,6},{6,10},{... | collective-permute-start | bytes 245768 | tf_op jit(solution)/shard_map/ppermute | solution.py:39
  456.9 15.6 %collective-permute-start.47 = (bf16[32,1280]{1,0:T(8,128)(2,1)S(1)}, bf16[32,1280]{1,0:T(8,128)(2,1)S(1)}, u32[]{:S(2)}, u32[]{:S(2)}) collective-permute-start(bf16[32,1280]{1,0:T(8,128)(2,1)S(1)} %get-tuple-element.263), channel_id=1, source_target_pairs={{0,12},{4,0},{8,4},{12,8},{1,13},{5,1},{9,5},{13,9},{2,14},{6,2},{... | collective-permute-start | bytes 245768 | tf_op jit(solution)/shard_map/ppermute | solution.py:39
  487.5 64.1 %all-gather.12.cloned.1.call-start = ((), (), s32[]{:S(2)}) async-start(), calls=%async_computation.15 | async-start | bytes 5570560 | tf_op jit(solution)/shard_map/all_gather | solution.py:691
  516.6 14.5 %collective-permute-start.31 = (bf16[128,2048]{1,0:T(8,128)(2,1)S(1)}, bf16[128,2048]{1,0:T(8,128)(2,1)S(1)}, u32[]{:S(2)}, u32[]{:S(2)}) collective-permute-start(bf16[128,2048]{1,0:T(8,128)(2,1)S(1)} %pad_maximum_fusion.8), channel_id=1, source_target_pairs={{0,32},{32,64},{64,96},{96,0},{1,33},{33,65},{65,97},{97,1},{2,34}... | collective-permute-start | bytes 1572872 | tf_op jit(solution)/shard_map/ppermute | solution.py:39
  516.8 14.3 %collective-permute-start.33 = (bf16[128,2048]{1,0:T(8,128)(2,1)S(1)}, bf16[128,2048]{1,0:T(8,128)(2,1)S(1)}, u32[]{:S(2)}, u32[]{:S(2)}) collective-permute-start(bf16[128,2048]{1,0:T(8,128)(2,1)S(1)} %pad_maximum_fusion.9), channel_id=1, source_target_pairs={{0,96},{32,0},{64,32},{96,64},{1,97},{33,1},{65,33},{97,65},{2,98}... | collective-permute-start | bytes 1572872 | tf_op jit(solution)/shard_map/ppermute | solution.py:39
  (123 other events, 959.9 us)
Sparse Core Ops, SparseCore 0:
  10.2 73.0 all-gather.5
  85.0 43.7 all-gather.9
  131.0 67.1 all-gather.7
  328.5 56.3 reduce-scatter.3
  387.2 42.6 reduce-scatter.5
  432.2 43.0 reduce-scatter.7
  496.3 55.2 all-gather.11

commit v4 on v3

--- a/solution.py
+++ b/solution.py
@@ -488,9 +488,13 @@
     return {0: (0, inner), 1: (1, inner), 2: (2 + inner // 2, inner % 2), 3: (4, inner)}[outer]
 
 
-def place_kernel(parts, *refs):
-    query, key, value, aux, gains, out = refs[-6:]
+def place_kernel(source, *refs):
+    query, key, value, aux, gains, out, parts, sems = refs[-8:]
+    copies = [pltpu.make_async_copy(source.at[r], parts.at[r], sems.at[r]) for r in range(16)]
+    for copy in copies:
+        copy.start()
     for r in range(16):
+        copies[r].wait()
         rows = slice(16 * r, 16 * r + 16)
         total = jnp.zeros((16, 128), f32)
         for f in range(8):
@@ -510,9 +514,10 @@
     return pl.pallas_call(
         place_kernel,
         out_shape=[jax.ShapeDtypeStruct(s, f32) for s in shapes],
-        in_specs=[VM] + [ANY] * len(events),
+        in_specs=[ANY] * (1 + len(events)),
         out_specs=[VM] * 6,
-        compiler_params=pltpu.CompilerParams(vmem_limit_bytes=40 * MIB),
+        scratch_shapes=[pltpu.VMEM((16, 8, 16, 1280), bf16), pltpu.SemaphoreType.DMA((16,))],
+        compiler_params=pltpu.CompilerParams(vmem_limit_bytes=60 * MIB),
         cost_estimate=pl.CostEstimate(flops=0, bytes_accessed=16 << 20, transcendentals=0),
         name="place_rows",
     )(parts, *events)
@@ -588,7 +593,8 @@
         return lax.dynamic_index_in_dim(blocks, (place_z + ahead) % 4, 0, keepdims=False)
 
     w_parts = [meant_for(0)] + [shift(meant_for(d), Z, d) for d in range(1, 4)]
-    h1_pieces = gather_fsdp(h1, lambda up, down: after([up, down], cosine, signed, in_own, *w_parts[1:]))
+    h1_pieces = gather_fsdp(h1, lambda up, down: after([up, down], cosine, signed, in_own))
+    w_parts[1:] = after(w_parts[1:], *[h1_pieces[k][0] for k in (1, 4, 5)])
     from_other = shift(jnp.stack([v[1] for v in w_parts]), C, 1)
     in_own, down_own = after(
         [in_own, w_down], *w_parts[1:], h1_pieces[4][0], h1_pieces[5][0]

time: 579 us -> 577 us (level)
  local copies, waits for them, and re-layouts: 60.9 us -> 53.8 us
    unnamed x180 -> x170, local copies, waits for them, and re-layouts: 33.9 us -> 27.9 us
where the time goes in v4:
time: 577 us; the launch traced here: 568 us
  waiting for transfers between devices  207 us (36%)
  Pallas kernels  131 us (23%)
  starting transfers between devices  93.6 us (16%)
  local copies, waits for them, and re-layouts  53.8 us (9%)
  other arithmetic  44.9 us (8%)
  matrix products  21.7 us (4%)
  between operations  16 us (3%)
    ppermute x53, waiting for transfers between devices, shift(): return lax.ppermute(v, axis, [(i, (i + by) % n) for i in range(n)])  125 us
    all_to_all x5, waiting for transfers between devices, exchanged(): return lax.all_to_all(v, EXPERT, 0, 0, tiled=True)  66.7 us
    ppermute x53, starting transfers between devices, shift(): return lax.ppermute(v, axis, [(i, (i + by) % n) for i in range(n)])  65 us
    pallas_call x2, Pallas kernels, expert_rows(): pl.pallas_call(functools.partial(expert_kernel, e), out_shape=[jax.ShapeD...  36.8 us
    pallas_call x1, Pallas kernels, weight_grads(): pl.pallas_call(weight_grads_kernel, grid=(2,), out_shape=[jax.ShapeDtypeS...  31.8 us
    unnamed x170, local copies, waits for them, and re-layouts  27.9 us
    all_to_all x5, starting transfers between devices, exchanged(): return lax.all_to_all(v, EXPERT, 0, 0, tiled=True)  24.2 us
    pallas_call x1, Pallas kernels, attention_forward(): pl.pallas_call(functools.partial(attention_kernel, spec), out_shape=[jax....  18.5 us
  transfers between devices with their start and end apart: 66, of which 30 were waited for; matrix products, arithmetic and copies ran while one was open for 16% of the time, Pallas kernels for 22%

profile of v4, /device:TPU:0, one launch (start us, length us, event | category | flops | bytes accessed | tf_op | source)
XLA Modules:
  0.0 568.5 jit_solution(16231509695199615033)
XLA Ops:
  26.1 21.0 %collective-permute-done.1.refs_0_ = bf16[128,2176]{1,0:T(8,128)(2,1)} collective-permute-done((bf16[128,2176]{1,0:T(8,128)(2,1)}, bf16[128,2176]{1,0:T(8,128)(2,1)}, u32[]{:S(2)}, u32[]{:S(2)}) %collective-permute-start.1) | collective-permute-done | bytes 557088 | tf_op jit(solution)/shard_map/ppermute | solution.py:39
  56.2 7.8 %collective-permute-done.11.refs_2_ = bf16[2,256,768]{2,1,0:T(8,128)(2,1)S(1)} collective-permute-done((bf16[2,256,768]{2,1,0:T(8,128)(2,1)}, bf16[2,256,768]{2,1,0:T(8,128)(2,1)S(1)}, u32[]{:S(2)}, u32[]{:S(2)}) %collective-permute-start.11) | collective-permute-done | bytes 786464 | tf_op jit(solution)/shard_map/ppermute | solution.py:39
  64.0 5.6 collective-permute-done.9.refs_0_
  83.9 18.5 %attention_forward.1 = (bf16[2048,768]{1,0:T(8,128)(2,1)}, bf16[1024,2176]{1,0:T(8,128)(2,1)}, f32[1024,512]{1,0:T(8,128)}, f32[1024,128]{1,0:T(8,128)}, bf16[10...) custom-call(s32[4]{0:T(128)} %pad_add_fusion.place, ...), custom_call_target="tpu_custom_call" | custom-call | flops 9663676416 | bytes 29360128 | tf_op jit(solution)/shard_map/attention_forward/pallas_call | solution.py:223
  113.0 10.8 %collective-permute-done.14 = bf16[64,2048]{1,0:T(8,128)(2,1)S(1)} collective-permute-done((bf16[64,2048]{1,0:T(8,128)(2,1)S(1)}, bf16[64,2048]{1,0:T(8,128)(2,1)S(1)}, u32[]{:S(2)}, u32[]{:S(2)}) %collective-permute-start.14) | collective-permute-done | bytes 262176 | tf_op jit(solution)/shard_map/ppermute | solution.py:39
  129.1 12.0 %collective-permute-done.15 = bf16[128,2048]{1,0:T(8,128)(2,1)} collective-permute-done((bf16[128,2048]{1,0:T(8,128)(2,1)S(1)}, bf16[128,2048]{1,0:T(8,128)(2,1)}, u32[]{:S(2)}, u32[]{:S(2)}) %collective-permute-start.15) | collective-permute-done | bytes 524320 | tf_op jit(solution)/shard_map/ppermute | solution.py:39
  146.7 6.8 %all-to-all-start = ((bf16[16,40,2176]{2,1,0:T(8,128)(2,1)}), bf16[16,40,2176]{2,1,0:T(8,128)(2,1)S(1)}, u32[]{:S(2)}, u32[]{:S(2)}) async-start(bf16[16,40,2176]{2,1,0:T(8,128)(2,1)} %fusion.2), calls=%async_computation | async-start | bytes 5570560 | tf_op jit(solution)/shard_map/all_to_all | solution.py:576
  164.5 30.6 %all-to-all-done.refs_1_ = bf16[16,40,2176]{2,1,0:T(8,128)(2,1)S(1)} async-done(((bf16[16,40,2176]{2,1,0:T(8,128)(2,1)}), bf16[16,40,2176]{2,1,0:T(8,128)(2,1)S(1)}, u32[]{:S(2)}, u32[]{:S(2)}) %all-to-all-start) | async-done | bytes 2785312 | tf_op jit(solution)/shard_map/all_to_all | solution.py:576
  196.6 4.5 all-to-all-start.1
  202.5 4.7 convolution_convert_fusion.2
  207.3 18.4 %expert_rows.2 = (bf16[640,2176]{1,0:T(8,128)(2,1)}, bf16[640,768]{1,0:T(8,128)(2,1)S(1)}, bf16[640,768]{1,0:T(8,128)(2,1)S(1)}, bf16[640,768]{1,0:T(8,128)(2,1)S(1)}) custom-call(bf16[640,2176]{1,0:T(8,128)(2,1)} %bitcast.265, bf16[640,2048]{1,0:T(8,128)(2,1)S(1)} %bitcast.252, bf16[4,2048,768]{2,1,0:T(8,128)(2,1)} %all-gather.8.cloned.1.call-done.w_in, ...), custom_call_target="tpu_custom_call" | custom-call | flops 10737418240 | bytes 20971520 | tf_op jit(solution)/shard_map/expert_rows/pallas_call | solution.py:270
  228.6 11.4 %all-to-all-done.1.refs_1_ = bf16[16,40,2176]{2,1,0:T(8,128)(2,1)} async-done(((bf16[16,40,2176]{2,1,0:T(8,128)(2,1)}), bf16[16,40,2176]{2,1,0:T(8,128)(2,1)}, u32[]{:S(2)}, u32[]{:S(2)}) %all-to-all-start.1) | async-done | bytes 2785312 | tf_op jit(solution)/shard_map/all_to_all | solution.py:576
  239.9 4.6 all-to-all-start.2
  244.6 4.6 convolution_convert_fusion
  249.2 18.4 %expert_rows.3 = (bf16[640,2176]{1,0:T(8,128)(2,1)}, bf16[640,768]{1,0:T(8,128)(2,1)S(1)}, bf16[640,768]{1,0:T(8,128)(2,1)S(1)}, bf16[640,768]{1,0:T(8,128)(2,1)S(1)}) custom-call(bf16[640,2176]{1,0:T(8,128)(2,1)} %bitcast.46.xs_in.refs_6_, bf16[640,2048]{1,0:T(8,128)(2,1)S(1)} %bitcast.254, bf16[4,2048,768]{2,1,0:T(8,128)(2,1)} %all-gather.8.cloned.1.call-done.w_in, ...), custom_call_target="tpu_custom_call" | custom-call | flops 10737418240 | bytes 20971520 | tf_op jit(solution)/shard_map/expert_rows/pallas_call | solution.py:270
  270.5 11.8 %all-to-all-done.2.refs_13_.refs_1_ = bf16[16,40,2176]{2,1,0:T(8,128)(2,1)} async-done(((bf16[16,40,2176]{2,1,0:T(8,128)(2,1)}), bf16[16,40,2176]{2,1,0:T(8,128)(2,1)}, u32[]{:S(2)}, u32[]{:S(2)}) %all-to-all-start.2) | async-done | bytes 2785312 | tf_op jit(solution)/shard_map/all_to_all | solution.py:576
  289.4 31.8 %weight_grads.1 = (bf16[2,2048,768]{2,1,0:T(8,128)(2,1)}, bf16[2,2048,768]{2,1,0:T(8,128)(2,1)}, bf16[2,768,2048]{2,1,0:T(8,128)(2,1)}, bf16[16,80,2048]{2,1,0:T(8,128)(2,1)}) custom-call(bf16[640,2176]{1,0:T(8,128)(2,1)} %bitcast.266, bf16[640,2048]{1,0:T(8,128)(2,1)} %bitcast.253, bf16[640,768]{1,0:T(8,128)(2,1)} %copy-done.19, ...), custom_call_target="tpu_custom_call" | custom-call | flops 17179869184 | bytes 50331648 | tf_op jit(solution)/shard_map/weight_grads/pallas_call | solution.py:308
  321.1 5.3 all-to-all-done.3.refs_0_
  332.4 4.6 all-to-all-start.4
  345.2 16.8 %collective-permute-done.20.rest_3_ = bf16[128,2048]{1,0:T(8,128)(2,1)S(1)} collective-permute-done((bf16[128,2048]{1,0:T(8,128)(2,1)S(1)}, bf16[128,2048]{1,0:T(8,128)(2,1)S(1)}, u32[]{:S(2)}, u32[]{:S(2)}) %collective-permute-start.20) | collective-permute-done | bytes 524320 | tf_op jit(solution)/shard_map/ppermute | solution.py:39
  366.0 7.5 %collective-permute-done.21.rest_4_ = bf16[64,2048]{1,0:T(8,128)(2,1)S(1)} collective-permute-done((bf16[64,2048]{1,0:T(8,128)(2,1)S(1)}, bf16[64,2048]{1,0:T(8,128)(2,1)S(1)}, u32[]{:S(2)}, u32[]{:S(2)}) %collective-permute-start.21) | collective-permute-done | bytes 262176 | tf_op jit(solution)/shard_map/ppermute | solution.py:39
  378.5 6.3 %out_back.1 = (bf16[1024,512]{1,0:T(8,128)(2,1)S(1)}, bf16[16,128,512]{2,1,0:T(8,128)(2,1)S(1)}) custom-call(s32[4]{0:T(128)S(1)} %copy-done.13, bf16[512,2048]{1,0:T(8,128)(2,1)S(1)} %copy-done.15, bf16[1024,512]{1,0:T(8,128)(2,1)S(1)} %copy-done.18, bf16[128,2048]{1,0:T(8,128)(2,1)S(1)} %fusion.72.rest_0_, ...), custom_call_target="tpu_custom_call" | custom-call | flops 5368709120 | bytes 12582912 | tf_op jit(solution)/shard_map/out_back/pallas_call | solution.py:343
  386.1 13.6 %attention_backward.1 = (bf16[1024,512]{1,0:T(8,128)(2,1)S(1)}, f32[1024,256]{1,0:T(8,128)S(1)}, f32[1,128]{1,0:T(1,128)S(1)}) custom-call(bf16[1024,512]{1,0:T(8,128)(2,1)S(1)} %get-tuple-element.93.dob, bf16[1024,512]{1,0:T(8,128)(2,1)} %get-tuple-element.92.a_b, bf16[4,1024,128]{2,1,0:T(8,128)(2,1)} %get-tuple-element.94.q_b, ...), custom_call_target="tpu_custom_call" | custom-call | flops 10737418240 | bytes 12582912 | tf_op jit(solution)/shard_map/attention_backward/pallas_call | solution.py:391
  403.5 7.6 %all-to-all-done.4 = bf16[16,80,2048]{2,1,0:T(8,128)(2,1)} async-done(((bf16[16,80,2048]{2,1,0:T(8,128)(2,1)}), bf16[16,80,2048]{2,1,0:T(8,128)(2,1)}, u32[]{:S(2)}, u32[]{:S(2)}) %all-to-all-start.4) | async-done | bytes 5242912 | tf_op jit(solution)/shard_map/all_to_all | solution.py:576
  411.1 13.0 %projection_grads.1 = (bf16[4,64,1280]{2,1,0:T(8,128)(2,1)}, bf16[4,64,1280]{2,1,0:T(8,128)(2,1)}, bf16[2,64,1280]{2,1,0:T(8,128)(2,1)S(1)}, bf16[2,64,1280]{2,1...) custom-call(s32[4]{0:T(128)S(1)} %copy-done.13, ...), custom_call_target="tpu_custom_call" | custom-call | flops 3221225472 | bytes 16777216 | tf_op jit(solution)/shard_map/projection_grads/pallas_call | solution.py:446
  459.9 8.4 %collective-permute-done.34 = bf16[4,64,1280]{2,1,0:T(8,128)(2,1)S(1)} collective-permute-done((bf16[4,64,1280]{2,1,0:T(8,128)(2,1)S(1)}, bf16[4,64,1280]{2,1,0:T(8,128)(2,1)S(1)}, u32[]{:S(2)}, u32[]{:S(2)}) %collective-permute-start.34) | collective-permute-done | bytes 655392 | tf_op jit(solution)/shard_map/ppermute | solution.py:39
  497.2 4.9 input_grad.1
  510.2 5.9 %collective-permute-done.30 = bf16[64,2048]{1,0:T(8,128)(2,1)S(1)} collective-permute-done((bf16[64,2048]{1,0:T(8,128)(2,1)S(1)}, bf16[64,2048]{1,0:T(8,128)(2,1)S(1)}, u32[]{:S(2)}, u32[]{:S(2)}) %collective-permute-start.30) | collective-permute-done | bytes 262176 | tf_op jit(solution)/shard_map/ppermute | solution.py:39
  519.9 4.2 fusion.12
  524.1 6.7 %collective-permute-done.31 = bf16[128,2048]{1,0:T(8,128)(2,1)S(1)} collective-permute-done((bf16[128,2048]{1,0:T(8,128)(2,1)S(1)}, bf16[128,2048]{1,0:T(8,128)(2,1)S(1)}, u32[]{:S(2)}, u32[]{:S(2)}) %collective-permute-start.31) | collective-permute-done | bytes 524320 | tf_op jit(solution)/shard_map/ppermute | solution.py:39
  540.2 11.1 %all-gather.12.cloned.1.call-done = bf16[128,16,1280]{2,1,0:T(8,128)(2,1)} async-done(((bf16[8,16,1280]{2,1,0:T(8,128)(2,1)}), bf16[128,16,1280]{2,1,0:T(8,128)(2,1)}) %all-gather.12.cloned.1.call-update) | async-done | bytes 5242896 | tf_op jit(solution)/shard_map/all_gather | solution.py:697
  551.3 6.4 %place_rows.1 = (f32[256,4096]{1,0:T(8,128)}, f32[256,512]{1,0:T(8,128)}, f32[256,512]{1,0:T(8,128)}, f32[256,128]{1,0:T(8,128)}, f32[8,16,128]{2,1,0:T(8,128)}, /*index=5*/f32[512,2048]{1,0:T(8,128)}) custom-call(bf16[16,8,16,1280]{3,2,1,0:T(8,128)(2,1)} %bitcast.272, bf16[128,2048]{1,0:T(8,128)(2,1)} %fusion.23.refs_0_, ...), custom_call_target="tpu_custom_call" | custom-call | bytes 16777216 | tf_op jit(solution)/shard_map/place_rows/pallas_call | solution.py:514
  (447 shorter events, 207.0 us)
Async XLA Ops:
  7.2 195.3 %all-gather.6.cloned.1.call-start = ((), (), s32[]{:S(2)}) async-start(), calls=%async_computation.9 | async-start | bytes 8912896 | tf_op jit(solution)/shard_map/all_gather | solution.py:578
  9.5 197.8 %all-gather.10.cloned.1.call-start = ((), (), s32[]{:S(2)}) async-start(), calls=%async_computation.11 | async-start | bytes 7077888 | tf_op jit(solution)/shard_map/all_gather | solution.py:603
  12.8 34.3 %collective-permute-start.1 = (bf16[128,2176]{1,0:T(8,128)(2,1)}, bf16[128,2176]{1,0:T(8,128)(2,1)}, u32[]{:S(2)}, u32[]{:S(2)}) collective-permute-start(bf16[128,2176]{1,0:T(8,128)(2,1)} %fusion.29.rest_0_), channel_id=1, source_target_pairs={{0,96},{32,0},{64,32},{96,64},{1,97},{33,1},{65,33},{97,65},{2,98}... | collective-permute-start | bytes 1671176 | tf_op jit(solution)/shard_map/ppermute | solution.py:39
  16.9 33.4 %collective-permute-start.2 = (bf16[128,2176]{1,0:T(8,128)(2,1)}, bf16[128,2176]{1,0:T(8,128)(2,1)}, u32[]{:S(2)}, u32[]{:S(2)}) collective-permute-start(bf16[128,2176]{1,0:T(8,128)(2,1)} %fusion.29.rest_0_), channel_id=1, source_target_pairs={{0,32},{32,64},{64,96},{96,0},{1,33},{33,65},{65,97},{97,1},{2,34}... | collective-permute-start | bytes 1671176 | tf_op jit(solution)/shard_map/ppermute | solution.py:39
  16.9 35.5 %collective-permute-start = (bf16[128,2176]{1,0:T(8,128)(2,1)}, bf16[128,2176]{1,0:T(8,128)(2,1)}, u32[]{:S(2)}, u32[]{:S(2)}) collective-permute-start(bf16[128,2176]{1,0:T(8,128)(2,1)} %fusion.29.rest_0_), channel_id=1, source_target_pairs={{0,16},{16,0},{1,17},{17,1},{2,18},{18,2},{3,19},{19,3},{4,20},{20... | collective-permute-start | bytes 1671176 | tf_op jit(solution)/shard_map/ppermute | solution.py:39
  22.7 33.4 %collective-permute-start.10 = (bf16[2,256,768]{2,1,0:T(8,128)(2,1)}, bf16[2,256,768]{2,1,0:T(8,128)(2,1)S(1)}, u32[]{:S(2)}, u32[]{:S(2)}) collective-permute-start(bf16[2,256,768]{2,1,0:T(8,128)(2,1)} %get-tuple-element.263), channel_id=1, source_target_pairs={{0,64},{32,96},{64,0},{96,32},{1,65},{33,97},{65,1},{97,33},{2,66}... | collective-permute-start | bytes 2359304 | tf_op jit(solution)/shard_map/ppermute | solution.py:39
  24.4 39.6 %collective-permute-start.11 = (bf16[2,256,768]{2,1,0:T(8,128)(2,1)}, bf16[2,256,768]{2,1,0:T(8,128)(2,1)S(1)}, u32[]{:S(2)}, u32[]{:S(2)}) collective-permute-start(bf16[2,256,768]{2,1,0:T(8,128)(2,1)} %get-tuple-element.262), channel_id=1, source_target_pairs={{0,96},{32,0},{64,32},{96,64},{1,97},{33,1},{65,33},{97,65},{2,98}... | collective-permute-start | bytes 2359304 | tf_op jit(solution)/shard_map/ppermute | solution.py:39
  47.1 22.5 %collective-permute-start.9 = (bf16[2,256,768]{2,1,0:T(8,128)(2,1)}, bf16[2,256,768]{2,1,0:T(8,128)(2,1)}, u32[]{:S(2)}, u32[]{:S(2)}) collective-permute-start(bf16[2,256,768]{2,1,0:T(8,128)(2,1)} %get-tuple-element.264), channel_id=1, source_target_pairs={{0,32},{32,64},{64,96},{96,0},{1,33},{33,65},{65,97},{97,1},{2,34}... | collective-permute-start | bytes 2359304 | tf_op jit(solution)/shard_map/ppermute | solution.py:39
  51.3 21.2 %collective-permute-start.3 = (bf16[64,2176]{1,0:T(8,128)(2,1)S(1)}, bf16[64,2176]{1,0:T(8,128)(2,1)S(1)}, u32[]{:S(2)}, u32[]{:S(2)}) collective-permute-start(bf16[64,2176]{1,0:T(8,128)(2,1)S(1)} %slice.334), channel_id=1, source_target_pairs={{0,32},{32,64},{64,96},{96,0},{1,33},{33,65},{65,97},{97,1},{2,34}... | collective-permute-start | bytes 835592 | tf_op jit(solution)/shard_map/ppermute | solution.py:39
  52.4 20.1 %collective-permute-start.4 = (bf16[64,2176]{1,0:T(8,128)(2,1)S(1)}, bf16[64,2176]{1,0:T(8,128)(2,1)S(1)}, u32[]{:S(2)}, u32[]{:S(2)}) collective-permute-start(bf16[64,2176]{1,0:T(8,128)(2,1)S(1)} %slice.335), channel_id=1, source_target_pairs={{0,96},{32,0},{64,32},{96,64},{1,97},{33,1},{65,33},{97,65},{2,98}... | collective-permute-start | bytes 835592 | tf_op jit(solution)/shard_map/ppermute | solution.py:39
  74.0 133.4 %all-gather.8.cloned.1.call-start = ((), (), s32[]{:S(2)}) async-start(), calls=%async_computation.10 | async-start | bytes 14155776 | tf_op jit(solution)/shard_map/all_gather | solution.py:602
  108.0 15.8 %collective-permute-start.14 = (bf16[64,2048]{1,0:T(8,128)(2,1)S(1)}, bf16[64,2048]{1,0:T(8,128)(2,1)S(1)}, u32[]{:S(2)}, u32[]{:S(2)}) collective-permute-start(bf16[64,2048]{1,0:T(8,128)(2,1)S(1)} %get-tuple-element.258), channel_id=1, source_target_pairs={{0,32},{32,64},{64,96},{96,0},{1,33},{33,65},{65,97},{97,1},{2,34}... | collective-permute-start | bytes 786440 | tf_op jit(solution)/shard_map/ppermute | solution.py:39
  108.1 15.9 %collective-permute-start.16 = (bf16[64,2048]{1,0:T(8,128)(2,1)S(1)}, bf16[64,2048]{1,0:T(8,128)(2,1)S(1)}, u32[]{:S(2)}, u32[]{:S(2)}) collective-permute-start(bf16[64,2048]{1,0:T(8,128)(2,1)S(1)} %get-tuple-element.259), channel_id=1, source_target_pairs={{0,96},{32,0},{64,32},{96,64},{1,97},{33,1},{65,33},{97,65},{2,98}... | collective-permute-start | bytes 786440 | tf_op jit(solution)/shard_map/ppermute | solution.py:39
  123.9 17.2 %collective-permute-start.15 = (bf16[128,2048]{1,0:T(8,128)(2,1)S(1)}, bf16[128,2048]{1,0:T(8,128)(2,1)}, u32[]{:S(2)}, u32[]{:S(2)}) collective-permute-start(bf16[128,2048]{1,0:T(8,128)(2,1)S(1)} %pad_maximum_fusion.6), channel_id=1, source_target_pairs={{0,32},{32,64},{64,96},{96,0},{1,33},{33,65},{65,97},{97,1},{2,34}... | collective-permute-start | bytes 1572872 | tf_op jit(solution)/shard_map/ppermute | solution.py:39
  124.9 16.2 %collective-permute-start.17 = (bf16[128,2048]{1,0:T(8,128)(2,1)}, bf16[128,2048]{1,0:T(8,128)(2,1)}, u32[]{:S(2)}, u32[]{:S(2)}) collective-permute-start(bf16[128,2048]{1,0:T(8,128)(2,1)} %pad_maximum_fusion.7), channel_id=1, source_target_pairs={{0,96},{32,0},{64,32},{96,64},{1,97},{33,1},{65,33},{97,65},{2,98}... | collective-permute-start | bytes 1572872 | tf_op jit(solution)/shard_map/ppermute | solution.py:39
  146.7 48.4 %all-to-all-start = ((bf16[16,40,2176]{2,1,0:T(8,128)(2,1)}), bf16[16,40,2176]{2,1,0:T(8,128)(2,1)S(1)}, u32[]{:S(2)}, u32[]{:S(2)}) async-start(bf16[16,40,2176]{2,1,0:T(8,128)(2,1)} %fusion.2), calls=%async_computation | async-start | bytes 5570560 | tf_op jit(solution)/shard_map/all_to_all | solution.py:576
  196.6 43.3 %all-to-all-start.1 = ((bf16[16,40,2176]{2,1,0:T(8,128)(2,1)}), bf16[16,40,2176]{2,1,0:T(8,128)(2,1)}, u32[]{:S(2)}, u32[]{:S(2)}) async-start(bf16[16,40,2176]{2,1,0:T(8,128)(2,1)} %after.13), calls=%async_computation.1 | async-start | bytes 5570560 | tf_op jit(solution)/shard_map/all_to_all | solution.py:576
  239.9 42.4 %all-to-all-start.2 = ((bf16[16,40,2176]{2,1,0:T(8,128)(2,1)}), bf16[16,40,2176]{2,1,0:T(8,128)(2,1)}, u32[]{:S(2)}, u32[]{:S(2)}) async-start(bf16[16,40,2176]{2,1,0:T(8,128)(2,1)} %after.14), calls=%async_computation.2 | async-start | bytes 5570560 | tf_op jit(solution)/shard_map/all_to_all | solution.py:576
  282.4 44.1 %all-to-all-start.3 = ((bf16[16,40,2176]{2,1,0:T(8,128)(2,1)}), bf16[16,40,2176]{2,1,0:T(8,128)(2,1)S(1)}, u32[]{:S(2)}, u32[]{:S(2)}) async-start(bf16[16,40,2176]{2,1,0:T(8,128)(2,1)} %after.15), calls=%async_computation.3 | async-start | bytes 5570560 | tf_op jit(solution)/shard_map/all_to_all | solution.py:576
  286.1 246.8 %reduce-scatter.4.cloned.1.call-start = ((), (), s32[]{:S(2)}) async-start(), calls=%async_computation.12 | async-start | bytes 7077888 | tf_op jit(solution)/shard_map/reduce_scatter | solution.py:670
  328.0 207.3 %reduce-scatter.6.cloned.1.call-start = ((), (), s32[]{:S(2)}) async-start(), calls=%async_computation.13 | async-start | bytes 7077888 | tf_op jit(solution)/shard_map/reduce_scatter | solution.py:670
  332.4 78.8 %all-to-all-start.4 = ((bf16[16,80,2048]{2,1,0:T(8,128)(2,1)}), bf16[16,80,2048]{2,1,0:T(8,128)(2,1)}, u32[]{:S(2)}, u32[]{:S(2)}) async-start(bf16[16,80,2048]{2,1,0:T(8,128)(2,1)} %after.17), calls=%async_computation.4 | async-start | bytes 10485760 | tf_op jit(solution)/shard_map/all_to_all | solution.py:576
  337.0 200.8 %reduce-scatter.8.cloned.1.call-start = ((), (), s32[]{:S(2)}) async-start(), calls=%async_computation.14 | async-start | bytes 7077888 | tf_op jit(solution)/shard_map/reduce_scatter | solution.py:670
  341.9 20.2 %collective-permute-start.20 = (bf16[128,2048]{1,0:T(8,128)(2,1)S(1)}, bf16[128,2048]{1,0:T(8,128)(2,1)S(1)}, u32[]{:S(2)}, u32[]{:S(2)}) collective-permute-start(bf16[128,2048]{1,0:T(8,128)(2,1)S(1)} %fusion.72.rest_0_), channel_id=1, source_target_pairs={{0,32},{32,64},{64,96},{96,0},{1,33},{33,65},{65,97},{97,1},{2,34}... | collective-permute-start | bytes 1572872 | tf_op jit(solution)/shard_map/ppermute | solution.py:39
  342.6 19.5 %collective-permute-start.19 = (bf16[128,2048]{1,0:T(8,128)(2,1)S(1)}, bf16[128,2048]{1,0:T(8,128)(2,1)S(1)}, u32[]{:S(2)}, u32[]{:S(2)}) collective-permute-start(bf16[128,2048]{1,0:T(8,128)(2,1)S(1)} %fusion.72.rest_0_), channel_id=1, source_target_pairs={{0,96},{32,0},{64,32},{96,64},{1,97},{33,1},{65,33},{97,65},{2,98}... | collective-permute-start | bytes 1572872 | tf_op jit(solution)/shard_map/ppermute | solution.py:39
  345.2 28.8 %collective-permute-start.18 = (bf16[128,2048]{1,0:T(8,128)(2,1)S(1)}, bf16[128,2048]{1,0:T(8,128)(2,1)S(1)}, u32[]{:S(2)}, u32[]{:S(2)}) collective-permute-start(bf16[128,2048]{1,0:T(8,128)(2,1)S(1)} %fusion.72.rest_0_), channel_id=1, source_target_pairs={{0,16},{16,0},{1,17},{17,1},{2,18},{18,2},{3,19},{19,3},{4,20},{20... | collective-permute-start | bytes 1572872 | tf_op jit(solution)/shard_map/ppermute | solution.py:39
  436.9 18.0 %collective-permute-start.42 = (bf16[4,64,1280]{2,1,0:T(8,128)(2,1)}, bf16[4,64,1280]{2,1,0:T(8,128)(2,1)}, u32[]{:S(2)}, u32[]{:S(2)}) collective-permute-start(bf16[4,64,1280]{2,1,0:T(8,128)(2,1)} %pad_maximum_fusion.4), channel_id=1, source_target_pairs={{0,1},{1,2},{2,3},{3,0},{4,5},{5,6},{6,7},{7,4},{8,9},{9,10},{10,1... | collective-permute-start | bytes 1966088 | tf_op jit(solution)/shard_map/ppermute | solution.py:39
  437.9 17.0 %collective-permute-start.44 = (bf16[4,64,1280]{2,1,0:T(8,128)(2,1)}, bf16[4,64,1280]{2,1,0:T(8,128)(2,1)}, u32[]{:S(2)}, u32[]{:S(2)}) collective-permute-start(bf16[4,64,1280]{2,1,0:T(8,128)(2,1)} %pad_maximum_fusion.5), channel_id=1, source_target_pairs={{0,3},{1,0},{2,1},{3,2},{4,7},{5,4},{6,5},{7,6},{8,11},{9,8},{10,9... | collective-permute-start | bytes 1966088 | tf_op jit(solution)/shard_map/ppermute | solution.py:39
  449.9 18.4 %collective-permute-start.34 = (bf16[4,64,1280]{2,1,0:T(8,128)(2,1)S(1)}, bf16[4,64,1280]{2,1,0:T(8,128)(2,1)S(1)}, u32[]{:S(2)}, u32[]{:S(2)}) collective-permute-start(bf16[4,64,1280]{2,1,0:T(8,128)(2,1)S(1)} %pad_maximum_fusion.2), channel_id=1, source_target_pairs={{0,4},{4,8},{8,12},{12,0},{1,5},{5,9},{9,13},{13,1},{2,6},{6,10},{... | collective-permute-start | bytes 1966088 | tf_op jit(solution)/shard_map/ppermute | solution.py:39
  451.5 17.0 %collective-permute-start.36 = (bf16[4,64,1280]{2,1,0:T(8,128)(2,1)S(1)}, bf16[4,64,1280]{2,1,0:T(8,128)(2,1)S(1)}, u32[]{:S(2)}, u32[]{:S(2)}) collective-permute-start(bf16[4,64,1280]{2,1,0:T(8,128)(2,1)S(1)} %pad_maximum_fusion.3), channel_id=1, source_target_pairs={{0,12},{4,0},{8,4},{12,8},{1,13},{5,1},{9,5},{13,9},{2,14},{6,2},{... | collective-permute-start | bytes 1966088 | tf_op jit(solution)/shard_map/ppermute | solution.py:39
  456.5 15.7 %collective-permute-start.45 = (bf16[32,1280]{1,0:T(8,128)(2,1)S(1)}, bf16[32,1280]{1,0:T(8,128)(2,1)S(1)}, u32[]{:S(2)}, u32[]{:S(2)}) collective-permute-start(bf16[32,1280]{1,0:T(8,128)(2,1)S(1)} %get-tuple-element.268), channel_id=1, source_target_pairs={{0,4},{4,8},{8,12},{12,0},{1,5},{5,9},{9,13},{13,1},{2,6},{6,10},{... | collective-permute-start | bytes 245768 | tf_op jit(solution)/shard_map/ppermute | solution.py:39
  487.2 64.1 %all-gather.12.cloned.1.call-start = ((), (), s32[]{:S(2)}) async-start(), calls=%async_computation.15 | async-start | bytes 5570560 | tf_op jit(solution)/shard_map/all_gather | solution.py:697
  (117 other events, 940.9 us)
Sparse Core Ops, SparseCore 0:
  10.2 73.0 all-gather.5
  85.0 48.7 all-gather.9
  136.0 68.2 all-gather.7
  328.2 56.2 reduce-scatter.3
  386.8 42.4 reduce-scatter.5
  431.5 43.4 reduce-scatter.7
  496.0 55.2 all-gather.11

commit v5 on v4

--- a/solution.py
+++ b/solution.py
@@ -280,21 +280,19 @@
 
 
 def weight_grads_kernel(*refs):
-    rows, w_down, grads, ys = refs[:12], refs[12], refs[14:17], refs[17]
+    rows, w_down, grads, ys = refs[:12], refs[12], refs[14:17], refs[17:19]
     first = pl.program_id(0) == 0
     for e in range(2):
         xs, dys, hid, dg, du, gate = rows[6 * e : 6 * e + 6]
 
         @pl.when(first if e == 0 else jnp.logical_not(first))
-        def _(e=e, xs=xs, dys=dys, hid=hid, dg=dg, du=du, gate=gate):
+        def _(xs=xs, dys=dys, hid=hid, dg=dg, du=du, gate=gate, out=ys[e]):
             s = gate[:, 0:1]
 
             def scaled(v):
                 return (v[...].astype(f32) * s).astype(bf16)
 
-            y = mm(hid[...], w_down[0])
-            for o in range(16):
-                ys[o, CAP * e : CAP * e + CAP] = y[CAP * o : CAP * o + CAP].astype(bf16)
+            out[...] = mm(hid[...], w_down[0]).astype(bf16)
             grads[0][0] = mm(xs[:, :MODEL_WIDTH], scaled(dg), TN).astype(bf16)
             grads[1][0] = mm(xs[:, :MODEL_WIDTH], scaled(du), TN).astype(bf16)
             grads[2][0] = mm(scaled(hid), dys[...], TN).astype(bf16)
@@ -309,9 +307,9 @@
         weight_grads_kernel,
         grid=(2,),
         out_shape=[jax.ShapeDtypeStruct((2, *s), bf16) for s in sizes]
-        + [jax.ShapeDtypeStruct((16, 2 * CAP, MODEL_WIDTH), bf16)],
+        + [jax.ShapeDtypeStruct((640, MODEL_WIDTH), bf16)] * 2,
         in_specs=[VM] * 12 + [per_expert(768, MODEL_WIDTH), ANY],
-        out_specs=[per_expert(*s) for s in sizes] + [VM],
+        out_specs=[per_expert(*s) for s in sizes] + [VM] * 2,
         compiler_params=pltpu.CompilerParams(vmem_limit_bytes=60 * MIB),
         cost_estimate=pl.CostEstimate(flops=16 << 30, bytes_accessed=48 << 20, transcendentals=0),
         name="weight_grads",
@@ -646,7 +644,8 @@
     kept = [
         (xs[e], dys[e], *kept, slot_gate[e]) for e, kept in enumerate((kept_first, kept_second))
     ]
-    grad_gate, grad_up, grad_down, ys = weight_grads([*kept[0], *kept[1]], down_all, from_first)
+    grad_gate, grad_up, grad_down, *ys = weight_grads([*kept[0], *kept[1]], down_all, from_first)
+    ys = jnp.concatenate([v.reshape(16, CAP, MODEL_WIDTH) for v in ys], axis=1)
     (from_second,) = after([from_second], ys)
     backs = [from_first, from_second]
     dh_sum = combined(backs)

time: 577 us -> 581 us (level)
  transfers between devices with their start and end apart: 66 -> 66, of which waited for: 30 -> 29; matrix products, arithmetic and copies ran while one was open for 16% -> 17% of each run, Pallas kernels for 22% -> 22%
where the time goes in v5:
time: 581 us; the launch traced here: 573 us
  waiting for transfers between devices  203 us (35%)
  Pallas kernels  131 us (23%)
  starting transfers between devices  95.3 us (16%)
  local copies, waits for them, and re-layouts  54 us (9%)
  other arithmetic  50.6 us (9%)
  matrix products  21.7 us (4%)
  between operations  16 us (3%)
    ppermute x53, waiting for transfers between devices, shift(): return lax.ppermute(v, axis, [(i, (i + by) % n) for i in range(n)])  126 us
    ppermute x53, starting transfers between devices, shift(): return lax.ppermute(v, axis, [(i, (i + by) % n) for i in range(n)])  64.1 us
    all_to_all x5, waiting for transfers between devices, exchanged(): return lax.all_to_all(v, EXPERT, 0, 0, tiled=True)  62.1 us
    pallas_call x2, Pallas kernels, expert_rows(): pl.pallas_call(functools.partial(expert_kernel, e), out_shape=[jax.ShapeD...  36.9 us
    pallas_call x1, Pallas kernels, weight_grads(): pl.pallas_call(weight_grads_kernel, grid=(2,), out_shape=[jax.ShapeDtypeS...  31.8 us
    unnamed x170, local copies, waits for them, and re-layouts  28 us
    all_to_all x5, starting transfers between devices, exchanged(): return lax.all_to_all(v, EXPERT, 0, 0, tiled=True)  26.9 us
    pallas_call x1, Pallas kernels, attention_forward(): pl.pallas_call(functools.partial(attention_kernel, spec), out_shape=[jax....  18.5 us
  transfers between devices with their start and end apart: 66, of which 29 were waited for; matrix products, arithmetic and copies ran while one was open for 17% of the time, Pallas kernels for 22%

profile of v5, /device:TPU:0, one launch (start us, length us, event | category | flops | bytes accessed | tf_op | source)
XLA Modules:
  0.0 572.5 jit_solution(16769970921193669796)
XLA Ops:
  26.0 21.1 %collective-permute-done.1.refs_0_ = bf16[128,2176]{1,0:T(8,128)(2,1)} collective-permute-done((bf16[128,2176]{1,0:T(8,128)(2,1)}, bf16[128,2176]{1,0:T(8,128)(2,1)}, u32[]{:S(2)}, u32[]{:S(2)}) %collective-permute-start.1) | collective-permute-done | bytes 557088 | tf_op jit(solution)/shard_map/ppermute | solution.py:39
  56.1 7.8 %collective-permute-done.11.refs_2_ = bf16[2,256,768]{2,1,0:T(8,128)(2,1)S(1)} collective-permute-done((bf16[2,256,768]{2,1,0:T(8,128)(2,1)}, bf16[2,256,768]{2,1,0:T(8,128)(2,1)S(1)}, u32[]{:S(2)}, u32[]{:S(2)}) %collective-permute-start.11) | collective-permute-done | bytes 786464 | tf_op jit(solution)/shard_map/ppermute | solution.py:39
  63.9 5.6 collective-permute-done.9.refs_0_
  83.9 18.5 %attention_forward.1 = (bf16[2048,768]{1,0:T(8,128)(2,1)}, bf16[1024,2176]{1,0:T(8,128)(2,1)}, f32[1024,512]{1,0:T(8,128)}, f32[1024,128]{1,0:T(8,128)}, bf16[10...) custom-call(s32[4]{0:T(128)} %pad_add_fusion.place, ...), custom_call_target="tpu_custom_call" | custom-call | flops 9663676416 | bytes 29360128 | tf_op jit(solution)/shard_map/attention_forward/pallas_call | solution.py:223
  113.5 10.8 %collective-permute-done.14 = bf16[64,2048]{1,0:T(8,128)(2,1)S(1)} collective-permute-done((bf16[64,2048]{1,0:T(8,128)(2,1)S(1)}, bf16[64,2048]{1,0:T(8,128)(2,1)S(1)}, u32[]{:S(2)}, u32[]{:S(2)}) %collective-permute-start.14) | collective-permute-done | bytes 262176 | tf_op jit(solution)/shard_map/ppermute | solution.py:39
  129.7 11.4 %collective-permute-done.15 = bf16[128,2048]{1,0:T(8,128)(2,1)} collective-permute-done((bf16[128,2048]{1,0:T(8,128)(2,1)S(1)}, bf16[128,2048]{1,0:T(8,128)(2,1)}, u32[]{:S(2)}, u32[]{:S(2)}) %collective-permute-start.15) | collective-permute-done | bytes 524320 | tf_op jit(solution)/shard_map/ppermute | solution.py:39
  146.7 6.8 %all-to-all-start = ((bf16[16,40,2176]{2,1,0:T(8,128)(2,1)}), bf16[16,40,2176]{2,1,0:T(8,128)(2,1)S(1)}, u32[]{:S(2)}, u32[]{:S(2)}) async-start(bf16[16,40,2176]{2,1,0:T(8,128)(2,1)} %fusion.2), calls=%async_computation | async-start | bytes 5570560 | tf_op jit(solution)/shard_map/all_to_all | solution.py:574
  164.6 30.5 %all-to-all-done.refs_1_ = bf16[16,40,2176]{2,1,0:T(8,128)(2,1)S(1)} async-done(((bf16[16,40,2176]{2,1,0:T(8,128)(2,1)}), bf16[16,40,2176]{2,1,0:T(8,128)(2,1)S(1)}, u32[]{:S(2)}, u32[]{:S(2)}) %all-to-all-start) | async-done | bytes 2785312 | tf_op jit(solution)/shard_map/all_to_all | solution.py:574
  196.6 4.5 all-to-all-start.1
  202.5 4.7 convolution_convert_fusion.2
  207.3 18.5 %expert_rows.2 = (bf16[640,2176]{1,0:T(8,128)(2,1)}, bf16[640,768]{1,0:T(8,128)(2,1)S(1)}, bf16[640,768]{1,0:T(8,128)(2,1)S(1)}, bf16[640,768]{1,0:T(8,128)(2,1)S(1)}) custom-call(bf16[640,2176]{1,0:T(8,128)(2,1)} %bitcast.267, bf16[640,2048]{1,0:T(8,128)(2,1)S(1)} %bitcast.254, bf16[4,2048,768]{2,1,0:T(8,128)(2,1)} %all-gather.8.cloned.1.call-done.w_in, ...), custom_call_target="tpu_custom_call" | custom-call | flops 10737418240 | bytes 20971520 | tf_op jit(solution)/shard_map/expert_rows/pallas_call | solution.py:270
  228.8 11.2 %all-to-all-done.1.refs_1_ = bf16[16,40,2176]{2,1,0:T(8,128)(2,1)} async-done(((bf16[16,40,2176]{2,1,0:T(8,128)(2,1)}), bf16[16,40,2176]{2,1,0:T(8,128)(2,1)}, u32[]{:S(2)}, u32[]{:S(2)}) %all-to-all-start.1) | async-done | bytes 2785312 | tf_op jit(solution)/shard_map/all_to_all | solution.py:574
  239.9 4.7 all-to-all-start.2
  244.6 4.6 convolution_convert_fusion
  249.2 18.5 %expert_rows.3 = (bf16[640,2176]{1,0:T(8,128)(2,1)}, bf16[640,768]{1,0:T(8,128)(2,1)S(1)}, bf16[640,768]{1,0:T(8,128)(2,1)S(1)}, bf16[640,768]{1,0:T(8,128)(2,1)S(1)}) custom-call(bf16[640,2176]{1,0:T(8,128)(2,1)} %bitcast.46.xs_in.refs_6_, bf16[640,2048]{1,0:T(8,128)(2,1)S(1)} %bitcast.256, bf16[4,2048,768]{2,1,0:T(8,128)(2,1)} %all-gather.8.cloned.1.call-done.w_in, ...), custom_call_target="tpu_custom_call" | custom-call | flops 10737418240 | bytes 20971520 | tf_op jit(solution)/shard_map/expert_rows/pallas_call | solution.py:270
  270.6 11.7 %all-to-all-done.2.refs_13_.refs_1_ = bf16[16,40,2176]{2,1,0:T(8,128)(2,1)} async-done(((bf16[16,40,2176]{2,1,0:T(8,128)(2,1)}), bf16[16,40,2176]{2,1,0:T(8,128)(2,1)}, u32[]{:S(2)}, u32[]{:S(2)}) %all-to-all-start.2) | async-done | bytes 2785312 | tf_op jit(solution)/shard_map/all_to_all | solution.py:574
  289.4 31.8 %weight_grads.1 = (bf16[2,2048,768]{2,1,0:T(8,128)(2,1)}, bf16[2,2048,768]{2,1,0:T(8,128)(2,1)}, bf16[2,768,2048]{2,1,0:T(8,128)(2,1)}, bf16[640,2048]{1,0:T(8,128)(2,1)}, bf16[640,2048]{1,0:T(8,128)(2,1)}) custom-call(bf16[640,2176]{1,0:T(8,128)(2,1)} %bitcast.268, bf16[640,2048]{1,0:T(8,128)(2,1)} %bitcast.255, bf16[640,768]{1,0:T(8,128)(2,1)} %copy-done.19, ...), custom_call_target="tpu_custom_call" | custom-call | flops 17179869184 | bytes 50331648 | tf_op jit(solution)/shard_map/weight_grads/pallas_call | solution.py:306
  321.2 5.8 %pad_maximum_fusion.refs_1_.refs_0_ = bf16[16,80,2048]{2,1,0:T(8,128)(2,1)} fusion(bf16[16,40,2048]{2,1,0:T(8,128)(2,1)} %bitcast.276, bf16[16,40,2048]{2,1,0:T(8,128)(2,1)} %bitcast.275), kind=kLoop, calls=%fused_computation.3 | loop fusion | flops 10485760 | bytes 10485760 | tf_op jit(solution)/shard_map/concatenate | solution.py:648
  332.8 7.2 %all-to-all-start.4 = ((bf16[16,80,2048]{2,1,0:T(8,128)(2,1)}), bf16[16,80,2048]{2,1,0:T(8,128)(2,1)}, u32[]{:S(2)}, u32[]{:S(2)}) async-start(bf16[16,80,2048]{2,1,0:T(8,128)(2,1)} %after.17), calls=%async_computation.4 | async-start | bytes 10485760 | tf_op jit(solution)/shard_map/all_to_all | solution.py:574
  348.2 17.1 %collective-permute-done.20.rest_3_ = bf16[128,2048]{1,0:T(8,128)(2,1)S(1)} collective-permute-done((bf16[128,2048]{1,0:T(8,128)(2,1)S(1)}, bf16[128,2048]{1,0:T(8,128)(2,1)S(1)}, u32[]{:S(2)}, u32[]{:S(2)}) %collective-permute-start.20) | collective-permute-done | bytes 524320 | tf_op jit(solution)/shard_map/ppermute | solution.py:39
  369.3 7.8 %collective-permute-done.21.rest_4_ = bf16[64,2048]{1,0:T(8,128)(2,1)S(1)} collective-permute-done((bf16[64,2048]{1,0:T(8,128)(2,1)S(1)}, bf16[64,2048]{1,0:T(8,128)(2,1)S(1)}, u32[]{:S(2)}, u32[]{:S(2)}) %collective-permute-start.21) | collective-permute-done | bytes 262176 | tf_op jit(solution)/shard_map/ppermute | solution.py:39
  381.9 6.3 %out_back.1 = (bf16[1024,512]{1,0:T(8,128)(2,1)S(1)}, bf16[16,128,512]{2,1,0:T(8,128)(2,1)S(1)}) custom-call(s32[4]{0:T(128)S(1)} %copy-done.13, bf16[512,2048]{1,0:T(8,128)(2,1)S(1)} %copy-done.15, bf16[1024,512]{1,0:T(8,128)(2,1)S(1)} %copy-done.18, bf16[128,2048]{1,0:T(8,128)(2,1)S(1)} %fusion.72.rest_0_, ...), custom_call_target="tpu_custom_call" | custom-call | flops 5368709120 | bytes 12582912 | tf_op jit(solution)/shard_map/out_back/pallas_call | solution.py:341
  389.6 13.6 %attention_backward.1 = (bf16[1024,512]{1,0:T(8,128)(2,1)S(1)}, f32[1024,256]{1,0:T(8,128)S(1)}, f32[1,128]{1,0:T(1,128)S(1)}) custom-call(bf16[1024,512]{1,0:T(8,128)(2,1)S(1)} %get-tuple-element.95.dob, bf16[1024,512]{1,0:T(8,128)(2,1)} %get-tuple-element.94.a_b, bf16[4,1024,128]{2,1,0:T(8,128)(2,1)} %get-tuple-element.96.q_b, ...), custom_call_target="tpu_custom_call" | custom-call | flops 10737418240 | bytes 12582912 | tf_op jit(solution)/shard_map/attention_backward/pallas_call | solution.py:389
  407.0 8.8 %all-to-all-done.4 = bf16[16,80,2048]{2,1,0:T(8,128)(2,1)} async-done(((bf16[16,80,2048]{2,1,0:T(8,128)(2,1)}), bf16[16,80,2048]{2,1,0:T(8,128)(2,1)}, u32[]{:S(2)}, u32[]{:S(2)}) %all-to-all-start.4) | async-done | bytes 5242912 | tf_op jit(solution)/shard_map/all_to_all | solution.py:574
  415.7 13.0 %projection_grads.1 = (bf16[4,64,1280]{2,1,0:T(8,128)(2,1)}, bf16[4,64,1280]{2,1,0:T(8,128)(2,1)}, bf16[2,64,1280]{2,1,0:T(8,128)(2,1)S(1)}, bf16[2,64,1280]{2,1...) custom-call(s32[4]{0:T(128)S(1)} %copy-done.13, ...), custom_call_target="tpu_custom_call" | custom-call | flops 3221225472 | bytes 16777216 | tf_op jit(solution)/shard_map/projection_grads/pallas_call | solution.py:444
  464.0 9.0 %collective-permute-done.34 = bf16[4,64,1280]{2,1,0:T(8,128)(2,1)S(1)} collective-permute-done((bf16[4,64,1280]{2,1,0:T(8,128)(2,1)S(1)}, bf16[4,64,1280]{2,1,0:T(8,128)(2,1)S(1)}, u32[]{:S(2)}, u32[]{:S(2)}) %collective-permute-start.34) | collective-permute-done | bytes 655392 | tf_op jit(solution)/shard_map/ppermute | solution.py:39
  501.8 4.9 input_grad.1
  514.8 5.9 %collective-permute-done.30 = bf16[64,2048]{1,0:T(8,128)(2,1)S(1)} collective-permute-done((bf16[64,2048]{1,0:T(8,128)(2,1)S(1)}, bf16[64,2048]{1,0:T(8,128)(2,1)S(1)}, u32[]{:S(2)}, u32[]{:S(2)}) %collective-permute-start.30) | collective-permute-done | bytes 262176 | tf_op jit(solution)/shard_map/ppermute | solution.py:39
  524.4 4.2 fusion.12
  528.6 6.7 %collective-permute-done.31 = bf16[128,2048]{1,0:T(8,128)(2,1)S(1)} collective-permute-done((bf16[128,2048]{1,0:T(8,128)(2,1)S(1)}, bf16[128,2048]{1,0:T(8,128)(2,1)S(1)}, u32[]{:S(2)}, u32[]{:S(2)}) %collective-permute-start.31) | collective-permute-done | bytes 524320 | tf_op jit(solution)/shard_map/ppermute | solution.py:39
  544.8 10.6 %all-gather.12.cloned.1.call-done = bf16[128,16,1280]{2,1,0:T(8,128)(2,1)} async-done(((bf16[8,16,1280]{2,1,0:T(8,128)(2,1)}), bf16[128,16,1280]{2,1,0:T(8,128)(2,1)}) %all-gather.12.cloned.1.call-update) | async-done | bytes 5242896 | tf_op jit(solution)/shard_map/all_gather | solution.py:696
  555.4 6.4 %place_rows.1 = (f32[256,4096]{1,0:T(8,128)}, f32[256,512]{1,0:T(8,128)}, f32[256,512]{1,0:T(8,128)}, f32[256,128]{1,0:T(8,128)}, f32[8,16,128]{2,1,0:T(8,128)}, /*index=5*/f32[512,2048]{1,0:T(8,128)}) custom-call(bf16[16,8,16,1280]{3,2,1,0:T(8,128)(2,1)} %bitcast.274, bf16[128,2048]{1,0:T(8,128)(2,1)} %fusion.23.refs_0_, ...), custom_call_target="tpu_custom_call" | custom-call | bytes 16777216 | tf_op jit(solution)/shard_map/place_rows/pallas_call | solution.py:512
  (448 shorter events, 206.8 us)
Async XLA Ops:
  7.2 195.3 %all-gather.6.cloned.1.call-start = ((), (), s32[]{:S(2)}) async-start(), calls=%async_computation.9 | async-start | bytes 8912896 | tf_op jit(solution)/shard_map/all_gather | solution.py:576
  9.5 197.8 %all-gather.10.cloned.1.call-start = ((), (), s32[]{:S(2)}) async-start(), calls=%async_computation.11 | async-start | bytes 7077888 | tf_op jit(solution)/shard_map/all_gather | solution.py:601
  12.8 34.3 %collective-permute-start.1 = (bf16[128,2176]{1,0:T(8,128)(2,1)}, bf16[128,2176]{1,0:T(8,128)(2,1)}, u32[]{:S(2)}, u32[]{:S(2)}) collective-permute-start(bf16[128,2176]{1,0:T(8,128)(2,1)} %fusion.29.rest_0_), channel_id=1, source_target_pairs={{0,96},{32,0},{64,32},{96,64},{1,97},{33,1},{65,33},{97,65},{2,98}... | collective-permute-start | bytes 1671176 | tf_op jit(solution)/shard_map/ppermute | solution.py:39
  16.9 33.4 %collective-permute-start.2 = (bf16[128,2176]{1,0:T(8,128)(2,1)}, bf16[128,2176]{1,0:T(8,128)(2,1)}, u32[]{:S(2)}, u32[]{:S(2)}) collective-permute-start(bf16[128,2176]{1,0:T(8,128)(2,1)} %fusion.29.rest_0_), channel_id=1, source_target_pairs={{0,32},{32,64},{64,96},{96,0},{1,33},{33,65},{65,97},{97,1},{2,34}... | collective-permute-start | bytes 1671176 | tf_op jit(solution)/shard_map/ppermute | solution.py:39
  16.9 35.5 %collective-permute-start = (bf16[128,2176]{1,0:T(8,128)(2,1)}, bf16[128,2176]{1,0:T(8,128)(2,1)}, u32[]{:S(2)}, u32[]{:S(2)}) collective-permute-start(bf16[128,2176]{1,0:T(8,128)(2,1)} %fusion.29.rest_0_), channel_id=1, source_target_pairs={{0,16},{16,0},{1,17},{17,1},{2,18},{18,2},{3,19},{19,3},{4,20},{20... | collective-permute-start | bytes 1671176 | tf_op jit(solution)/shard_map/ppermute | solution.py:39
  22.7 33.4 %collective-permute-start.10 = (bf16[2,256,768]{2,1,0:T(8,128)(2,1)}, bf16[2,256,768]{2,1,0:T(8,128)(2,1)S(1)}, u32[]{:S(2)}, u32[]{:S(2)}) collective-permute-start(bf16[2,256,768]{2,1,0:T(8,128)(2,1)} %get-tuple-element.265), channel_id=1, source_target_pairs={{0,64},{32,96},{64,0},{96,32},{1,65},{33,97},{65,1},{97,33},{2,66}... | collective-permute-start | bytes 2359304 | tf_op jit(solution)/shard_map/ppermute | solution.py:39
  24.4 39.6 %collective-permute-start.11 = (bf16[2,256,768]{2,1,0:T(8,128)(2,1)}, bf16[2,256,768]{2,1,0:T(8,128)(2,1)S(1)}, u32[]{:S(2)}, u32[]{:S(2)}) collective-permute-start(bf16[2,256,768]{2,1,0:T(8,128)(2,1)} %get-tuple-element.264), channel_id=1, source_target_pairs={{0,96},{32,0},{64,32},{96,64},{1,97},{33,1},{65,33},{97,65},{2,98}... | collective-permute-start | bytes 2359304 | tf_op jit(solution)/shard_map/ppermute | solution.py:39
  47.1 22.5 %collective-permute-start.9 = (bf16[2,256,768]{2,1,0:T(8,128)(2,1)}, bf16[2,256,768]{2,1,0:T(8,128)(2,1)}, u32[]{:S(2)}, u32[]{:S(2)}) collective-permute-start(bf16[2,256,768]{2,1,0:T(8,128)(2,1)} %get-tuple-element.266), channel_id=1, source_target_pairs={{0,32},{32,64},{64,96},{96,0},{1,33},{33,65},{65,97},{97,1},{2,34}... | collective-permute-start | bytes 2359304 | tf_op jit(solution)/shard_map/ppermute | solution.py:39
  51.3 21.2 %collective-permute-start.3 = (bf16[64,2176]{1,0:T(8,128)(2,1)S(1)}, bf16[64,2176]{1,0:T(8,128)(2,1)S(1)}, u32[]{:S(2)}, u32[]{:S(2)}) collective-permute-start(bf16[64,2176]{1,0:T(8,128)(2,1)S(1)} %slice.334), channel_id=1, source_target_pairs={{0,32},{32,64},{64,96},{96,0},{1,33},{33,65},{65,97},{97,1},{2,34}... | collective-permute-start | bytes 835592 | tf_op jit(solution)/shard_map/ppermute | solution.py:39
  52.4 20.1 %collective-permute-start.4 = (bf16[64,2176]{1,0:T(8,128)(2,1)S(1)}, bf16[64,2176]{1,0:T(8,128)(2,1)S(1)}, u32[]{:S(2)}, u32[]{:S(2)}) collective-permute-start(bf16[64,2176]{1,0:T(8,128)(2,1)S(1)} %slice.335), channel_id=1, source_target_pairs={{0,96},{32,0},{64,32},{96,64},{1,97},{33,1},{65,33},{97,65},{2,98}... | collective-permute-start | bytes 835592 | tf_op jit(solution)/shard_map/ppermute | solution.py:39
  73.9 133.4 %all-gather.8.cloned.1.call-start = ((), (), s32[]{:S(2)}) async-start(), calls=%async_computation.10 | async-start | bytes 14155776 | tf_op jit(solution)/shard_map/all_gather | solution.py:600
  108.5 15.8 %collective-permute-start.14 = (bf16[64,2048]{1,0:T(8,128)(2,1)S(1)}, bf16[64,2048]{1,0:T(8,128)(2,1)S(1)}, u32[]{:S(2)}, u32[]{:S(2)}) collective-permute-start(bf16[64,2048]{1,0:T(8,128)(2,1)S(1)} %get-tuple-element.260), channel_id=1, source_target_pairs={{0,32},{32,64},{64,96},{96,0},{1,33},{33,65},{65,97},{97,1},{2,34}... | collective-permute-start | bytes 786440 | tf_op jit(solution)/shard_map/ppermute | solution.py:39
  108.6 15.9 %collective-permute-start.16 = (bf16[64,2048]{1,0:T(8,128)(2,1)S(1)}, bf16[64,2048]{1,0:T(8,128)(2,1)S(1)}, u32[]{:S(2)}, u32[]{:S(2)}) collective-permute-start(bf16[64,2048]{1,0:T(8,128)(2,1)S(1)} %get-tuple-element.261), channel_id=1, source_target_pairs={{0,96},{32,0},{64,32},{96,64},{1,97},{33,1},{65,33},{97,65},{2,98}... | collective-permute-start | bytes 786440 | tf_op jit(solution)/shard_map/ppermute | solution.py:39
  124.4 16.7 %collective-permute-start.15 = (bf16[128,2048]{1,0:T(8,128)(2,1)S(1)}, bf16[128,2048]{1,0:T(8,128)(2,1)}, u32[]{:S(2)}, u32[]{:S(2)}) collective-permute-start(bf16[128,2048]{1,0:T(8,128)(2,1)S(1)} %pad_maximum_fusion.7), channel_id=1, source_target_pairs={{0,32},{32,64},{64,96},{96,0},{1,33},{33,65},{65,97},{97,1},{2,34}... | collective-permute-start | bytes 1572872 | tf_op jit(solution)/shard_map/ppermute | solution.py:39
  146.7 48.4 %all-to-all-start = ((bf16[16,40,2176]{2,1,0:T(8,128)(2,1)}), bf16[16,40,2176]{2,1,0:T(8,128)(2,1)S(1)}, u32[]{:S(2)}, u32[]{:S(2)}) async-start(bf16[16,40,2176]{2,1,0:T(8,128)(2,1)} %fusion.2), calls=%async_computation | async-start | bytes 5570560 | tf_op jit(solution)/shard_map/all_to_all | solution.py:574
  196.6 43.3 %all-to-all-start.1 = ((bf16[16,40,2176]{2,1,0:T(8,128)(2,1)}), bf16[16,40,2176]{2,1,0:T(8,128)(2,1)}, u32[]{:S(2)}, u32[]{:S(2)}) async-start(bf16[16,40,2176]{2,1,0:T(8,128)(2,1)} %after.13), calls=%async_computation.1 | async-start | bytes 5570560 | tf_op jit(solution)/shard_map/all_to_all | solution.py:574
  239.9 42.4 %all-to-all-start.2 = ((bf16[16,40,2176]{2,1,0:T(8,128)(2,1)}), bf16[16,40,2176]{2,1,0:T(8,128)(2,1)}, u32[]{:S(2)}, u32[]{:S(2)}) async-start(bf16[16,40,2176]{2,1,0:T(8,128)(2,1)} %after.14), calls=%async_computation.2 | async-start | bytes 5570560 | tf_op jit(solution)/shard_map/all_to_all | solution.py:574
  282.3 44.6 %all-to-all-start.3 = ((bf16[16,40,2176]{2,1,0:T(8,128)(2,1)}), bf16[16,40,2176]{2,1,0:T(8,128)(2,1)S(1)}, u32[]{:S(2)}, u32[]{:S(2)}) async-start(bf16[16,40,2176]{2,1,0:T(8,128)(2,1)} %after.15), calls=%async_computation.3 | async-start | bytes 5570560 | tf_op jit(solution)/shard_map/all_to_all | solution.py:574
  286.1 251.4 %reduce-scatter.4.cloned.1.call-start = ((), (), s32[]{:S(2)}) async-start(), calls=%async_computation.12 | async-start | bytes 7077888 | tf_op jit(solution)/shard_map/reduce_scatter | solution.py:669
  328.5 211.3 %reduce-scatter.6.cloned.1.call-start = ((), (), s32[]{:S(2)}) async-start(), calls=%async_computation.13 | async-start | bytes 7077888 | tf_op jit(solution)/shard_map/reduce_scatter | solution.py:669
  332.8 82.9 %all-to-all-start.4 = ((bf16[16,80,2048]{2,1,0:T(8,128)(2,1)}), bf16[16,80,2048]{2,1,0:T(8,128)(2,1)}, u32[]{:S(2)}, u32[]{:S(2)}) async-start(bf16[16,80,2048]{2,1,0:T(8,128)(2,1)} %after.17), calls=%async_computation.4 | async-start | bytes 10485760 | tf_op jit(solution)/shard_map/all_to_all | solution.py:574
  340.1 202.2 %reduce-scatter.8.cloned.1.call-start = ((), (), s32[]{:S(2)}) async-start(), calls=%async_computation.14 | async-start | bytes 7077888 | tf_op jit(solution)/shard_map/reduce_scatter | solution.py:669
  344.9 20.5 %collective-permute-start.20 = (bf16[128,2048]{1,0:T(8,128)(2,1)S(1)}, bf16[128,2048]{1,0:T(8,128)(2,1)S(1)}, u32[]{:S(2)}, u32[]{:S(2)}) collective-permute-start(bf16[128,2048]{1,0:T(8,128)(2,1)S(1)} %fusion.72.rest_0_), channel_id=1, source_target_pairs={{0,32},{32,64},{64,96},{96,0},{1,33},{33,65},{65,97},{97,1},{2,34}... | collective-permute-start | bytes 1572872 | tf_op jit(solution)/shard_map/ppermute | solution.py:39
  345.6 19.9 %collective-permute-start.19 = (bf16[128,2048]{1,0:T(8,128)(2,1)S(1)}, bf16[128,2048]{1,0:T(8,128)(2,1)S(1)}, u32[]{:S(2)}, u32[]{:S(2)}) collective-permute-start(bf16[128,2048]{1,0:T(8,128)(2,1)S(1)} %fusion.72.rest_0_), channel_id=1, source_target_pairs={{0,96},{32,0},{64,32},{96,64},{1,97},{33,1},{65,33},{97,65},{2,98}... | collective-permute-start | bytes 1572872 | tf_op jit(solution)/shard_map/ppermute | solution.py:39
  348.1 29.5 %collective-permute-start.18 = (bf16[128,2048]{1,0:T(8,128)(2,1)S(1)}, bf16[128,2048]{1,0:T(8,128)(2,1)S(1)}, u32[]{:S(2)}, u32[]{:S(2)}) collective-permute-start(bf16[128,2048]{1,0:T(8,128)(2,1)S(1)} %fusion.72.rest_0_), channel_id=1, source_target_pairs={{0,16},{16,0},{1,17},{17,1},{2,18},{18,2},{3,19},{19,3},{4,20},{20... | collective-permute-start | bytes 1572872 | tf_op jit(solution)/shard_map/ppermute | solution.py:39
  441.4 17.5 %collective-permute-start.42 = (bf16[4,64,1280]{2,1,0:T(8,128)(2,1)}, bf16[4,64,1280]{2,1,0:T(8,128)(2,1)}, u32[]{:S(2)}, u32[]{:S(2)}) collective-permute-start(bf16[4,64,1280]{2,1,0:T(8,128)(2,1)} %pad_maximum_fusion.5), channel_id=1, source_target_pairs={{0,1},{1,2},{2,3},{3,0},{4,5},{5,6},{6,7},{7,4},{8,9},{9,10},{10,1... | collective-permute-start | bytes 1966088 | tf_op jit(solution)/shard_map/ppermute | solution.py:39
  442.4 16.5 %collective-permute-start.44 = (bf16[4,64,1280]{2,1,0:T(8,128)(2,1)}, bf16[4,64,1280]{2,1,0:T(8,128)(2,1)}, u32[]{:S(2)}, u32[]{:S(2)}) collective-permute-start(bf16[4,64,1280]{2,1,0:T(8,128)(2,1)} %pad_maximum_fusion.6), channel_id=1, source_target_pairs={{0,3},{1,0},{2,1},{3,2},{4,7},{5,4},{6,5},{7,6},{8,11},{9,8},{10,9... | collective-permute-start | bytes 1966088 | tf_op jit(solution)/shard_map/ppermute | solution.py:39
  454.4 18.5 %collective-permute-start.34 = (bf16[4,64,1280]{2,1,0:T(8,128)(2,1)S(1)}, bf16[4,64,1280]{2,1,0:T(8,128)(2,1)S(1)}, u32[]{:S(2)}, u32[]{:S(2)}) collective-permute-start(bf16[4,64,1280]{2,1,0:T(8,128)(2,1)S(1)} %pad_maximum_fusion.3), channel_id=1, source_target_pairs={{0,4},{4,8},{8,12},{12,0},{1,5},{5,9},{9,13},{13,1},{2,6},{6,10},{... | collective-permute-start | bytes 1966088 | tf_op jit(solution)/shard_map/ppermute | solution.py:39
  456.2 17.0 %collective-permute-start.36 = (bf16[4,64,1280]{2,1,0:T(8,128)(2,1)S(1)}, bf16[4,64,1280]{2,1,0:T(8,128)(2,1)S(1)}, u32[]{:S(2)}, u32[]{:S(2)}) collective-permute-start(bf16[4,64,1280]{2,1,0:T(8,128)(2,1)S(1)} %pad_maximum_fusion.4), channel_id=1, source_target_pairs={{0,12},{4,0},{8,4},{12,8},{1,13},{5,1},{9,5},{13,9},{2,14},{6,2},{... | collective-permute-start | bytes 1966088 | tf_op jit(solution)/shard_map/ppermute | solution.py:39
  460.5 16.2 %collective-permute-start.45 = (bf16[32,1280]{1,0:T(8,128)(2,1)S(1)}, bf16[32,1280]{1,0:T(8,128)(2,1)S(1)}, u32[]{:S(2)}, u32[]{:S(2)}) collective-permute-start(bf16[32,1280]{1,0:T(8,128)(2,1)S(1)} %get-tuple-element.270), channel_id=1, source_target_pairs={{0,4},{4,8},{8,12},{12,0},{1,5},{5,9},{9,13},{13,1},{2,6},{6,10},{... | collective-permute-start | bytes 245768 | tf_op jit(solution)/shard_map/ppermute | solution.py:39
  461.1 15.7 %collective-permute-start.47 = (bf16[32,1280]{1,0:T(8,128)(2,1)S(1)}, bf16[32,1280]{1,0:T(8,128)(2,1)S(1)}, u32[]{:S(2)}, u32[]{:S(2)}) collective-permute-start(bf16[32,1280]{1,0:T(8,128)(2,1)S(1)} %get-tuple-element.271), channel_id=1, source_target_pairs={{0,12},{4,0},{8,4},{12,8},{1,13},{5,1},{9,5},{13,9},{2,14},{6,2},{... | collective-permute-start | bytes 245768 | tf_op jit(solution)/shard_map/ppermute | solution.py:39
  491.7 63.6 %all-gather.12.cloned.1.call-start = ((), (), s32[]{:S(2)}) async-start(), calls=%async_computation.15 | async-start | bytes 5570560 | tf_op jit(solution)/shard_map/all_gather | solution.py:696
  (117 other events, 945.1 us)
Sparse Core Ops, SparseCore 0:
  10.2 73.0 all-gather.5
  85.0 48.1 all-gather.9
  135.4 68.7 all-gather.7
  328.7 60.0 reduce-scatter.3
  391.0 42.4 reduce-scatter.5
  435.8 43.0 reduce-scatter.7
  500.6 54.7 all-gather.11
